TPU v7x, 128 devices: a whole 4x4x4 slice. The times are simulated.
128 devices in a mesh: fsdp: 8 (over z_hi, y), seq: 16 (over x, z_lo, core).
Axes of the slice: x: 4, y: 4, z: 4 (z_hi: 2, z_lo: 2; z = z_hi * 2 + z_lo), core: 2. Of those that a mesh axis runs over, the one named last changes fastest.
Arguments:
- tokens: bfloat16 [16384, 1024], P(('fsdp', 'seq')), may hold values from -6 to 6
- gain_mix: bfloat16 [1024], P(('fsdp', 'seq')), may hold values from 0.5 to 1.5
- in_weight: bfloat16 [1024, 3072], P(('fsdp', 'seq')), may hold values from -0.1875 to 0.1875
- conv_weight: bfloat16 [3, 1024], P(None, ('fsdp', 'seq')), may hold values from -3 to 3
- out_weight: bfloat16 [1024, 1024], P(('fsdp', 'seq')), may hold values from -0.1875 to 0.1875
- gain_ffn: bfloat16 [1024], P(('fsdp', 'seq')), may hold values from 0.5 to 1.5
- gate_weight: bfloat16 [1024, 4608], P(('fsdp', 'seq')), may hold values from -0.1875 to 0.1875
- up_weight: bfloat16 [1024, 4608], P(('fsdp', 'seq')), may hold values from -0.1875 to 0.1875
- down_weight: bfloat16 [4608, 1024], P(None, ('fsdp', 'seq')), may hold values from -0.09375 to 0.09375
- live_counts: int32 [8, 16], P('fsdp', 'seq'), may hold values from 64 to 128, as said below
- positions: int32 [16384], P(('fsdp', 'seq')), may hold values from 0 to 2, as said below
- cotangent: bfloat16 [16384, 1024], P(('fsdp', 'seq')), may hold values from -24 to 24
Outputs:
- mixed_out: bfloat16 [16384, 1024], P(('fsdp', 'seq'))
- grad_tokens: bfloat16 [16384, 1024], P(('fsdp', 'seq'))
- grad_gain_mix: float32 [1024], P(('fsdp', 'seq'))
- grad_in: float32 [1024, 3072], P(('fsdp', 'seq'))
- grad_conv: float32 [3, 1024], P(None, ('fsdp', 'seq'))
- grad_out: float32 [1024, 1024], P(('fsdp', 'seq'))
- grad_gain_ffn: float32 [1024], P(('fsdp', 'seq'))
- grad_gate: float32 [1024, 4608], P(('fsdp', 'seq'))
- grad_up: float32 [1024, 4608], P(('fsdp', 'seq'))
- grad_down: float32 [4608, 1024], P(None, ('fsdp', 'seq'))
Inputs may be any that keep to these rules, and one draw needn't show every extreme that they name: `live_counts`: the live tokens of a device fill the first slots of its block of 128; the other slots are padding. In every draw some device of each fsdp index has all 128 slots live. `positions`: each live token's index within its sequence, capped at 2; 0 at a sequence's first token and on padding slots. Sequences run through the live tokens of one fsdp index in order of seq and slot and never cross fsdp indices. In every draw one sequence of each fsdp index holds tokens of its first and of its last seq device.
All inputs are finite; a program needn't handle non-finite values.
Results may differ from a plain program's by a relative error of at most 0.038.
Values may be sent and summed in bfloat16 or wider, within the bound.
A program may use at most 128 MiB of HBM per device.

v0:
```python
import jax
import jax.numpy as jnp
from jax import lax
from jax.sharding import PartitionSpec as P

EPS = 1e-05
FLOAT = jnp.float32
HALF = jnp.bfloat16


def norm_scale(values):
    return lax.rsqrt(jnp.mean(values * values, axis=-1, keepdims=True) + EPS)


def norm_back(values, row_scale, gain_row, upstream):
    normal = values * row_scale
    weighted = upstream * gain_row
    grad_gain = jnp.sum(upstream * normal, axis=0)
    grad_values = row_scale * (
        weighted - normal * jnp.mean(weighted * normal, axis=-1, keepdims=True)
    )
    return (grad_values, grad_gain)


def conv_inputs(mix_value, counts, seq_count, slot_count):
    feat_count = mix_value.shape[1]
    blocks = mix_value.reshape(seq_count, slot_count, feat_count)
    tail_index = counts[:, None] - 2 + jnp.arange(2, dtype=jnp.int32)[None, :]
    tail_rows = jnp.take_along_axis(blocks, tail_index[:, :, None], axis=1)
    before = jnp.concatenate([jnp.zeros((1, 2, feat_count), FLOAT), tail_rows[:-1]], axis=0)
    extended = jnp.concatenate([before, blocks], axis=1)
    return (
        extended[:, 1:-1].reshape(-1, feat_count),
        extended[:, :-2].reshape(-1, feat_count),
        tail_index,
    )


def fold_sources(value, seq_count, fsdp_count):
    shaped = value.reshape(value.shape[0], value.shape[1], seq_count, fsdp_count, value.shape[3])
    return jnp.sum(shaped, axis=3)


def local(
    tokens,
    gain_mix,
    in_weight,
    conv_weight,
    out_weight,
    gain_ffn,
    gate_weight,
    up_weight,
    down_weight,
    live_counts,
    positions,
    cotangent,
):
    seq_count = lax.axis_size("seq")
    fsdp_count = lax.axis_size("fsdp")
    slot_count, model_width = tokens.shape
    piece_rows = in_weight.shape[0]
    hid_part = gate_weight.shape[1] // seq_count
    feat_count = model_width // seq_count
    in_local = in_weight.reshape(piece_rows, 3 * fsdp_count, seq_count, piece_rows)
    gate_local = gate_weight.reshape(piece_rows, 1, seq_count, hid_part)
    up_local = up_weight.reshape(piece_rows, 1, seq_count, hid_part)
    down_local = jnp.transpose(down_weight).reshape(piece_rows, 1, seq_count, hid_part)
    swapped = (
        lax.all_to_all(in_local, "seq", split_axis=2, concat_axis=0, tiled=True),
        lax.all_to_all(gate_local, "seq", split_axis=2, concat_axis=0, tiled=True),
        lax.all_to_all(up_local, "seq", split_axis=2, concat_axis=0, tiled=True),
        lax.all_to_all(down_local, "seq", split_axis=2, concat_axis=0, tiled=True),
    )
    gain_pair = jnp.stack([gain_mix, gain_ffn])
    slab_parts = (
        lax.all_gather(swapped[0], "fsdp", axis=0, tiled=True),
        lax.all_gather(swapped[1], "fsdp", axis=0, tiled=True),
        lax.all_gather(swapped[2], "fsdp", axis=0, tiled=True),
        lax.all_gather(swapped[3], "fsdp", axis=0, tiled=True),
        lax.all_gather(conv_weight, "fsdp", axis=1, tiled=True),
        lax.all_gather(out_weight, "fsdp", axis=0, tiled=True),
        lax.all_gather(gain_pair, "fsdp", axis=1, tiled=True),
    )
    w_in = slab_parts[0].reshape(model_width, 3 * feat_count)
    w_gate = slab_parts[1].reshape(model_width, hid_part)
    w_up = slab_parts[2].reshape(model_width, hid_part)
    w_down = slab_parts[3].reshape(model_width, hid_part)
    conv_taps = slab_parts[4].astype(FLOAT)
    w_out = slab_parts[5]
    own_count = live_counts[0, 0]
    keep_own = (jnp.arange(slot_count, dtype=jnp.int32) < own_count).astype(FLOAT)[:, None]
    d_out = keep_own * cotangent.astype(FLOAT)
    d_ffn = d_out.astype(HALF)
    flag_rows = jnp.stack([keep_own[:, 0], positions.astype(FLOAT)]).astype(HALF)
    streams = (
        lax.all_gather(tokens, "seq", axis=0, tiled=True),
        lax.all_gather(d_ffn, "seq", axis=0, tiled=True),
        lax.all_gather(flag_rows, "seq", axis=1, tiled=True),
        lax.all_gather(slab_parts[6], "seq", axis=1, tiled=True),
    )
    stream_x, stream_dffn, stream_flags, gain_seq = streams
    gain_rows = (
        gain_seq.astype(FLOAT)
        .reshape(2, seq_count, fsdp_count, piece_rows)
        .transpose(0, 2, 1, 3)
        .reshape(2, model_width)
    )
    x_stream = stream_x.astype(FLOAT)
    normed = (x_stream * norm_scale(x_stream) * gain_rows[0]).astype(HALF)
    projected = jnp.dot(normed, w_in, preferred_element_type=FLOAT)
    b_part = projected[:, :feat_count]
    c_part = projected[:, feat_count : 2 * feat_count]
    v_part = projected[:, 2 * feat_count :]
    mix_value = b_part * v_part
    counts = jnp.sum(stream_flags[0].astype(FLOAT).reshape(seq_count, slot_count), axis=1).astype(
        jnp.int32
    )
    places = stream_flags[1].astype(FLOAT)[:, None]
    first_ok = (places >= 1.0).astype(FLOAT)
    second_ok = (places >= 2.0).astype(FLOAT)
    one_back, two_back, tail_index = conv_inputs(mix_value, counts, seq_count, slot_count)
    conv_value = (
        conv_taps[0] * mix_value
        + first_ok * conv_taps[1] * one_back
        + second_ok * conv_taps[2] * two_back
    )
    gated = (c_part * conv_value).astype(HALF)
    x_own = tokens.astype(FLOAT)
    scale_mix = norm_scale(x_own)
    branch_own = lax.psum_scatter(
        jnp.dot(gated, w_out, preferred_element_type=FLOAT).astype(jnp.bfloat16),
        "seq",
        scatter_dimension=0,
        tiled=True,
    ).astype(jnp.float32)
    resid = x_own + branch_own
    scale_ffn = norm_scale(resid)
    normed_two = (resid * scale_ffn * gain_rows[1]).astype(HALF)
    stream_two = lax.all_gather(normed_two, "seq", axis=0, tiled=True)
    gate_value = jnp.dot(stream_two, w_gate, preferred_element_type=FLOAT)
    up_value = jnp.dot(stream_two, w_up, preferred_element_type=FLOAT)
    sig_gate = jax.nn.sigmoid(gate_value)
    swish_gate = gate_value * sig_gate
    active = (swish_gate * up_value).astype(HALF)
    ffn_own = lax.psum_scatter(
        jnp.einsum("tf,df->td", active, w_down, preferred_element_type=FLOAT).astype(jnp.bfloat16),
        "seq",
        scatter_dimension=0,
        tiled=True,
    ).astype(jnp.float32)
    mixed_out = (keep_own * (resid + ffn_own)).astype(HALF)
    grad_down_t = jnp.einsum("td,tf->df", stream_dffn, active, preferred_element_type=FLOAT)
    d_active = jnp.einsum("td,df->tf", stream_dffn, w_down, preferred_element_type=FLOAT)
    d_gate = (d_active * up_value * (sig_gate * (1.0 + gate_value * (1.0 - sig_gate)))).astype(HALF)
    d_upper = (d_active * swish_gate).astype(HALF)
    grad_gate = jnp.einsum("td,tf->df", stream_two, d_gate, preferred_element_type=FLOAT)
    grad_up = jnp.einsum("td,tf->df", stream_two, d_upper, preferred_element_type=FLOAT)
    first_term = jnp.einsum("tf,df->td", d_gate, w_gate, preferred_element_type=FLOAT)
    d_normed_two = lax.psum_scatter(
        (first_term + jnp.einsum("tf,df->td", d_upper, w_up, preferred_element_type=FLOAT)).astype(
            jnp.bfloat16
        ),
        "seq",
        scatter_dimension=0,
        tiled=True,
    ).astype(jnp.float32)
    d_norm_two, grad_gain_ffn = norm_back(resid, scale_ffn, gain_rows[1], d_normed_two)
    d_resid = d_out + d_norm_two
    d_branch = d_resid.astype(HALF)
    stream_back = lax.all_gather(d_branch, "seq", axis=0, tiled=True)
    grad_out = jnp.einsum("tc,td->cd", gated, stream_back, preferred_element_type=FLOAT)
    d_gated = jnp.einsum("td,cd->tc", stream_back, w_out, preferred_element_type=FLOAT)
    d_c = d_gated * conv_value
    d_conv = d_gated * c_part
    grad_conv = jnp.stack(
        [
            jnp.sum(d_conv * mix_value, axis=0),
            jnp.sum(d_conv * first_ok * one_back, axis=0),
            jnp.sum(d_conv * second_ok * two_back, axis=0),
        ]
    )
    block_shape = (seq_count, slot_count, feat_count)
    term_one = (first_ok * conv_taps[1] * d_conv).reshape(block_shape)
    term_two = (second_ok * conv_taps[2] * d_conv).reshape(block_shape)
    d_ext = jnp.pad(term_one, ((0, 0), (1, 1), (0, 0))) + jnp.pad(
        term_two, ((0, 0), (0, 2), (0, 0))
    )
    d_blocks = d_ext[:, 2:] + (conv_taps[0] * d_conv).reshape(block_shape)
    d_tails = jnp.concatenate([d_ext[1:, :2], jnp.zeros((1, 2, feat_count), FLOAT)], axis=0)
    slot_line = jnp.arange(slot_count, dtype=jnp.int32)[None, :]
    first_hit = (slot_line == tail_index[:, 0:1]).astype(FLOAT)[:, :, None]
    second_hit = (slot_line == tail_index[:, 1:2]).astype(FLOAT)[:, :, None]
    d_blocks = d_blocks + first_hit * d_tails[:, None, 0] + second_hit * d_tails[:, None, 1]
    d_mixed = d_blocks.reshape(-1, feat_count)
    d_projected = jnp.concatenate([d_mixed * v_part, d_c, d_mixed * b_part], axis=1).astype(HALF)
    grad_in = jnp.einsum("td,te->de", normed, d_projected, preferred_element_type=FLOAT)
    d_normed = lax.psum_scatter(
        jnp.einsum("te,de->td", d_projected, w_in, preferred_element_type=FLOAT).astype(
            jnp.bfloat16
        ),
        "seq",
        scatter_dimension=0,
        tiled=True,
    ).astype(jnp.float32)
    d_norm_one, grad_gain_mix = norm_back(x_own, scale_mix, gain_rows[0], d_normed)
    grad_tokens = (d_resid + d_norm_one).astype(HALF)
    gain_grads = jnp.stack([grad_gain_mix, grad_gain_ffn], axis=1).reshape(model_width, 1, 1, 2)
    moved = (
        lax.all_to_all(
            lax.all_to_all(
                grad_in.reshape(model_width, 3 * fsdp_count, 1, piece_rows).astype(jnp.bfloat16),
                "fsdp",
                split_axis=0,
                concat_axis=2,
                tiled=True,
            ),
            "seq",
            split_axis=0,
            concat_axis=2,
            tiled=True,
        ).astype(jnp.float32),
        lax.all_to_all(
            lax.all_to_all(
                grad_gate.reshape(model_width, 1, 1, hid_part).astype(jnp.bfloat16),
                "fsdp",
                split_axis=0,
                concat_axis=2,
                tiled=True,
            ),
            "seq",
            split_axis=0,
            concat_axis=2,
            tiled=True,
        ).astype(jnp.float32),
        lax.all_to_all(
            lax.all_to_all(
                grad_up.reshape(model_width, 1, 1, hid_part).astype(jnp.bfloat16),
                "fsdp",
                split_axis=0,
                concat_axis=2,
                tiled=True,
            ),
            "seq",
            split_axis=0,
            concat_axis=2,
            tiled=True,
        ).astype(jnp.float32),
        lax.all_to_all(
            lax.all_to_all(
                grad_down_t.reshape(model_width, 1, 1, hid_part).astype(jnp.bfloat16),
                "fsdp",
                split_axis=0,
                concat_axis=2,
                tiled=True,
            ),
            "seq",
            split_axis=0,
            concat_axis=2,
            tiled=True,
        ).astype(jnp.float32),
        lax.all_to_all(
            lax.all_to_all(
                gain_grads.astype(jnp.bfloat16), "fsdp", split_axis=0, concat_axis=2, tiled=True
            ),
            "seq",
            split_axis=0,
            concat_axis=2,
            tiled=True,
        ).astype(gain_grads.dtype),
    )
    owned_in = fold_sources(moved[0], seq_count, fsdp_count).reshape(piece_rows, 3 * model_width)
    owned_gate = fold_sources(moved[1], seq_count, fsdp_count).reshape(piece_rows, -1)
    owned_up = fold_sources(moved[2], seq_count, fsdp_count).reshape(piece_rows, -1)
    owned_down = jnp.transpose(
        fold_sources(moved[3], seq_count, fsdp_count).reshape(piece_rows, -1)
    )
    owned_gains = jnp.sum(fold_sources(moved[4], seq_count, fsdp_count), axis=2).reshape(
        piece_rows, 2
    )
    small_sums = (
        lax.psum_scatter(
            grad_conv.astype(jnp.bfloat16), "fsdp", scatter_dimension=1, tiled=True
        ).astype(jnp.float32),
        lax.psum_scatter(
            grad_out.astype(jnp.bfloat16), "fsdp", scatter_dimension=0, tiled=True
        ).astype(jnp.float32),
    )
    return (
        mixed_out,
        grad_tokens,
        owned_gains[:, 0],
        owned_in,
        small_sums[0],
        small_sums[1],
        owned_gains[:, 1],
        owned_gate,
        owned_up,
        owned_down,
    )


def solution(mesh):
    placed = (
        P(("fsdp", "seq"), None),
        P(("fsdp", "seq")),
        P(("fsdp", "seq"), None),
        P(None, ("fsdp", "seq")),
        P(("fsdp", "seq"), None),
        P(("fsdp", "seq")),
        P(("fsdp", "seq"), None),
        P(("fsdp", "seq"), None),
        P(None, ("fsdp", "seq")),
        P("fsdp", "seq"),
        P(("fsdp", "seq")),
        P(("fsdp", "seq"), None),
    )
    return jax.shard_map(
        local,
        mesh=mesh,
        in_specs=placed,
        out_specs=(
            P(("fsdp", "seq"), None),
            P(("fsdp", "seq"), None),
            P(("fsdp", "seq")),
            P(("fsdp", "seq"), None),
            P(None, ("fsdp", "seq")),
            P(("fsdp", "seq"), None),
            P(("fsdp", "seq")),
            P(("fsdp", "seq"), None),
            P(("fsdp", "seq"), None),
            P(None, ("fsdp", "seq")),
        ),
        check_vma=False,
    )
```

profile of v0, /device:TPU:1, one launch (start us, length us, event | category | flops | bytes accessed | tf_op | source)
XLA Modules:
  0.0 767.7 jit_solution(3845897198144568595)
XLA Ops:
  11.5 7.2 all-to-all-start
  19.4 20.3 %all-gather = bf16[8,8,2]{1,2,0:T(2,128)(2,1)S(1)} all-gather(bf16[1,8,2]{1,2,0:T(2,128)(2,1)S(1)} %maximum_bitcast_fusion), channel_id=1, replica_groups=mesh['fsdp'=8,'seq'=16] {'fsdp'}, dimensions={0}, use_global_device_ids=true | all-gather | bytes 288 | tf_op jit(solution)/shard_map/all_gather | solution.py:82
  39.8 22.9 %all-gather.1 = bf16[16,64,2]{1,2,0:T(2,128)(2,1)S(1)} all-gather(bf16[1,64,2]{1,2,0:T(2,128)(2,1)S(1)} %reshape.397), channel_id=1, replica_groups=mesh['fsdp'=8,'seq'=16] {'seq'}, dimensions={0}, use_global_device_ids=true | all-gather | bytes 4352 | tf_op jit(solution)/shard_map/all_gather | solution.py:99
  62.8 16.1 %all_gather.44 = bf16[2,2048]{1,0:T(2,128)(2,1)S(1)} all-gather(bf16[2,128]{1,0:T(2,128)(2,1)S(1)} %pad_maximum_fusion.5), channel_id=1, replica_groups=mesh['fsdp'=8,'seq'=16] {'seq'}, dimensions={1}, use_global_device_ids=true | all-gather | bytes 8704 | tf_op jit(solution)/shard_map/all_gather | solution.py:98
  80.0 14.7 %all-gather.2 = bf16[8,8,3]{1,2,0:T(4,128)(2,1)S(1)} all-gather(bf16[1,8,3]{1,2,0:T(4,128)(2,1)S(1)} %bitcast.313), channel_id=1, replica_groups=mesh['fsdp'=8,'seq'=16] {'fsdp'}, dimensions={0}, use_global_device_ids=true | all-gather | bytes 432 | tf_op jit(solution)/shard_map/all_gather | solution.py:80
  96.8 28.2 %all_gather.45 = bf16[64,1024]{1,0:T(8,128)(2,1)S(1)} all-gather(bf16[8,1024]{1,0:T(8,128)(2,1)S(1)} %copy-done.30), channel_id=1, replica_groups=mesh['fsdp'=8,'seq'=16] {'fsdp'}, dimensions={0}, use_global_device_ids=true | all-gather | bytes 147456 | tf_op jit(solution)/shard_map/all_gather | solution.py:81
  125.6 26.7 %all_gather.42 = bf16[1024,24,1,8]{0,3,2,1:T(8,128)(2,1)S(1)} all-gather(bf16[128,24,1,8]{0,3,2,1:T(8,128)(2,1)S(1)} %copy.209), channel_id=1, replica_groups=mesh['fsdp'=8,'seq'=16] {'fsdp'}, dimensions={0}, use_global_device_ids=true | all-gather | bytes 442368 | tf_op jit(solution)/shard_map/all_gather | solution.py:76
  167.1 69.4 %reduce-scatter.7.cloned.1.call-done = bf16[128,1024]{1,0:T(8,128)(2,1)} async-done(((bf16[2048,1024]{1,0:T(8,128)(2,1)}), bf16[128,1024]{1,0:T(8,128)(2,1)}) %reduce-scatter.7.cloned.1.call-update) | async-done | bytes 262160 | tf_op jit(solution)/shard_map/reduce_scatter | solution.py:130
  243.1 7.6 all-to-all-start.3
  261.0 32.6 %all_gather.49 = bf16[1024,1,1,288]{3,0,2,1:T(8,128)(2,1)} all-gather(bf16[128,1,1,288]{3,0,2,1:T(8,128)(2,1)S(1)} %bitcast.293), channel_id=1, replica_groups=mesh['fsdp'=8,'seq'=16] {'fsdp'}, dimensions={0}, use_global_device_ids=true | all-gather | bytes 663552 | tf_op jit(solution)/shard_map/all_gather | solution.py:79
  293.6 10.7 %all-to-all-start.1 = ((bf16[8,1,16,288]{3,0,1,2:T(8,128)(2,1)}), bf16[8,1,16,288]{3,0,1,2:T(8,128)(2,1)S(1)}, u32[]{:S(2)}, u32[]{:S(2)}) async-start(bf16[8,1,16,288]{3,0,1,2:T(8,128)(2,1)} %copy.215), calls=%async_computation.2 | async-start | bytes 196608 | tf_op jit(solution)/shard_map/all_to_all | solution.py:70
  304.3 32.2 %all_gather.48 = bf16[1024,1,1,288]{3,0,2,1:T(8,128)(2,1)} all-gather(bf16[128,1,1,288]{3,0,2,1:T(8,128)(2,1)S(1)} %bitcast.294), channel_id=1, replica_groups=mesh['fsdp'=8,'seq'=16] {'fsdp'}, dimensions={0}, use_global_device_ids=true | all-gather | bytes 663552 | tf_op jit(solution)/shard_map/all_gather | solution.py:78
  336.6 32.3 %all_gather.47 = bf16[1024,1,1,288]{3,0,2,1:T(8,128)(2,1)} all-gather(bf16[128,1,1,288]{3,0,2,1:T(8,128)(2,1)S(1)} %bitcast.295), channel_id=1, replica_groups=mesh['fsdp'=8,'seq'=16] {'fsdp'}, dimensions={0}, use_global_device_ids=true | all-gather | bytes 663552 | tf_op jit(solution)/shard_map/all_gather | solution.py:77
  368.9 5.4 fusion.21
  377.2 7.3 multiply_convert_fusion
  387.0 4.6 add_convert_fusion
  391.6 76.0 %reduce-scatter.11.cloned.1.call-done = bf16[128,1024]{1,0:T(8,128)(2,1)} async-done(((bf16[2048,1024]{1,0:T(8,128)(2,1)}), bf16[128,1024]{1,0:T(8,128)(2,1)}) %reduce-scatter.11.cloned.1.call-update) | async-done | bytes 262160 | tf_op jit(solution)/shard_map/reduce_scatter | solution.py:159
  473.4 38.7 %all-gather.14.cloned.1.call-done = bf16[2048,1024]{1,0:T(8,128)(2,1)} async-done(((bf16[128,1024]{1,0:T(8,128)(2,1)}), bf16[2048,1024]{1,0:T(8,128)(2,1)}) %all-gather.14.cloned.1.call-update) | async-done | bytes 4194320 | tf_op jit(solution)/shard_map/all_gather | solution.py:170
  516.3 4.7 multiply_reduce_fusion
  556.5 6.4 all-to-all-start.12
  569.9 5.5 all-to-all-done.12
  601.0 8.3 %all-to-all-done.10 = bf16[8,2,18432]{2,1,0:T(2,128)(2,1)} async-done(((bf16[8,2,18432]{2,1,0:T(2,128)(2,1)}), bf16[8,2,18432]{2,1,0:T(2,128)(2,1)}, u32[]{:S(2)}, u32[]{:S(2)}) %all-to-all-start.10) | async-done | bytes 589856 | tf_op jit(solution)/shard_map/all_to_all | solution.py:236
  609.3 5.1 all-to-all-start.9
  614.4 4.6 reshape.418
  629.0 6.2 all-to-all-start.11
  635.2 4.6 reshape.420
  649.6 5.7 all-to-all-start.13
  680.3 4.7 all-to-all-done.6
  689.9 4.9 reshape.413
  699.3 18.3 %all-reduce.4 = bf16[3,64]{1,0:T(4,128)(2,1)S(1)} all-reduce(bf16[3,64]{1,0:T(4,128)(2,1)S(1)} %pad_maximum_fusion.4), channel_id=6, replica_groups=mesh['fsdp'=8,'seq'=16] {'fsdp'}, use_global_device_ids=true, to_apply=%region_18.19.clone | all-reduce | flops 192 | bytes 768
  734.9 6.5 all-to-all-done.4
  743.1 10.8 %all-to-all-start.5 = ((bf16[128,1,8,2]{2,3,1,0:T(2,128)(2,1)}), bf16[128,1,8,2]{2,3,1,0:T(2,128)(2,1)S(1)}, u32[]{:S(2)}, u32[]{:S(2)}) async-start(bf16[128,1,8,2]{2,3,1,0:T(2,128)(2,1)} %copy.227), calls=%async_computation.9 | async-start | bytes 131072 | tf_op jit(solution)/shard_map/all_to_all | solution.py:261
  (308 shorter events, 202.0 us)
Async XLA Ops:
  7.2 55.6 %copy-start.56 = (s32[128]{0:T(128)S(1)}, s32[128]{0:T(128)}, u32[]{:S(2)}) copy-start(s32[128]{0:T(128)} %param.22) | copy-start | bytes 1540
  7.2 72.7 %copy-start.50 = (bf16[3,8]{1,0:T(4,128)(2,1)S(1)}, bf16[3,8]{1,0:T(4,128)(2,1)}, u32[]{:S(2)}) copy-start(bf16[3,8]{1,0:T(4,128)(2,1)} %param.15) | copy-start | bytes 148
  7.2 89.6 %copy-start.30 = (bf16[8,1024]{1,0:T(8,128)(2,1)S(1)}, bf16[8,1024]{1,0:T(8,128)(2,1)}, u32[]{:S(2)}) copy-start(bf16[8,1024]{1,0:T(8,128)(2,1)} %param.16) | copy-start | bytes 49156
  7.2 145.1 %all-gather.8.cloned.1.call-start = ((), (), s32[]{:S(2)}) async-start(), calls=%async_computation.19 | async-start | bytes 4456448 | tf_op jit(solution)/shard_map/all_gather | solution.py:96
  11.5 113.5 %all-to-all-start = ((bf16[16,2,768]{2,1,0:T(2,128)(2,1)}), bf16[16,2,768]{2,1,0:T(2,128)(2,1)S(1)}, u32[]{:S(2)}, u32[]{:S(2)}) async-start(bf16[16,2,768]{2,1,0:T(2,128)(2,1)} %reshape.407), calls=%async_computation | async-start | bytes 98304 | tf_op jit(solution)/shard_map/all_to_all | solution.py:69
  18.7 217.8 %reduce-scatter.7.cloned.1.call-start = ((), (), s32[]{:S(2)}) async-start(), calls=%async_computation.20 | async-start | bytes 4456448 | tf_op jit(solution)/shard_map/reduce_scatter | solution.py:130
  164.6 71.9 %copy-start = (bf16[128,1024]{1,0:T(8,128)(2,1)S(1)}, bf16[128,1024]{1,0:T(8,128)(2,1)}, u32[]{:S(2)}) copy-start(bf16[128,1024]{1,0:T(8,128)(2,1)} %param.12) | copy-start | bytes 786436
  164.6 76.0 %copy-start.13 = (bf16[128,1024]{1,0:T(8,128)(2,1)S(1)}, bf16[128,1024]{1,0:T(8,128)(2,1)}, u32[]{:S(2)}) copy-start(bf16[128,1024]{1,0:T(8,128)(2,1)} %param.23) | copy-start | bytes 786436
  164.6 204.3 %all-gather.10.cloned.1.call-start = ((), (), s32[]{:S(2)}) async-start(), calls=%async_computation.21 | async-start | bytes 4456448 | tf_op jit(solution)/shard_map/all_gather | solution.py:139
  239.9 137.3 %all-gather.12.cloned.1.call-start = ((), (), s32[]{:S(2)}) async-start(), calls=%async_computation.23 | async-start | bytes 4456448 | tf_op jit(solution)/shard_map/all_gather | solution.py:97
  243.1 14.2 %all-to-all-start.3 = ((bf16[8,1,16,288]{3,0,1,2:T(8,128)(2,1)}), bf16[8,1,16,288]{3,0,1,2:T(8,128)(2,1)S(1)}, u32[]{:S(2)}, u32[]{:S(2)}) async-start(bf16[8,1,16,288]{3,0,1,2:T(8,128)(2,1)} %copy.219), calls=%async_computation.4 | async-start | bytes 196608 | tf_op jit(solution)/shard_map/all_to_all | solution.py:72
  257.3 36.3 %all-to-all-start.2 = ((bf16[8,1,16,288]{3,0,1,2:T(8,128)(2,1)}), bf16[8,1,16,288]{3,0,1,2:T(8,128)(2,1)S(1)}, u32[]{:S(2)}, u32[]{:S(2)}) async-start(bf16[8,1,16,288]{3,0,1,2:T(8,128)(2,1)} %copy.217), calls=%async_computation.3 | async-start | bytes 196608 | tf_op jit(solution)/shard_map/all_to_all | solution.py:71
  293.6 42.9 %all-to-all-start.1 = ((bf16[8,1,16,288]{3,0,1,2:T(8,128)(2,1)}), bf16[8,1,16,288]{3,0,1,2:T(8,128)(2,1)S(1)}, u32[]{:S(2)}, u32[]{:S(2)}) async-start(bf16[8,1,16,288]{3,0,1,2:T(8,128)(2,1)} %copy.215), calls=%async_computation.2 | async-start | bytes 196608 | tf_op jit(solution)/shard_map/all_to_all | solution.py:70
  304.3 163.4 %reduce-scatter.11.cloned.1.call-start = ((), (), s32[]{:S(2)}) async-start(), calls=%async_computation.24 | async-start | bytes 4456448 | tf_op jit(solution)/shard_map/reduce_scatter | solution.py:159
  391.6 76.1 %copy-start.2 = (bf16[128,1024]{1,0:T(8,128)(2,1)S(1)}, bf16[128,1024]{1,0:T(8,128)(2,1)}, u32[]{:S(2)}) copy-start(bf16[128,1024]{1,0:T(8,128)(2,1)} %reduce-scatter.7.cloned.1.call-done) | copy-start | bytes 786436
  391.6 120.5 %all-gather.14.cloned.1.call-start = ((), (), s32[]{:S(2)}) async-start(), calls=%async_computation.25 | async-start | bytes 4456448 | tf_op jit(solution)/shard_map/all_gather | solution.py:170
  472.0 246.3 %reduce-scatter.15.cloned.1.call-start = ((), (), s32[]{:S(2)}) async-start(), calls=%async_computation.27 | async-start | bytes 147456 | tf_op jit(solution)/shard_map/reduce_scatter | solution.py:284
  515.8 211.8 %reduce-scatter.13.cloned.1.call-start = ((), (), s32[]{:S(2)}) async-start(), calls=%async_computation.26 | async-start | bytes 4456448 | tf_op jit(solution)/shard_map/reduce_scatter | solution.py:197
  543.0 214.8 %reduce-scatter.9.cloned.1.call-start = ((), (), s32[]{:S(2)}) async-start(), calls=%async_computation.22 | async-start | bytes 4456448 | tf_op jit(solution)/shard_map/reduce_scatter | solution.py:145
  556.5 18.9 %all-to-all-start.12 = ((bf16[8,2,18432]{2,1,0:T(2,128)(2,1)}), bf16[8,2,18432]{2,1,0:T(2,128)(2,1)S(1)}, u32[]{:S(2)}, u32[]{:S(2)}) async-start(bf16[8,2,18432]{2,1,0:T(2,128)(2,1)} %reshape.419), calls=%async_computation.17 | async-start | bytes 1179648 | tf_op jit(solution)/shard_map/all_to_all | solution.py:249
  575.4 16.0 %all-to-all-start.8 = ((bf16[8,2,18432]{2,1,0:T(2,128)(2,1)}), bf16[8,2,18432]{2,1,0:T(2,128)(2,1)S(1)}, u32[]{:S(2)}, u32[]{:S(2)}) async-start(bf16[8,2,18432]{2,1,0:T(2,128)(2,1)} %reshape.415), calls=%async_computation.13 | async-start | bytes 1179648 | tf_op jit(solution)/shard_map/all_to_all | solution.py:223
  591.4 17.9 %all-to-all-start.10 = ((bf16[8,2,18432]{2,1,0:T(2,128)(2,1)}), bf16[8,2,18432]{2,1,0:T(2,128)(2,1)}, u32[]{:S(2)}, u32[]{:S(2)}) async-start(bf16[8,2,18432]{2,1,0:T(2,128)(2,1)} %reshape.417), calls=%async_computation.15 | async-start | bytes 1179648 | tf_op jit(solution)/shard_map/all_to_all | solution.py:236
  609.3 18.7 %all-to-all-start.9 = ((bf16[128,1,8,288]{3,2,1,0:T(8,128)(2,1)}), bf16[128,1,8,288]{3,2,1,0:T(8,128)(2,1)S(1)}, u32[]{:S(2)}, u32[]{:S(2)}) async-start(bf16[128,1,8,288]{3,2,1,0:T(8,128)(2,1)} %copy.236), calls=%async_computation.14 | async-start | bytes 1572864 | tf_op jit(solution)/shard_map/all_to_all | solution.py:222
  629.0 20.6 %all-to-all-start.11 = ((bf16[128,1,8,288]{3,2,1,0:T(8,128)(2,1)}), bf16[128,1,8,288]{3,2,1,0:T(8,128)(2,1)S(1)}, u32[]{:S(2)}, u32[]{:S(2)}) async-start(bf16[128,1,8,288]{3,2,1,0:T(8,128)(2,1)} %copy.243), calls=%async_computation.16 | async-start | bytes 1572864 | tf_op jit(solution)/shard_map/all_to_all | solution.py:235
  649.6 20.5 %all-to-all-start.13 = ((bf16[128,1,8,288]{3,2,1,0:T(8,128)(2,1)}), bf16[128,1,8,288]{3,2,1,0:T(8,128)(2,1)}, u32[]{:S(2)}, u32[]{:S(2)}) async-start(bf16[128,1,8,288]{3,2,1,0:T(8,128)(2,1)} %copy.250), calls=%async_computation.18 | async-start | bytes 1572864 | tf_op jit(solution)/shard_map/all_to_all | solution.py:248
  670.0 15.0 %all-to-all-start.6 = ((bf16[8,2,12288]{2,1,0:T(2,128)(2,1)}), bf16[8,2,12288]{2,1,0:T(2,128)(2,1)S(1)}, u32[]{:S(2)}, u32[]{:S(2)}) async-start(bf16[8,2,12288]{2,1,0:T(2,128)(2,1)} %reshape.411), calls=%async_computation.10 | async-start | bytes 786432 | tf_op jit(solution)/shard_map/all_to_all | solution.py:210
  694.8 24.9 %all-to-all-start.7 = ((bf16[16,2,6144]{2,1,0:T(2,128)(2,1)}), bf16[16,2,6144]{2,1,0:T(2,128)(2,1)S(1)}, u32[]{:S(2)}, u32[]{:S(2)}) async-start(bf16[16,2,6144]{2,1,0:T(2,128)(2,1)} %reshape.413), calls=%async_computation.11 | async-start | bytes 786432 | tf_op jit(solution)/shard_map/all_to_all | solution.py:209
  726.1 31.6 %copy-start.14 = (bf16[128,1024]{1,0:T(8,128)(2,1)S(1)}, bf16[128,1024]{1,0:T(8,128)(2,1)}, u32[]{:S(2)}) copy-start(bf16[128,1024]{1,0:T(8,128)(2,1)} %param.23) | copy-start | bytes 786436
  726.1 31.6 %copy-start.15 = (bf16[128,1024]{1,0:T(8,128)(2,1)S(1)}, bf16[128,1024]{1,0:T(8,128)(2,1)}, u32[]{:S(2)}) copy-start(bf16[128,1024]{1,0:T(8,128)(2,1)} %reduce-scatter.11.cloned.1.call-done) | copy-start | bytes 786436
  726.1 31.6 %copy-start.36 = (f32[128]{0:T(128)S(1)}, f32[128]{0:T(128)}, u32[]{:S(2)}) copy-start(f32[128]{0:T(128)} %copy-done.35) | copy-start | bytes 1540
  730.8 10.6 %all-to-all-start.4 = ((bf16[8,2,128]{2,1,0:T(2,128)(2,1)}), bf16[8,2,128]{2,1,0:T(2,128)(2,1)S(1)}, u32[]{:S(2)}, u32[]{:S(2)}) async-start(bf16[8,2,128]{2,1,0:T(2,128)(2,1)} %reshape.409), calls=%async_computation.8 | async-start | bytes 8192 | tf_op jit(solution)/shard_map/all_to_all | solution.py:262
  743.1 16.9 %all-to-all-start.5 = ((bf16[128,1,8,2]{2,3,1,0:T(2,128)(2,1)}), bf16[128,1,8,2]{2,3,1,0:T(2,128)(2,1)S(1)}, u32[]{:S(2)}, u32[]{:S(2)}) async-start(bf16[128,1,8,2]{2,3,1,0:T(2,128)(2,1)} %copy.227), calls=%async_computation.9 | async-start | bytes 131072 | tf_op jit(solution)/shard_map/all_to_all | solution.py:261
  (50 other events, 328.7 us)
Sparse Core Ops, SparseCore 0:
  9.8 41.0 all-gather.7
  164.7 71.7 reduce-scatter.6
  240.1 42.5 all-gather.9
  284.8 38.8 all-gather.11
  391.7 75.9 reduce-scatter.10
  472.2 39.8 all-gather.13
  515.9 67.4 reduce-scatter.14
  585.9 99.0 reduce-scatter.12
  687.3 70.3 reduce-scatter.8
where the time goes:
time: 780 us; the launch traced here: 768 us
  blocking collectives  244 us (31%)
  waiting for transfers between devices  229 us (29%)
  local copies, waits for them, and re-layouts  104 us (13%)
  starting transfers between devices  84.3 us (11%)
  matrix products  59.2 us (8%)
  other arithmetic  30.2 us (4%)
  between operations  16.6 us (2%)
    reduce_scatter x1, waiting for transfers between devices, local(): lax.psum_scatter((first_term + jnp.einsum('tf,df->td', d_upper, w_up, pre...  76 us
    reduce_scatter x1, waiting for transfers between devices, local(): lax.psum_scatter(jnp.dot(gated, w_out, preferred_element_type=FLOAT).asty...  69.4 us
    unnamed x148, local copies, waits for them, and re-layouts  51.3 us
    all_gather x1, waiting for transfers between devices, local(): stream_back = lax.all_gather(d_branch, 'seq', axis=0, tiled=True)  38.7 us
    all_gather x1, blocking collectives, local(): lax.all_gather(swapped[3], 'fsdp', axis=0, tiled=True)  32.6 us
    all_gather x1, blocking collectives, local(): lax.all_gather(swapped[1], 'fsdp', axis=0, tiled=True)  32.3 us
    all_gather x1, blocking collectives, local(): lax.all_gather(swapped[2], 'fsdp', axis=0, tiled=True)  32.2 us
    all_gather x1, blocking collectives, local(): lax.all_gather(out_weight, 'fsdp', axis=0, tiled=True)  28.2 us
  transfers between devices with their start and end apart: 23, of which 13 were waited for; matrix products, arithmetic and copies ran while one was open for 20% of the time, Pallas kernels for 0%

commit v1 on v0

v1 whole, which is shorter than its diff:
```python
import jax
import jax.numpy as jnp
from jax import lax
from jax.experimental import pallas as pl
from jax.experimental.pallas import tpu as pltpu
from jax.sharding import PartitionSpec as P

EPS = 1e-05
FLOAT = jnp.float32
HALF = jnp.bfloat16
MESH = pl.DeviceIdType.MESH
LANE = 128
D = 1024
SLAB = 1152
MIX_COLS = 34 * LANE
FFN_COLS = 28 * LANE
MIX_HALF = MIX_COLS // 2
FFN_HALF = FFN_COLS // 2
OWN_COLS = MIX_HALF + 4 * FFN_HALF
MIX_PARTS = ((0, 9), (9, 4), (13, 4))
MIX_GATHER = (("y", "z", "x"), ("z", "x", "y"), ("x", "y", "z"))
MIX_REDUCE = (("x", "z", "y"), ("y", "x", "z"), ("z", "y", "x"))
FFN_PARTS = ((0, 7), (7, 7))
FFN_GATHER = (("y", "z"), ("z", "y"))
FFN_REDUCE = (("y", "z"), ("z", "y"))
GRID = (2, 4, 4, 2)
MIX_LANDING = 4 * 3 * len(MIX_PARTS)
VMEM_LIMIT = 56 * 2**20


class Here:
    def __init__(self):
        fsdp = lax.axis_index("fsdp")
        seq = lax.axis_index("seq")
        self.fsdp, self.seq = fsdp, seq
        self.at = {
            "x": lax.div(seq, 4),
            "y": lax.rem(fsdp, 4),
            "z": lax.div(fsdp, 4) * 2 + lax.rem(lax.div(seq, 2), 2),
        }
        self.core = lax.rem(seq, 2)

    def device(self, core, **moved):
        at = {**self.at, **moved}
        return (
            lax.div(at["z"], 2) * 4 + at["y"],
            (at["x"] * 2 + lax.rem(at["z"], 2)) * 2 + core,
        )

    def ring(self, axis, step):
        return lax.rem(self.at[axis] + (step + 4) % 4, 4)

    def beside(self, axis, step):
        return self.device(self.core, **{axis: self.ring(axis, step)})

    def twin(self):
        return self.device(1 - self.core)

    def along(self, step):
        return (self.fsdp, lax.rem(self.seq + (step + 16) % 16, 16))


def greet(devices):
    barrier = pltpu.get_barrier_semaphore()
    for device in devices:
        pl.semaphore_signal(barrier, inc=1, device_id=device, device_id_type=MESH)
    pl.semaphore_wait(barrier, len(devices))


class Mail:
    def __init__(self, send, recv):
        self.send, self.recv, self.posted = send, recv, []

    def post(self, src, dst, device):
        place = len(self.posted)
        copy = pltpu.make_async_remote_copy(
            src_ref=src,
            dst_ref=dst,
            send_sem=self.send.at[place],
            recv_sem=self.recv.at[place],
            device_id=device,
            device_id_type=MESH,
        )
        copy.start()
        self.posted.append(copy)
        return copy

    def close(self):
        for copy in self.posted:
            copy.wait_send()


def cut(start, count):
    return pl.ds(pl.multiple_of(start, LANE), count)


def blocks(ref, at, cols):
    whole = slice(None)
    z = at["z"]
    high, low = (whole, whole) if z is None else (lax.div(z, 2), lax.rem(z, 2))
    y = whole if at["y"] is None else at["y"]
    x = whole if at["x"] is None else at["x"]
    return ref.at[high, y, x, low, :, cols]


class RingGather:
    def __init__(self, here, mail, axis, pick):
        self.here, self.mail, self.axis, self.pick = here, mail, axis, pick

    def start(self, source=None):
        here, axis = self.here, self.axis
        own = self.pick(here.at[axis], None)
        source = own if source is None else source
        self.to_up = self.mail.post(source, own, here.beside(axis, 1))
        self.to_down = self.mail.post(source, own, here.beside(axis, -1))

    def relay(self):
        here, axis = self.here, self.axis
        self.to_up.wait_recv()
        first = self.pick(here.ring(axis, -1), 0)
        self.far_up = self.mail.post(first, first, here.beside(axis, 1))
        self.to_down.wait_recv()
        second = self.pick(here.ring(axis, 1), 1)
        self.far_down = self.mail.post(second, second, here.beside(axis, -1))

    def finish(self):
        self.far_up.wait_recv()
        self.far_down.wait_recv()


class RingReduce:
    def __init__(self, here, mail, axis, pick, near, far):
        self.here, self.mail, self.axis, self.pick = here, mail, axis, pick
        self.near, self.far = near, far

    def start(self):
        here, axis = self.here, self.axis
        away = here.ring(axis, 2)
        self.far_up = self.mail.post(self.pick(away, 0), self.far[0], here.beside(axis, 1))
        self.far_down = self.mail.post(self.pick(away, 1), self.far[1], here.beside(axis, -1))

    def relay(self):
        here, axis = self.here, self.axis
        above, below = here.ring(axis, 1), here.ring(axis, -1)
        self.far_up.wait_recv()
        add_into(self.pick(above, 0), self.far[0])
        self.to_up = self.mail.post(self.pick(above, None), self.near[0], here.beside(axis, 1))
        self.far_down.wait_recv()
        add_into(self.pick(below, 1), self.far[1])
        self.to_down = self.mail.post(self.pick(below, None), self.near[1], here.beside(axis, -1))

    def finish(self):
        self.to_up.wait_recv()
        self.to_down.wait_recv()
        own = self.pick(self.here.at[self.axis], None)
        add_into(own, self.near[0], self.near[1])


def add_into(target, *terms):
    total = target[...].astype(FLOAT)
    for term in terms:
        total = total + term[...].astype(FLOAT)
    target[...] = total.astype(target.dtype)


def column_pick(ref, fixed, axis, start, chunks):
    split = (chunks + 1) // 2

    def pick(place, half):
        first, count = {None: (0, chunks), 0: (0, split), 1: (split, chunks - split)}[half]
        return blocks(ref, {**fixed, axis: place}, cut(start + first * LANE, count * LANE))

    return pick


def row_pick(ref):
    def pick(place, half):
        rows = ref.shape[-2]
        part = {None: slice(None), 0: pl.ds(0, rows // 2), 1: pl.ds(rows // 2, rows // 2)}[half]
        return ref.at[place, part]

    return pick


def gather_rings(here, mail, ref, base, parts, orders, stage):
    rings = []
    for (first, chunks), order in zip(parts, orders):
        fixed = dict(here.at)
        for axis in ("x", "y", "z"):
            if axis not in order or axis in order[:stage]:
                fixed[axis] = None
        pick = column_pick(ref, fixed, order[stage], base + first * LANE, chunks)
        rings.append(RingGather(here, mail, order[stage], pick))
    return rings


def run_rings(rings):
    for ring in rings:
        ring.start()
    for ring in rings:
        ring.relay()
    for ring in rings:
        ring.finish()


def run_last(here, mail, rings):
    def swap(ring, step):
        piece = ring.pick(here.ring(ring.axis, step), None)
        return mail.post(piece, piece, here.twin())

    swaps = []
    for ring in rings:
        ring.start()
    for ring in rings:
        swaps.append(swap(ring, 0))
    for ring in rings:
        ring.relay()
    for ring in rings:
        swaps += [swap(ring, 1), swap(ring, -1)]
    for ring in rings:
        ring.finish()
        swaps.append(swap(ring, 2))
    for copy in swaps:
        copy.wait_recv()


def near_list(here, axes):
    return [here.beside(axis, step) for axis in axes for step in (1, -1)]


def gather_kernel(own, tail, back, mix, ffn, backs, halo, mate, full, send, recv, local_sem):
    here = Here()
    mail = Mail(send, recv)
    x = here.at["x"]
    keep_back = pltpu.make_async_copy(back, backs.at[x], local_sem.at[0])
    keep_back.start()
    greet(
        near_list(here, ("x", "y", "z"))
        + [here.beside("x", 2), here.twin(), here.along(1), here.along(-1)]
    )
    rows = mail.post(own.at[1 - here.core], mate, here.twin())
    stream = RingGather(here, mail, "x", row_pick(backs))
    stream.start(back)
    halo_in = mail.post(tail, halo, here.along(1))
    rows.wait_recv()
    mine = lax.broadcasted_iota(jnp.int32, (16, OWN_COLS), 0) // 8 == here.core
    full[...] = jnp.where(mine, own[here.core].astype(FLOAT), mate[...].astype(FLOAT)).astype(HALF)

    mix_base, ffn_base = here.core * MIX_HALF, here.core * FFN_HALF
    ffn_own = blocks(ffn, here.at, cut(ffn_base, FFN_HALF))

    def slab(place):
        return full.at[:, cut(MIX_HALF + place * FFN_HALF, FFN_HALF)]

    rings = gather_rings(here, mail, mix, mix_base, MIX_PARTS, MIX_GATHER, 0)
    for ring, (first, chunks) in zip(rings, MIX_PARTS):
        ring.start(full.at[:, first * LANE : (first + chunks) * LANE])
    slabs = [
        mail.post(slab(here.ring("x", step)), ffn_own, here.beside("x", step)) for step in (1, 3, 2)
    ]
    keeps = [
        pltpu.make_async_copy(
            full.at[:, 0:MIX_HALF], blocks(mix, here.at, cut(mix_base, MIX_HALF)), local_sem.at[1]
        ),
        pltpu.make_async_copy(slab(x), ffn_own, local_sem.at[2]),
    ]
    for copy in keeps:
        copy.start()
    for ring in rings:
        ring.relay()
    for ring in rings:
        ring.finish()
    for copy in keeps:
        copy.wait()
    for copy in slabs:
        copy.wait_recv()
    rings = gather_rings(here, mail, mix, mix_base, MIX_PARTS, MIX_GATHER, 1)
    rings += gather_rings(here, mail, ffn, ffn_base, FFN_PARTS, FFN_GATHER, 0)
    run_rings(rings)
    stream.relay()
    rings = gather_rings(here, mail, mix, mix_base, MIX_PARTS, MIX_GATHER, 2)
    rings += gather_rings(here, mail, ffn, ffn_base, FFN_PARTS, FFN_GATHER, 1)
    run_last(here, mail, rings)
    stream.finish()
    keep_back.wait()
    halo_in.wait_recv()
    mail.close()


def gather_stream_kernel(rows, stream, send, recv):
    here = Here()
    mail = Mail(send, recv)
    greet(near_list(here, ("x",)))
    ring = RingGather(here, mail, "x", row_pick(stream))
    ring.start(rows)
    stream[here.at["x"]] = rows[...]
    ring.relay()
    ring.finish()
    mail.close()


def reduce_stream_kernel(sums, owned, work, near_a, near_b, far_a, far_b, send, recv, local_sem):
    here = Here()
    mail = Mail(send, recv)
    load = pltpu.make_async_copy(sums, work, local_sem.at[0])
    load.start()
    greet(near_list(here, ("x",)))
    load.wait()
    ring = RingReduce(here, mail, "x", row_pick(work), (near_a, near_b), (far_a, far_b))
    ring.start()
    ring.relay()
    ring.finish()
    owned[...] = work[here.at["x"]].astype(FLOAT)
    mail.close()


def reduce_rings(here, mail, ref, parts, orders, near, far, stage):
    rings = []
    for number, ((first, chunks), order) in enumerate(zip(parts, orders)):
        fixed = {"x": None, "y": None, "z": None}
        for axis in order[:stage]:
            fixed[axis] = here.at[axis]
        pick = column_pick(ref, fixed, order[stage], first * LANE, chunks)
        rings.append(
            RingReduce(here, mail, order[stage], pick, near[number][stage], far[number][stage])
        )
    return rings


def landing_shapes(parts, orders):
    shapes = []
    for (_, chunks), order in zip(parts, orders):
        split = (chunks + 1) // 2
        done = []
        for stage in range(len(order)):
            gone = order[: stage + 1]
            lead = ()
            if "z" not in gone:
                lead += (2,)
            if "y" not in gone:
                lead += (4,)
            if "x" not in gone:
                lead += (4,)
            if "z" not in gone:
                lead += (2,)
            for count, copies in ((chunks, 2), (split, 1), (chunks - split, 1)):
                done += [lead + (16, count * LANE)] * copies
        shapes.append(done)
    return shapes


def landing_refs(orders, refs):
    near, far = [], []
    place = 0
    for order in orders:
        near.append([])
        far.append([])
        for _ in order:
            near[-1].append(refs[place : place + 2])
            far[-1].append(refs[place + 2 : place + 4])
            place += 4
    return near, far


def twin_send(here, mail, grads, half, landed):
    other = (1 - here.core) * half
    return mail.post(grads.at[:, :, :, :, :, cut(other, half)], landed, here.twin())


def twin_sum(here, grads, half, landed, total):
    base = here.core * half

    @pl.loop(0, 32)
    def _(index):
        high, y = lax.div(index, 16), lax.rem(lax.div(index, 4), 4)
        x = lax.rem(index, 4)
        for low in range(2):
            total[high, y, x, low] = (
                grads[high, y, x, low, :, cut(base, half)].astype(FLOAT)
                + landed[high, y, x, low].astype(FLOAT)
            ).astype(HALF)


def reduce_kernel(mix, ffn, sums, tail, mix_owned, ffn_owned, tokens, halo, *scratch):
    mix_landed, mix_total, mix_mate, ffn_landed, ffn_total, ffn_rest, ffn_mate, work = scratch[:8]
    *landing, near_a, near_b, far_a, far_b, send, recv, local_sem = scratch[8:]
    mix_near, mix_far = landing_refs(MIX_REDUCE, landing[:MIX_LANDING])
    ffn_near, ffn_far = landing_refs(FFN_REDUCE, landing[MIX_LANDING:])
    here = Here()
    mail = Mail(send, recv)
    x = here.at["x"]
    load = pltpu.make_async_copy(sums, work, local_sem.at[0])
    load.start()
    greet(
        near_list(here, ("x", "y", "z"))
        + [here.beside("x", 2), here.twin(), here.along(1), here.along(-1)]
    )
    mix_twin = twin_send(here, mail, mix, MIX_HALF, mix_landed)
    ffn_twin = twin_send(here, mail, ffn, FFN_HALF, ffn_landed)
    halo_in = mail.post(tail, halo, here.along(-1))
    load.wait()
    stream = RingReduce(here, mail, "x", row_pick(work), (near_a, near_b), (far_a, far_b))
    stream.start()
    mix_twin.wait_recv()
    twin_sum(here, mix, MIX_HALF, mix_landed, mix_total)
    mix_rings = reduce_rings(here, mail, mix_total, MIX_PARTS, MIX_REDUCE, mix_near, mix_far, 0)
    for ring in mix_rings:
        ring.start()
    stream.relay()
    ffn_twin.wait_recv()
    twin_sum(here, ffn, FFN_HALF, ffn_landed, ffn_total)
    ffn_rings = reduce_rings(here, mail, ffn_total, FFN_PARTS, FFN_REDUCE, ffn_near, ffn_far, 0)
    for ring in ffn_rings:
        ring.start()
    for ring in mix_rings + ffn_rings:
        ring.relay()
    for ring in mix_rings + ffn_rings + [stream]:
        ring.finish()
    tokens[...] = work[x].astype(FLOAT)
    run_rings(
        reduce_rings(here, mail, mix_total, MIX_PARTS, MIX_REDUCE, mix_near, mix_far, 1)
        + reduce_rings(here, mail, ffn_total, FFN_PARTS, FFN_REDUCE, ffn_near, ffn_far, 1)
    )
    copies = []
    for step in (1, 3, 2):
        there = here.ring("x", step)
        copies.append(
            mail.post(
                blocks(ffn_total, {**here.at, "x": there}, slice(None)),
                ffn_rest.at[x],
                here.beside("x", step),
            )
        )
    ffn_rest[x] = blocks(ffn_total, here.at, slice(None))[...]
    run_rings(reduce_rings(here, mail, mix_total, MIX_PARTS, MIX_REDUCE, mix_near, mix_far, 2))
    own = blocks(mix_total, here.at, slice(None))
    mix_swap = mail.post(own, mix_mate, here.twin())
    for copy in copies:
        copy.wait_recv()
    ffn_swap = mail.post(ffn_rest, ffn_mate, here.twin())
    mix_owned[:, cut(here.core * MIX_HALF, MIX_HALF)] = own[...].astype(FLOAT)
    ffn_owned[:, :, cut(here.core * FFN_HALF, FFN_HALF)] = ffn_rest[...].astype(FLOAT)
    mix_swap.wait_recv()
    mix_owned[:, cut((1 - here.core) * MIX_HALF, MIX_HALF)] = mix_mate[...].astype(FLOAT)
    ffn_swap.wait_recv()
    ffn_owned[:, :, cut((1 - here.core) * FFN_HALF, FFN_HALF)] = ffn_mate[...].astype(FLOAT)
    halo_in.wait_recv()
    mail.close()


def vmem():
    return pl.BlockSpec(memory_space=pltpu.VMEM)


def anywhere():
    return pl.BlockSpec(memory_space=pl.ANY)


def sems(count):
    return pltpu.SemaphoreType.DMA((count,))


def params(number):
    return pltpu.CompilerParams(
        collective_id=number, has_side_effects=True, vmem_limit_bytes=VMEM_LIMIT
    )


def shape(dims, dtype):
    return jax.ShapeDtypeStruct(dims, dtype)


def gather(own, tail, back):
    return pl.pallas_call(
        gather_kernel,
        out_shape=(
            shape(GRID + (16, MIX_COLS), HALF),
            shape(GRID + (16, FFN_COLS), HALF),
            shape((4, 128, D), HALF),
            shape((16, D), HALF),
        ),
        in_specs=[vmem()] * 3,
        out_specs=(anywhere(), anywhere(), anywhere(), vmem()),
        scratch_shapes=[
            pltpu.VMEM((16, OWN_COLS), HALF),
            pltpu.VMEM((16, OWN_COLS), HALF),
            sems(88),
            sems(88),
            sems(3),
        ],
        compiler_params=params(0),
        name="gather",
    )(own, tail, back)


def gather_stream(rows):
    return pl.pallas_call(
        gather_stream_kernel,
        out_shape=shape((4, 128, D), HALF),
        in_specs=[vmem()],
        out_specs=vmem(),
        scratch_shapes=[sems(4), sems(4)],
        compiler_params=params(1),
        name="gather_stream",
    )(rows)


def reduce_stream(sums):
    return pl.pallas_call(
        reduce_stream_kernel,
        out_shape=shape((128, D), FLOAT),
        in_specs=[anywhere()],
        out_specs=vmem(),
        scratch_shapes=[pltpu.VMEM((4, 128, D), HALF)]
        + [pltpu.VMEM((128, D), HALF)] * 2
        + [pltpu.VMEM((64, D), HALF)] * 2
        + [sems(4), sems(4), sems(1)],
        compiler_params=params(2),
        name="reduce_stream",
    )(sums)


def reduce(mix, ffn, sums, tail):
    landing = [
        pltpu.VMEM(dims, HALF)
        for part in landing_shapes(MIX_PARTS, MIX_REDUCE) + landing_shapes(FFN_PARTS, FFN_REDUCE)
        for dims in part
    ]
    return pl.pallas_call(
        reduce_kernel,
        out_shape=(
            shape((16, MIX_COLS), FLOAT),
            shape((4, 16, FFN_COLS), FLOAT),
            shape((128, D), FLOAT),
            shape((8, D), FLOAT),
        ),
        in_specs=[vmem(), vmem(), anywhere(), vmem()],
        out_specs=(vmem(),) * 4,
        scratch_shapes=[
            pltpu.VMEM(GRID + (16, MIX_HALF), HALF),
            pltpu.VMEM(GRID + (16, MIX_HALF), HALF),
            pltpu.VMEM((16, MIX_HALF), HALF),
            pltpu.VMEM(GRID + (16, FFN_HALF), HALF),
            pltpu.VMEM(GRID + (16, FFN_HALF), HALF),
            pltpu.VMEM((4, 16, FFN_HALF), HALF),
            pltpu.VMEM((4, 16, FFN_HALF), HALF),
            pltpu.VMEM((4, 128, D), HALF),
        ]
        + landing
        + [pltpu.VMEM((128, D), HALF)] * 2
        + [pltpu.VMEM((64, D), HALF)] * 2
        + [sems(72), sems(72), sems(1)],
        compiler_params=params(3),
        name="reduce",
    )(mix, ffn, sums, tail)


def norm_scale(values):
    return lax.rsqrt(jnp.mean(values * values, axis=-1, keepdims=True) + EPS)


def dot(left, right):
    return jnp.dot(left, right, preferred_element_type=FLOAT)


def dot_nt(left, right):
    return jnp.einsum("ta,ba->tb", left, right, preferred_element_type=FLOAT)


def dot_tn(left, right):
    return jnp.einsum("ta,tb->ab", left, right, preferred_element_type=FLOAT)


def norm_back(normal, row_scale, gain_row, upstream):
    weighted = upstream * gain_row
    return row_scale * (
        weighted - normal * jnp.mean(weighted * normal, axis=-1, keepdims=True)
    )


def local(
    tokens,
    gain_mix,
    in_weight,
    conv_weight,
    out_weight,
    gain_ffn,
    gate_weight,
    up_weight,
    down_weight,
    live_counts,
    positions,
    cotangent,
):
    seq = lax.axis_index("seq")
    core = lax.rem(seq, 2)
    count = live_counts[0, 0]
    small = jnp.stack([gain_mix, gain_ffn, conv_weight[0], conv_weight[1], conv_weight[2]], axis=1)
    ffn_rows = [
        weight.reshape(8, 4, SLAB) for weight in (gate_weight, up_weight, jnp.transpose(down_weight))
    ]
    ffn_rows = jnp.concatenate(ffn_rows + [jnp.zeros((8, 4, FFN_COLS - 3 * SLAB), HALF)], axis=2)
    ffn_rows = ffn_rows.reshape(8, 4, 2, FFN_HALF).transpose(2, 0, 1, 3)
    mix_rows = jnp.concatenate(
        [in_weight, out_weight, jnp.pad(small, ((0, 0), (0, MIX_COLS - 4 * D - 5)))], axis=1
    )
    mix_rows = mix_rows.reshape(8, 2, MIX_HALF).transpose(1, 0, 2)
    own = jnp.concatenate([mix_rows, ffn_rows.reshape(2, 8, 4 * FFN_HALF)], axis=2)
    own = jnp.concatenate([own, own], axis=1)
    tail = jnp.pad(lax.dynamic_slice(tokens, (count - 2, 0), (2, D)), ((0, 14), (0, 0)))
    follows = (seq > 0).astype(FLOAT)
    keep = (jnp.arange(128, dtype=jnp.int32) < count).astype(FLOAT)[:, None]
    d_out = keep * cotangent.astype(FLOAT)
    first_ok = (positions >= 1).astype(FLOAT)[:, None]
    second_ok = (positions >= 2).astype(FLOAT)[:, None]

    mix, ffn, backs, halo = gather(own, tail, d_out.astype(HALF))
    mix = mix.reshape(D, MIX_COLS)
    w_in = mix[:, : 3 * D]
    w_out = mix[:, 3 * D : 4 * D]
    small_rows = jnp.transpose(mix[:, 4 * D : 4 * D + 8]).astype(FLOAT)
    gain_one, gain_two = small_rows[0], small_rows[1]
    taps = small_rows[2:5]

    x_all = jnp.concatenate([tokens, halo], axis=0).astype(FLOAT)
    scale_all = norm_scale(x_all)
    unit_all = x_all * scale_all
    normed = (unit_all * gain_one).astype(HALF)
    projected = dot(normed, w_in)
    b_all = projected[:, :D]
    c_part = projected[:128, D : 2 * D]
    v_all = projected[:, 2 * D :]
    mixed_all = b_all * v_all
    mixed = mixed_all[:128]
    extended = jnp.concatenate([follows * mixed_all[128:130], mixed], axis=0)
    one_back = extended[1:129]
    two_back = extended[:128]
    conv = taps[0] * mixed + first_ok * taps[1] * one_back + second_ok * taps[2] * two_back
    gated = (c_part * conv).astype(HALF)
    x_own = tokens.astype(FLOAT)
    resid = x_own + dot(gated, w_out)
    scale_two = norm_scale(resid)
    unit_two = resid * scale_two
    normed_two = (unit_two * gain_two).astype(HALF)

    twos = gather_stream(normed_two)
    ffn = ffn.reshape(D, FFN_COLS)
    w_gate, w_up, w_down = ffn[:, :SLAB], ffn[:, SLAB : 2 * SLAB], ffn[:, 2 * SLAB : 3 * SLAB]
    twos = twos.reshape(512, D)
    backs = backs.reshape(512, D)
    gate = dot(twos, w_gate)
    upper = dot(twos, w_up)
    sig = jax.nn.sigmoid(gate)
    swish = gate * sig
    active = (swish * upper).astype(HALF)
    d_active = dot(backs, w_down)
    d_gate = (d_active * upper * (sig * (1.0 + gate * (1.0 - sig)))).astype(HALF)
    d_upper = (d_active * swish).astype(HALF)
    ffn_sum = dot_nt(active, w_down).astype(HALF)
    two_sum = (dot_nt(d_gate, w_gate) + dot_nt(d_upper, w_up)).astype(HALF)
    ffn_grads = jnp.concatenate(
        [
            dot_tn(twos, d_gate).astype(HALF),
            dot_tn(twos, d_upper).astype(HALF),
            dot_tn(backs, active).astype(HALF),
            jnp.zeros((D, FFN_COLS - 3 * SLAB), HALF),
        ],
        axis=1,
    )
    d_two = reduce_stream(two_sum.reshape(4, 128, D))

    grad_gain_two = jnp.sum(d_two * unit_two, axis=0)
    d_resid = d_out + norm_back(unit_two, scale_two, gain_two, d_two)
    d_branch = d_resid.astype(HALF)
    grad_out = dot_tn(gated, d_branch).astype(HALF)
    d_gated = dot_nt(d_branch, w_out)
    d_c = d_gated * conv
    d_conv = d_gated * c_part
    grad_taps = [
        jnp.sum(d_conv * mixed, axis=0),
        jnp.sum(d_conv * first_ok * one_back, axis=0),
        jnp.sum(d_conv * second_ok * two_back, axis=0),
    ]
    term_one = first_ok * taps[1] * d_conv
    term_two = second_ok * taps[2] * d_conv
    d_ext = jnp.pad(term_one, ((1, 1), (0, 0))) + jnp.pad(term_two, ((0, 2), (0, 0)))
    d_mixed = d_ext[2:] + taps[0] * d_conv
    d_mixed_all = jnp.concatenate(
        [d_mixed, jnp.pad(follows * d_ext[:2], ((0, 14), (0, 0)))], axis=0
    )
    d_projected = jnp.concatenate(
        [d_mixed_all * v_all, jnp.pad(d_c, ((0, 16), (0, 0))), d_mixed_all * b_all], axis=1
    ).astype(HALF)
    grad_in = dot_tn(normed, d_projected).astype(HALF)
    d_normed_all = dot_nt(d_projected, w_in)
    grad_gain_one = jnp.sum(d_normed_all * unit_all, axis=0)
    small_grads = jnp.stack([grad_gain_one, grad_gain_two] + grad_taps, axis=1).astype(HALF)
    mix_grads = jnp.concatenate(
        [grad_in, grad_out, jnp.pad(small_grads, ((0, 0), (0, MIX_COLS - 4 * D - 5)))], axis=1
    )
    owned_mix, owned_ffn, ffn_out, back_rows = reduce(
        mix_grads.reshape(GRID + (16, MIX_COLS)),
        ffn_grads.reshape(GRID + (16, FFN_COLS)),
        ffn_sum.reshape(4, 128, D),
        d_normed_all[128:136],
    )
    mixed_out = (keep * (resid + ffn_out)).astype(HALF)
    slots = jnp.arange(128, dtype=jnp.int32)[:, None]
    d_normed = (
        d_normed_all[:128]
        + (slots == count - 2).astype(FLOAT) * back_rows[0]
        + (slots == count - 1).astype(FLOAT) * back_rows[1]
    )
    d_norm_one = norm_back(unit_all[:128], scale_all[:128], gain_one, d_normed)
    grad_tokens = (d_resid + d_norm_one).astype(HALF)

    mine = lax.dynamic_slice(owned_mix, (8 * core, 0), (8, MIX_COLS))
    ffn_mine = lax.dynamic_slice(owned_ffn, (0, 8 * core, 0), (4, 8, FFN_COLS))
    ffn_mine = jnp.transpose(ffn_mine, (1, 0, 2))
    small_mine = jnp.transpose(mine[:, 4 * D : 4 * D + 5])
    return (
        mixed_out,
        grad_tokens,
        small_mine[0],
        mine[:, : 3 * D],
        small_mine[2:5],
        mine[:, 3 * D : 4 * D],
        small_mine[1],
        ffn_mine[:, :, :SLAB].reshape(8, 4 * SLAB),
        ffn_mine[:, :, SLAB : 2 * SLAB].reshape(8, 4 * SLAB),
        jnp.transpose(ffn_mine[:, :, 2 * SLAB : 3 * SLAB].reshape(8, 4 * SLAB)),
    )


def solution(mesh):
    rows = P(("fsdp", "seq"), None)
    flat = P(("fsdp", "seq"))
    cols = P(None, ("fsdp", "seq"))
    return jax.shard_map(
        local,
        mesh=mesh,
        in_specs=(rows, flat, rows, cols, rows, flat, rows, rows, cols, P("fsdp", "seq"), flat, rows),
        out_specs=(rows, rows, flat, rows, cols, rows, flat, rows, rows, cols),
        check_vma=False,
    )
```

time: 780 us -> 242 us (0.31); the launches traced: 768 us -> 240 us
  blocking collectives: 244 us -> 0 us
  waiting for transfers between devices: 229 us -> 0 us
  Pallas kernels: 0 us -> 161 us
  local copies, waits for them, and re-layouts: 104 us -> 14.3 us
  starting transfers between devices: 84.3 us -> 0 us
  matrix products: 59.2 us -> 41.4 us
  between operations: 16.6 us -> 1.9 us
  other arithmetic: 30.2 us -> 21.4 us
    all_gather x9 -> x0, blocking collectives: 226 us -> none  [the longest x1 32.6 us: local(): lax.all_gather(swapped[3], 'fsdp', axis=0, tiled=True)]
    pallas_call x0 -> x4, Pallas kernels: none -> 161 us  [the longest x1 71.5 us: reduce(): pl.pallas_call(reduce_kernel, out_shape=(shape((16, MIX_COLS), FLOAT), sh...]
    reduce_scatter x5 -> x0, waiting for transfers between devices: 149 us -> none  [the longest x1 76 us: local(): lax.psum_scatter((first_term + jnp.einsum('tf,df->td', d_upper, w_up, pre...]
    all_to_all x14 -> x0, starting transfers between devices: 83.5 us -> none  [the longest x1 10.8 us: local(): lax.all_to_all(lax.all_to_all(gain_grads.astype(jnp.bfloat16), 'fsdp', sp...]
    unnamed x148 -> x55, local copies, waits for them, and re-layouts: 51.3 us -> 1.97 us
    all_to_all x14 -> x0, waiting for transfers between devices: 40 us -> none  [the longest x1 8.29 us: local(): lax.all_to_all(grad_up.reshape(model_width, 1, 1, hid_part).astype(jnp.bf...]
    all_gather x4 -> x0, waiting for transfers between devices: 38.7 us -> none  [the longest x1 38.7 us: local(): stream_back = lax.all_gather(d_branch, 'seq', axis=0, tiled=True)]
    all_to_all x15 -> x0, local copies, waits for them, and re-layouts: 22.4 us -> none  [the longest x2 4.87 us: local(): lax.all_to_all(grad_up.reshape(model_width, 1, 1, hid_part).astype(jnp.bf...]
  transfers between devices with their start and end apart: 23 -> 0, of which waited for: 13 -> 0; matrix products, arithmetic and copies ran while one was open for 20% -> 0% of each run, Pallas kernels for 0% -> 0%
where the time goes in v1:
time: 242 us; the launch traced here: 240 us
  Pallas kernels  161 us (67%)
  matrix products  41.4 us (17%)
  other arithmetic  21.4 us (9%)
  local copies, waits for them, and re-layouts  14.3 us (6%)
    pallas_call x1, Pallas kernels, reduce(): pl.pallas_call(reduce_kernel, out_shape=(shape((16, MIX_COLS), FLOAT), sh...  71.5 us
    pallas_call x1, Pallas kernels, gather(): pl.pallas_call(gather_kernel, out_shape=(shape(GRID + (16, MIX_COLS), HAL...  63.3 us
    dot_general x5, matrix products, dot(): return jnp.dot(left, right, preferred_element_type=FLOAT)  17 us
    dot_general x5, matrix products, dot_nt(): return jnp.einsum('ta,ba->tb', left, right, preferred_element_type=FLOAT)  15.3 us
    pallas_call x1, Pallas kernels, gather_stream(): pl.pallas_call(gather_stream_kernel, out_shape=shape((4, 128, D), HALF),...  14.9 us
    pallas_call x1, Pallas kernels, reduce_stream(): pl.pallas_call(reduce_stream_kernel, out_shape=shape((128, D), FLOAT), in...  11.7 us
    dot_general x5, matrix products, dot_tn(): return jnp.einsum('ta,tb->ab', left, right, preferred_element_type=FLOAT)  9.07 us

profile of v1, /device:TPU:1, one launch (start us, length us, event | category | flops | bytes accessed | tf_op | source)
XLA Modules:
  0.0 240.5 jit_solution(2852442546877709522)
XLA Ops:
  5.9 1.0 maximum_maximum_fusion.2
  7.0 1.8 fusion.43.back
  8.7 0.9 maximum_maximum_fusion.1.own
  9.6 63.3 %gather.1 = (bf16[2,4,4,2,16,4352]{5,4,3,2,1,0:T(8,128)(2,1)}, bf16[2,4,4,2,16,3584]{5,4,3,2,1,0:T(8,128)(2,1)}, bf16[4,128,1024]{2,1,0:T(8,128)(2,1)}, bf16[16,1024]{1,0:T(8,128)(2,1)}) custom-call(bf16[2,16,9344]{2,1,0:T(8,128)(2,1)} %maximum_maximum_fusion.1.own, bf16[16,1024]{1,0:T(8,128)(2,1)} %pad.30.tail, bf16[128,1024]{1,0:T(8,128)(2,1)} %fusion.43.back), custom_call_target="tpu_custom_call" | custom-call | tf_op jit(solution)/shard_map/gather/pallas_call | solution.py:474
  72.9 0.9 fusion.35
  73.8 1.0 slice.160
  75.0 4.0 %fusion.4 = f32[144,3072]{1,0:T(8,128)S(1)} fusion(bf16[1024,4352]{1,0:T(8,128)(2,1)} %bitcast.76, f32[1024]{0:T(1024)S(1)} %bitcast.90, f32[144]{0:T(256)S(1)} %add_rsqrt_fusion, bf16[16,1024]{1,0:T(8,128)(2,1)} %get-tuple-element.18, bf16[128,1024]{1,0:T(8,128)(2,1)S(1)} %copy-done.12), kind=kOutput, calls=%fused_computation.7 | convolution fusion | flops 907001856 | bytes 8360512 | tf_op jit(solution)/shard_map/dot_general | solution.py:563
  79.4 2.2 multiply_reduce_fusion.7
  82.5 14.9 %gather_stream.1 = bf16[4,128,1024]{2,1,0:T(8,128)(2,1)} custom-call(bf16[128,1024]{1,0:T(8,128)(2,1)} %multiply_convert_fusion.8.rows), custom_call_target="tpu_custom_call" | custom-call | tf_op jit(solution)/shard_map/gather_stream/pallas_call | solution.py:497
  97.4 3.6 %fusion.9 = f32[512,1152]{1,0:T(8,128)S(1)} fusion(bf16[512,1024]{1,0:T(8,128)(2,1)} %bitcast.68, bf16[1024,3584]{1,0:T(8,128)(2,1)} %bitcast.106), kind=kOutput, calls=%fused_computation.22 | convolution fusion | flops 1207959552 | bytes 5767168 | tf_op jit(solution)/shard_map/dot_general | solution.py:563
  101.0 3.3 %fusion.17 = f32[512,1152]{1,0:T(8,128)S(1)} fusion(bf16[512,1024]{1,0:T(8,128)(2,1)S(1)} %bitcast.114, bf16[1024,3584]{1,0:T(8,128)(2,1)} %bitcast.107), kind=kOutput, calls=%fused_computation.30 | convolution fusion | flops 1207959552 | bytes 5767168 | tf_op jit(solution)/shard_map/dot_general | solution.py:563
  104.4 3.9 %multiply_convert_fusion = (bf16[512,1152]{1,0:T(8,128)(2,1)S(1)}, bf16[512,1152]{1,0:T(8,128)(2,1)S(1)}, bf16[512,1152]{1,0:T(8,128)(2,1)S(1)}) fusion(f32[512,1152]{1,0:T(8,128)S(1)} %fusion.9, f32[512,1152]{1,0:T(8,128)S(1)} %fusion.17, bf16[512,1024]{1,0:T(8,128)(2,1)S(1)} %bitcast.70, bf16[1024,3584]{1,0:T(8,128)(2,1)} %bitcast.108), kind=kOutput, calls=%fused_computation.14 | convolution fusion | flops 1216806912 | bytes 11665408 | tf_op jit(solution)/shard_map/dot_general | solution.py:563
  108.3 2.5 %fusion.25 = bf16[512,1024]{1,0:T(8,128)(2,1)} fusion(bf16[512,1152]{1,0:T(8,128)(2,1)S(1)} %get-tuple-element.66, bf16[1024,3584]{1,0:T(8,128)(2,1)S(1)} %bitcast.111), kind=kOutput, calls=%fused_computation.39 | convolution fusion | flops 1208483840 | bytes 4587520 | tf_op jit(solution)/shard_map/ta,ba->tb/dot_general | solution.py:567
  110.9 1.6 convolution_convert_fusion.1
  112.5 1.7 fusion.7
  114.2 2.6 %add_convert_fusion = bf16[512,1024]{1,0:T(8,128)(2,1)} fusion(f32[512,1024]{1,0:T(8,128)S(1)} %fusion.7, bf16[512,1152]{1,0:T(8,128)(2,1)S(1)} %get-tuple-element.68, bf16[1024,3584]{1,0:T(8,128)(2,1)S(1)} %bitcast.113), kind=kOutput, calls=%fused_computation.19 | convolution fusion | flops 1209008128 | bytes 6684672 | tf_op jit(solution)/shard_map/ta,ba->tb/dot_general | solution.py:567
  116.8 11.7 %reduce_stream.1 = f32[128,1024]{1,0:T(8,128)} custom-call(bf16[4,128,1024]{2,1,0:T(8,128)(2,1)} %bitcast.72), custom_call_target="tpu_custom_call" | custom-call | tf_op jit(solution)/shard_map/reduce_stream/pallas_call | solution.py:509
  128.5 1.3 multiply_reduce_fusion.5
  129.8 1.2 multiply_add_fusion
  131.1 2.6 %multiply_reduce_fusion.2 = (bf16[1024]{0:T(1024)(128)(2,1)S(1)}, bf16[1024]{0:T(1024)(128)(2,1)S(1)}, bf16[1024]{0:T(1024)(128)(2,1)S(1)}, f32[128,1024]{1,0:T(8,128)S(1)}, bf16[128,1024]{1,0:T(8,128)(2,1)S(1)}) fusion(f32[128,1024]{1,0:T(8,128)S(1)} %slice.167, f32[2,1024]{1,0:T(2,128)S(1)} %slice_multiply_fusion.2, f32[128]{0:T(128)S(1)} %get-tuple-element.90, ...), kind=kOutput, calls=%fused_computation.74 | convolution fusion | flops 270267392 | bytes 5520384 | tf_op jit(solution)/shard_map/ta,ba->tb/dot_general | solution.py:567
  134.8 5.9 %convert_multiply_fusion = (f32[144,1024]{1,0:T(8,128)}, bf16[1024]{0:T(1024)(128)(2,1)S(1)}, f32[144,1024]{1,0:T(8,128)}) fusion(f32[144]{0:T(256)S(1)} %add_rsqrt_fusion, bf16[16,1024]{1,0:T(8,128)(2,1)S(1)} %copy-done.18, bf16[128,1024]{1,0:T(8,128)(2,1)S(1)} %copy-done.13, bf16[1024,4352]{1,0:T(8,128)(2,1)} %bitcast.79, ...), kind=kOutput, calls=%fused_computation.47 | convolution fusion | flops 911424512 | bytes 8620608 | tf_op jit(solution)/shard_map/ta,ba->tb/dot_general | solution.py:567
  140.8 1.4 slice.180.tail
  143.1 3.3 %convolution_convert_fusion.2 = bf16[1024,1152]{1,0:T(8,128)(2,1)S(1)} fusion(bf16[512,1024]{1,0:T(8,128)(2,1)} %bitcast.69, bf16[512,1152]{1,0:T(8,128)(2,1)} %copy-done.21), kind=kOutput, calls=%fused_computation.10 | convolution fusion | flops 1209139200 | bytes 4587520 | tf_op jit(solution)/shard_map/ta,tb->ab/dot_general | solution.py:571
  146.4 1.6 convolution_convert_fusion.3
  148.0 4.0 %maximum_maximum_fusion = bf16[1024,3584]{1,0:T(8,128)(2,1)} fusion(bf16[1024,1152]{1,0:T(8,128)(2,1)S(1)} %convolution_convert_fusion.1, bf16[1024,1152]{1,0:T(8,128)(2,1)S(1)} %convolution_convert_fusion.2, bf16[1024,1152]{1,0:T(8,128)(2,1)S(1)} %convolution_convert_fusion.3, bf16[3584]{0:T(1024)(128)(2,1)S(1)} %pad.59.clone), kind=kLoop, calls=%fused_computation.3 | loop fusion | flops 29360128 | bytes 14425088 | tf_op jit(solution)/shard_map/concatenate | solution.py:661
  153.2 1.9 convolution_convert_fusion
  155.2 3.8 %fusion.1 = bf16[1024,4352]{1,0:T(8,128)(2,1)} fusion(bf16[1024,5]{1,0:T(8,128)(2,1)S(1)} %copy-done.2, bf16[1024,1024]{1,0:T(8,128)(2,1)S(1)} %convolution_convert_fusion.4, bf16[1024,3072]{1,0:T(8,128)(2,1)S(1)} %convolution_convert_fusion), kind=kLoop, calls=%fused_computation.2 | loop fusion | flops 35651584 | bytes 17311744 | tf_op jit(solution)/shard_map/concatenate | solution.py:698
  159.0 71.5 %reduce.5 = (f32[16,4352]{1,0:T(8,128)}, f32[4,16,3584]{2,1,0:T(8,128)}, f32[128,1024]{1,0:T(8,128)}, f32[8,1024]{1,0:T(8,128)}) custom-call(bf16[2,4,4,2,16,4352]{5,4,3,2,1,0:T(8,128)(2,1)} %bitcast.65, bf16[2,4,4,2,16,3584]{5,4,3,2,1,0:T(8,128)(2,1)} %bitcast.66, bf16[4,128,1024]{2,1,0:T(8,128)(2,1)} %bitcast.67, f32[8,1024]{1,0:T(8,128)} %slice.180.tail), custom_call_target="tpu_custom_call" | custom-call | tf_op jit(solution)/shard_map/reduce/pallas_call | solution.py:529
  230.6 1.9 multiply_convert_fusion.6
  235.8 1.0 add_convert_fusion.1
  236.7 1.4 dynamic-slice.2
  238.1 1.5 constant_dynamic-slice_fusion
  (100 shorter events, 13.3 us)
Async XLA Ops:
  0.6 72.3 %copy-start.12 = (bf16[128,1024]{1,0:T(8,128)(2,1)S(1)}, bf16[128,1024]{1,0:T(8,128)(2,1)}, u32[]{:S(2)}) copy-start(bf16[128,1024]{1,0:T(8,128)(2,1)} %param.12) | copy-start | bytes 786436
  73.8 79.0 %copy-start.19 = (f32[144]{0:T(256)}, f32[144]{0:T(256)S(1)}, u32[]{:S(2)}) copy-start(f32[144]{0:T(256)S(1)} %add_rsqrt_fusion) | copy-start | bytes 1732
  79.4 17.9 %copy-start.5 = (bf16[128,1024]{1,0:T(8,128)(2,1)}, bf16[128,1024]{1,0:T(8,128)(2,1)S(1)}, u32[]{:S(2)}) copy-start(bf16[128,1024]{1,0:T(8,128)(2,1)S(1)} %get-tuple-element.64) | copy-start | bytes 786436
  97.4 3.6 %copy-start.20 = (bf16[4,128,1024]{2,1,0:T(8,128)(2,1)S(1)}, bf16[4,128,1024]{2,1,0:T(8,128)(2,1)}, u32[]{:S(2)}) copy-start(bf16[4,128,1024]{2,1,0:T(8,128)(2,1)} %get-tuple-element.20) | copy-start | bytes 3145732
  101.0 3.4 %copy-start.3 = (bf16[4,128,1024]{2,1,0:T(8,128)(2,1)S(1)}, bf16[4,128,1024]{2,1,0:T(8,128)(2,1)}, u32[]{:S(2)}) copy-start(bf16[4,128,1024]{2,1,0:T(8,128)(2,1)} %gather_stream.1) | copy-start | bytes 3145732
  101.0 7.3 %slice-start.1 = ((s8[7340032]{0:T(1024)(128)(4,1)}), s8[4194304]{0:T(1024)(128)(4,1)S(1)}, s32[]{:S(2)}) async-start(s8[7340032]{0:T(1024)(128)(4,1)} %bitcast.109), calls=%async_computation.1 | async-start | bytes 8388608
  104.4 4.0 %slice-start.2 = ((s8[7340032]{0:T(1024)(128)(4,1)}), s8[3145728]{0:T(1024)(128)(4,1)S(1)}, s32[]{:S(2)}) async-start(s8[7340032]{0:T(1024)(128)(4,1)} %bitcast.109), calls=%async_computation.2 | async-start | bytes 6291456
  108.3 4.2 %copy-start.22 = (bf16[512,1152]{1,0:T(8,128)(2,1)}, bf16[512,1152]{1,0:T(8,128)(2,1)S(1)}, u32[]{:S(2)}) copy-start(bf16[512,1152]{1,0:T(8,128)(2,1)S(1)} %get-tuple-element.67) | copy-start | bytes 3538948
  108.3 5.9 %copy-start.21 = (bf16[512,1152]{1,0:T(8,128)(2,1)}, bf16[512,1152]{1,0:T(8,128)(2,1)S(1)}, u32[]{:S(2)}) copy-start(bf16[512,1152]{1,0:T(8,128)(2,1)S(1)} %get-tuple-element.68) | copy-start | bytes 3538948
  116.8 13.0 %copy-start.7 = (bf16[128,1024]{1,0:T(8,128)(2,1)S(1)}, bf16[128,1024]{1,0:T(8,128)(2,1)}, u32[]{:S(2)}) copy-start(bf16[128,1024]{1,0:T(8,128)(2,1)} %param.23) | copy-start | bytes 786436
  133.7 0.7 copy-start.15
  133.9 1.0 copy-start.13
  133.9 0.9 copy-start.18
  134.2 6.5 %copy-start.8 = (bf16[144,1024]{1,0:T(8,128)(2,1)}, bf16[144,1024]{1,0:T(8,128)(2,1)S(1)}, u32[]{:S(2)}) copy-start(bf16[144,1024]{1,0:T(8,128)(2,1)S(1)} %get-tuple-element.69) | copy-start | bytes 884740
  134.3 6.5 %copy-start.10 = (bf16[144,1024]{1,0:T(8,128)(2,1)}, bf16[144,1024]{1,0:T(8,128)(2,1)S(1)}, u32[]{:S(2)}) copy-start(bf16[144,1024]{1,0:T(8,128)(2,1)S(1)} %get-tuple-element.70) | copy-start | bytes 884740
  143.1 3.3 %copy-start.4 = (bf16[4,128,1024]{2,1,0:T(8,128)(2,1)S(1)}, bf16[4,128,1024]{2,1,0:T(8,128)(2,1)}, u32[]{:S(2)}) copy-start(bf16[4,128,1024]{2,1,0:T(8,128)(2,1)} %gather_stream.1) | copy-start | bytes 3145732
  143.1 3.3 %copy-start.23 = (bf16[512,1152]{1,0:T(8,128)(2,1)S(1)}, bf16[512,1152]{1,0:T(8,128)(2,1)}, u32[]{:S(2)}) copy-start(bf16[512,1152]{1,0:T(8,128)(2,1)} %copy-done.22) | copy-start | bytes 3538948
  148.0 4.1 %copy-start.6 = (bf16[128,1024]{1,0:T(8,128)(2,1)S(1)}, bf16[128,1024]{1,0:T(8,128)(2,1)}, u32[]{:S(2)}) copy-start(bf16[128,1024]{1,0:T(8,128)(2,1)} %copy-done.5) | copy-start | bytes 786436
  152.0 1.0 copy-start.9
  152.0 1.0 copy-start.11
  152.0 1.1 copy-start.14
  152.0 1.2 copy-start.16
  153.2 1.9 copy-start.2
  159.0 76.4 %copy-start = (f32[144,1024]{1,0:T(8,128)S(1)}, f32[144,1024]{1,0:T(8,128)}, u32[]{:S(2)}) copy-start(f32[144,1024]{1,0:T(8,128)} %get-tuple-element.93) | copy-start | bytes 1769476
  159.0 76.4 %copy-start.1 = (f32[144,1024]{1,0:T(8,128)S(1)}, f32[144,1024]{1,0:T(8,128)}, u32[]{:S(2)}) copy-start(f32[144,1024]{1,0:T(8,128)} %get-tuple-element.77) | copy-start | bytes 1769476
  230.5 5.2 %slice-start = ((f32[144]{0:T(256)}), f32[128]{0:T(128)S(1)}, s32[]{:S(2)}) async-start(f32[144]{0:T(256)} %copy-done.19), calls=%async_computation | async-start | bytes 1024 | tf_op jit(solution)/shard_map/slice | solution.py:714
  230.6 7.5 %copy-start.17 = (f32[4,16,3584]{2,1,0:T(8,128)S(1)}, f32[4,16,3584]{2,1,0:T(8,128)}, u32[]{:S(2)}) copy-start(f32[4,16,3584]{2,1,0:T(8,128)} %get-tuple-element.25) | copy-start | bytes 2752516

commit v2 on v1

v2 whole, which is shorter than its diff:
```python
import jax
import jax.numpy as jnp
from jax import lax
from jax.experimental import pallas as pl
from jax.experimental.pallas import tpu as pltpu
from jax.sharding import PartitionSpec as P

EPS = 1e-05
FLOAT = jnp.float32
HALF = jnp.bfloat16
MESH = pl.DeviceIdType.MESH
LANE = 128
D = 1024
SLAB = 1152
MIX_COLS = 34 * LANE
FFN_COLS = 28 * LANE
MIX_HALF = MIX_COLS // 2
FFN_HALF = FFN_COLS // 2
OWN_COLS = MIX_HALF + 4 * FFN_HALF
HALF_D = D // 2
OUT_AT = 3 * HALF_D
SMALL_AT = 4 * HALF_D
TILE = 256
TOK = 128
ALL = TOK + 16
MIX_PARTS = ((0, 9), (9, 4), (13, 4))
MIX_GATHER = (("y", "z", "x"), ("z", "x", "y"), ("x", "y", "z"))
MIX_REDUCE = (("x", "z", "y"), ("y", "x", "z"), ("z", "y", "x"))
FFN_PARTS = ((0, 7), (7, 7))
FFN_GATHER = (("y", "z"), ("z", "y"))
FFN_REDUCE = (("y", "z"), ("z", "y"))
GRID = (2, 4, 4, 2)
MIX_LANDING = 4 * 3 * len(MIX_PARTS)
VMEM_LIMIT = 60 * 2**20


class Here:
    def __init__(self):
        fsdp = lax.axis_index("fsdp")
        seq = lax.axis_index("seq")
        self.fsdp, self.seq = fsdp, seq
        self.at = {
            "x": lax.div(seq, 4),
            "y": lax.rem(fsdp, 4),
            "z": lax.div(fsdp, 4) * 2 + lax.rem(lax.div(seq, 2), 2),
        }
        self.core = lax.rem(seq, 2)

    def device(self, core, **moved):
        at = {**self.at, **moved}
        return (
            lax.div(at["z"], 2) * 4 + at["y"],
            (at["x"] * 2 + lax.rem(at["z"], 2)) * 2 + core,
        )

    def ring(self, axis, step):
        return lax.rem(self.at[axis] + (step + 4) % 4, 4)

    def beside(self, axis, step):
        return self.device(self.core, **{axis: self.ring(axis, step)})

    def twin(self):
        return self.device(1 - self.core)

    def along(self, step):
        return (self.fsdp, lax.rem(self.seq + (step + 16) % 16, 16))


def greet(devices):
    barrier = pltpu.get_barrier_semaphore()
    for device in devices:
        pl.semaphore_signal(barrier, inc=1, device_id=device, device_id_type=MESH)
    pl.semaphore_wait(barrier, len(devices))


class Mail:
    def __init__(self, send, recv):
        self.send, self.recv, self.posted = send, recv, []

    def post(self, src, dst, device):
        place = len(self.posted)
        copy = pltpu.make_async_remote_copy(
            src_ref=src,
            dst_ref=dst,
            send_sem=self.send.at[place],
            recv_sem=self.recv.at[place],
            device_id=device,
            device_id_type=MESH,
        )
        copy.start()
        self.posted.append(copy)
        return copy

    def close(self):
        for copy in self.posted:
            copy.wait_send()


def cut(start, count):
    return pl.ds(pl.multiple_of(start, LANE), count)


def blocks(ref, at, cols):
    whole = slice(None)
    z = at["z"]
    high, low = (whole, whole) if z is None else (lax.div(z, 2), lax.rem(z, 2))
    y = whole if at["y"] is None else at["y"]
    x = whole if at["x"] is None else at["x"]
    return ref.at[high, y, x, low, :, cols]


class RingGather:
    def __init__(self, here, mail, axis, pick):
        self.here, self.mail, self.axis, self.pick = here, mail, axis, pick

    def start(self, source=None):
        here, axis = self.here, self.axis
        own = self.pick(here.at[axis], None)
        source = own if source is None else source
        self.to_up = self.mail.post(source, own, here.beside(axis, 1))
        self.to_down = self.mail.post(source, own, here.beside(axis, -1))

    def relay(self):
        here, axis = self.here, self.axis
        self.to_up.wait_recv()
        first = self.pick(here.ring(axis, -1), 0)
        self.far_up = self.mail.post(first, first, here.beside(axis, 1))
        self.to_down.wait_recv()
        second = self.pick(here.ring(axis, 1), 1)
        self.far_down = self.mail.post(second, second, here.beside(axis, -1))

    def finish(self):
        self.far_up.wait_recv()
        self.far_down.wait_recv()


class RingReduce:
    def __init__(self, here, mail, axis, pick, near, far):
        self.here, self.mail, self.axis, self.pick = here, mail, axis, pick
        self.near, self.far = near, far

    def start(self):
        here, axis = self.here, self.axis
        away = here.ring(axis, 2)
        self.far_up = self.mail.post(self.pick(away, 0), self.far[0], here.beside(axis, 1))
        self.far_down = self.mail.post(self.pick(away, 1), self.far[1], here.beside(axis, -1))

    def relay(self):
        here, axis = self.here, self.axis
        above, below = here.ring(axis, 1), here.ring(axis, -1)
        self.far_up.wait_recv()
        add_into(self.pick(above, 0), self.far[0])
        self.to_up = self.mail.post(self.pick(above, None), self.near[0], here.beside(axis, 1))
        self.far_down.wait_recv()
        add_into(self.pick(below, 1), self.far[1])
        self.to_down = self.mail.post(self.pick(below, None), self.near[1], here.beside(axis, -1))

    def finish(self):
        self.to_up.wait_recv()
        self.to_down.wait_recv()
        own = self.pick(self.here.at[self.axis], None)
        add_into(own, self.near[0], self.near[1])


def add_into(target, *terms):
    total = target[...].astype(FLOAT)
    for term in terms:
        total = total + term[...].astype(FLOAT)
    target[...] = total.astype(target.dtype)


def column_pick(ref, fixed, axis, start, chunks):
    split = (chunks + 1) // 2

    def pick(place, half):
        first, count = {None: (0, chunks), 0: (0, split), 1: (split, chunks - split)}[half]
        return blocks(ref, {**fixed, axis: place}, cut(start + first * LANE, count * LANE))

    return pick


def row_pick(ref):
    def pick(place, half):
        rows = ref.shape[-2]
        part = {None: slice(None), 0: pl.ds(0, rows // 2), 1: pl.ds(rows // 2, rows // 2)}[half]
        return ref.at[place, part]

    return pick


def gather_rings(here, mail, ref, base, parts, orders, stage):
    rings = []
    for (first, chunks), order in zip(parts, orders):
        fixed = dict(here.at)
        for axis in ("x", "y", "z"):
            if axis not in order or axis in order[:stage]:
                fixed[axis] = None
        pick = column_pick(ref, fixed, order[stage], base + first * LANE, chunks)
        rings.append(RingGather(here, mail, order[stage], pick))
    return rings


def start_all(rings):
    for ring in rings:
        ring.start()


def relay_all(rings):
    for ring in rings:
        ring.relay()


def finish_all(rings):
    for ring in rings:
        ring.finish()


def run_rings(rings):
    start_all(rings)
    relay_all(rings)
    finish_all(rings)


def swap_pieces(here, mail, rings, steps):
    copies = []
    for ring in rings:
        for step in steps:
            piece = ring.pick(here.ring(ring.axis, step), None)
            copies.append(mail.post(piece, piece, here.twin()))
    return copies


def wait_all(copies):
    for copy in copies:
        copy.wait_recv()


def near_list(here, axes):
    return [here.beside(axis, step) for axis in axes for step in (1, -1)]


def mat(ref, cols):
    block = ref[:, :, :, :, :, cols]
    return block.reshape(D, block.shape[-1])


def mat_rows(ref, tile, cols):
    block = ref[lax.div(tile, 2), pl.ds(lax.rem(tile, 2) * 2, 2), :, :, :, cols]
    return block.reshape(TILE, block.shape[-1])


def mix_cols(tile, which):
    return cut(lax.div(tile, 2) * MIX_HALF + which * HALF_D + lax.rem(tile, 2) * TILE, TILE)


def dot(left, right):
    return jnp.dot(left, right, preferred_element_type=FLOAT)


def dot_nt(left, right):
    return lax.dot_general(
        left, right, (((1,), (1,)), ((), ())), preferred_element_type=FLOAT
    )


def norm_scale(values):
    return lax.rsqrt(jnp.mean(values * values, axis=-1, keepdims=True) + EPS)


def norm_back(normal, row_scale, gain_row, upstream):
    weighted = upstream * gain_row
    return row_scale * (
        weighted - normal * jnp.mean(weighted * normal, axis=-1, keepdims=True)
    )


def row_index(rows, cols):
    return lax.broadcasted_iota(jnp.int32, (rows, cols), 0)


def conv_terms(mixed, halo):
    rows = row_index(TOK, mixed.shape[1])
    one = pltpu.roll(mixed, 1, 0)
    two = pltpu.roll(mixed, 2, 0)
    one = jnp.where(rows == 0, halo[1:2], one)
    two = jnp.where(rows == 0, halo[0:1], jnp.where(rows == 1, halo[1:2], two))
    return one, two


def follows_of(here):
    return jnp.minimum(here.seq, 1).astype(FLOAT)


def mixer_forward(here, tokens, halo, flags, mix, proj, normed, gated, resid, rows, two):
    small = jnp.transpose(mat(mix, slice(SMALL_AT, SMALL_AT + LANE)).astype(FLOAT))
    rows[...] = small[0:8]
    gain = rows[0:1]
    x = tokens[...].astype(FLOAT)
    normed[0:TOK] = (x * norm_scale(x) * gain).astype(HALF)
    before = halo[...].astype(FLOAT)
    normed[TOK:ALL] = (before * norm_scale(before) * gain).astype(HALF)
    follows = follows_of(here)
    first_ok, second_ok = flags[:, 0:1], flags[:, 1:2]

    @pl.loop(0, D // TILE)
    def _(tile):
        feats = cut(tile * TILE, TILE)
        parts = [dot(normed[...], mat(mix, mix_cols(tile, which))) for which in range(3)]
        for which in range(3):
            proj[which, :, feats] = parts[which]
        mixed = parts[0] * parts[2]
        own = mixed[0:TOK]
        one, second = conv_terms(own, mixed[TOK:ALL] * follows)
        conv = (
            rows[2:3, feats] * own
            + first_ok * rows[3:4, feats] * one
            + second_ok * rows[4:5, feats] * second
        )
        gated[:, feats] = (parts[1][0:TOK] * conv).astype(HALF)

    @pl.loop(0, D // TILE)
    def _(tile):
        feats = cut(tile * TILE, TILE)
        branch = dot(gated[...], mat(mix, mix_cols(tile, 3)))
        resid[:, feats] = tokens[:, feats].astype(FLOAT) + branch

    value = resid[...]
    two[...] = (value * norm_scale(value) * rows[1:2]).astype(HALF)


def forward_kernel(
    own, tail, back, tokens, flags,
    mix_out, ffn, backs, twos, proj, normed, gated, resid, rows, halo,
    mate, full, mix, two, send, recv, local_sem,
):
    here = Here()
    mail = Mail(send, recv)
    x = here.at["x"]
    keep_back = pltpu.make_async_copy(back, backs.at[x], local_sem.at[0])
    keep_back.start()
    greet(
        near_list(here, ("x", "y", "z"))
        + [here.beside("x", 2), here.twin(), here.along(1), here.along(-1)]
    )
    rows_in = mail.post(own.at[1 - here.core], mate, here.twin())
    halo_in = mail.post(tail, halo, here.along(1))
    rows_in.wait_recv()
    mine = lax.broadcasted_iota(jnp.int32, (16, OWN_COLS), 0) // 8 == here.core
    full[...] = jnp.where(mine, own[here.core].astype(FLOAT), mate[...].astype(FLOAT)).astype(HALF)

    mix_base, ffn_base = here.core * MIX_HALF, here.core * FFN_HALF
    ffn_own = blocks(ffn, here.at, cut(ffn_base, FFN_HALF))

    def slab(place):
        return full.at[:, cut(MIX_HALF + place * FFN_HALF, FFN_HALF)]

    rings = gather_rings(here, mail, mix, mix_base, MIX_PARTS, MIX_GATHER, 0)
    for ring, (first, chunks) in zip(rings, MIX_PARTS):
        ring.start(full.at[:, first * LANE : (first + chunks) * LANE])
    slabs = [
        mail.post(slab(here.ring("x", step)), ffn_own, here.beside("x", step)) for step in (1, 3, 2)
    ]
    keep_mix = pltpu.make_async_copy(
        full.at[:, 0:MIX_HALF], blocks(mix, here.at, cut(mix_base, MIX_HALF)), local_sem.at[1]
    )
    keep_slab = pltpu.make_async_copy(slab(x), ffn_own, local_sem.at[2])
    keep_mix.start()
    keep_slab.start()
    relay_all(rings)
    finish_all(rings)
    keep_mix.wait()
    keep_slab.wait()
    wait_all(slabs)
    mix_rings = gather_rings(here, mail, mix, mix_base, MIX_PARTS, MIX_GATHER, 1)
    ffn_rings = gather_rings(here, mail, ffn, ffn_base, FFN_PARTS, FFN_GATHER, 0)
    run_rings(mix_rings + ffn_rings)
    mix_rings = gather_rings(here, mail, mix, mix_base, MIX_PARTS, MIX_GATHER, 2)
    ffn_rings = gather_rings(here, mail, ffn, ffn_base, FFN_PARTS, FFN_GATHER, 1)
    start_all(mix_rings)
    swaps = swap_pieces(here, mail, mix_rings, (0,))
    relay_all(mix_rings)
    swaps += swap_pieces(here, mail, mix_rings, (1, -1))
    start_all(ffn_rings)
    stream = RingGather(here, mail, "x", row_pick(backs))
    stream.start(back)
    finish_all(mix_rings)
    swaps += swap_pieces(here, mail, mix_rings, (2,))
    ffn_swaps = swap_pieces(here, mail, ffn_rings, (0,))
    wait_all(swaps)
    halo_in.wait_recv()
    keep_all = pltpu.make_async_copy(mix, mix_out, local_sem.at[1])
    keep_all.start()
    mixer_forward(here, tokens, halo, flags, mix, proj, normed, gated, resid, rows, two)
    two_ring = RingGather(here, mail, "x", row_pick(twos))
    two_ring.start(two)
    keep_two = pltpu.make_async_copy(two, twos.at[x], local_sem.at[2])
    keep_two.start()
    relay_all(ffn_rings)
    stream.relay()
    ffn_swaps += swap_pieces(here, mail, ffn_rings, (1, -1))
    two_ring.relay()
    finish_all(ffn_rings)
    ffn_swaps += swap_pieces(here, mail, ffn_rings, (2,))
    stream.finish()
    two_ring.finish()
    wait_all(ffn_swaps)
    keep_back.wait()
    keep_two.wait()
    keep_all.wait()
    mail.close()


def reduce_rings(here, mail, ref, parts, orders, near, far, stage):
    rings = []
    for number, ((first, chunks), order) in enumerate(zip(parts, orders)):
        fixed = {"x": None, "y": None, "z": None}
        for axis in order[:stage]:
            fixed[axis] = here.at[axis]
        pick = column_pick(ref, fixed, order[stage], first * LANE, chunks)
        rings.append(
            RingReduce(here, mail, order[stage], pick, near[number][stage], far[number][stage])
        )
    return rings


def landing_shapes(parts, orders):
    shapes = []
    for (_, chunks), order in zip(parts, orders):
        split = (chunks + 1) // 2
        done = []
        for stage in range(len(order)):
            gone = order[: stage + 1]
            lead = ()
            if "z" not in gone:
                lead += (2,)
            if "y" not in gone:
                lead += (4,)
            if "x" not in gone:
                lead += (4,)
            if "z" not in gone:
                lead += (2,)
            for count, copies in ((chunks, 2), (split, 1), (chunks - split, 1)):
                done += [lead + (16, count * LANE)] * copies
        shapes.append(done)
    return shapes


def landing_refs(orders, refs):
    near, far = [], []
    place = 0
    for order in orders:
        near.append([])
        far.append([])
        for _ in order:
            near[-1].append(refs[place : place + 2])
            far[-1].append(refs[place + 2 : place + 4])
            place += 4
    return near, far


def twin_send(here, mail, grads, half, landed):
    other = (1 - here.core) * half
    return mail.post(grads.at[:, :, :, :, :, cut(other, half)], landed, here.twin())


def twin_sum(here, grads, half, landed, total):
    base = here.core * half

    @pl.loop(0, 32)
    def _(index):
        high, y = lax.div(index, 16), lax.rem(lax.div(index, 4), 4)
        x = lax.rem(index, 4)
        for low in range(2):
            total[high, y, x, low] = (
                grads[high, y, x, low, :, cut(base, half)].astype(FLOAT)
                + landed[high, y, x, low].astype(FLOAT)
            ).astype(HALF)


def mixer_backward(here, flags, mix, proj, rows, branch, grads, small):
    follows = follows_of(here)
    first_ok, second_ok = flags[:, 0:1], flags[:, 1:2]

    @pl.loop(0, D // TILE)
    def _(tile):
        feats = cut(tile * TILE, TILE)
        gated = dot_nt(branch[0], mat_rows(mix, tile, slice(OUT_AT, OUT_AT + HALF_D)))
        gated += dot_nt(
            branch[1], mat_rows(mix, tile, slice(MIX_HALF + OUT_AT, MIX_HALF + OUT_AT + HALF_D))
        )
        b_all, c_all, v_all = (proj[which, :, feats] for which in range(3))
        mixed = b_all * v_all
        own = mixed[0:TOK]
        one, second = conv_terms(own, mixed[TOK:ALL] * follows)
        tap_one, tap_two = rows[3:4, feats], rows[4:5, feats]
        conv = rows[2:3, feats] * own + first_ok * tap_one * one + second_ok * tap_two * second
        d_c = gated * conv
        d_conv = gated * c_all[0:TOK]
        small[2:3, feats] = jnp.sum(d_conv * own, axis=0, keepdims=True)
        small[3:4, feats] = jnp.sum(d_conv * first_ok * one, axis=0, keepdims=True)
        small[4:5, feats] = jnp.sum(d_conv * second_ok * second, axis=0, keepdims=True)
        term_one = first_ok * tap_one * d_conv
        term_two = second_ok * tap_two * d_conv
        lines = row_index(TOK, TILE)
        zero = jnp.zeros((TOK, TILE), FLOAT)
        d_mixed = (
            rows[2:3, feats] * d_conv
            + jnp.where(lines < TOK - 1, pltpu.roll(term_one, TOK - 1, 0), zero)
            + jnp.where(lines < TOK - 2, pltpu.roll(term_two, TOK - 2, 0), zero)
        )
        lines = row_index(16, TILE)
        zero = jnp.zeros((16, TILE), FLOAT)
        d_halo = follows * (
            jnp.where(lines < 2, term_two[0:16], zero)
            + jnp.where(lines == 1, pltpu.roll(term_one[0:16], 1, 0), zero)
        )
        half, place = lax.div(tile, 2), lax.rem(tile, 2) * TILE
        for which, (main, edge) in enumerate(
            (
                (d_mixed * v_all[0:TOK], d_halo * v_all[TOK:ALL]),
                (d_c, zero),
                (d_mixed * b_all[0:TOK], d_halo * b_all[TOK:ALL]),
            )
        ):
            cols = cut(which * HALF_D + place, TILE)
            grads[half, 0:TOK, cols] = main.astype(HALF)
            grads[half, TOK:ALL, cols] = edge.astype(HALF)


def projection_back(mix, grads, normed_grad):
    @pl.loop(0, D // TILE)
    def _(tile):
        total = dot_nt(grads[0], mat_rows(mix, tile, slice(0, OUT_AT)))
        total += dot_nt(grads[1], mat_rows(mix, tile, slice(MIX_HALF, MIX_HALF + OUT_AT)))
        normed_grad[:, cut(tile * TILE, TILE)] = total


def mixer_weight_grads(here, grads, branch, turned, grads_in, branch_in, total):
    def put(cols, value):
        total[:, :, :, :, :, cols] = value.astype(HALF).reshape(GRID + (16, TILE))

    @pl.loop(0, OUT_AT // TILE)
    def _(tile):
        cols = cut(tile * TILE, TILE)
        put(cols, dot(turned[0], grads[here.core, :, cols]) + dot(turned[1], grads_in[:, cols]))

    @pl.loop(0, HALF_D // TILE)
    def _(tile):
        cols = cut(tile * TILE, TILE)
        value = dot(turned[2, :, 0:TOK], branch[here.core, :, cols])
        value += dot(turned[3, :, 0:TOK], branch_in[:, cols])
        put(cut(OUT_AT + tile * TILE, TILE), value)


def backward_kernel(
    mix_in, proj, normed, gated, resid, rows, tokens, halo, flags, cotangent, two_sum, ffn_sum, ffn,
    mixed_out, grad_tokens, mix_owned, ffn_owned,
    mix, total, mix_mate, ffn_landed, ffn_total, ffn_rest, ffn_mate, work, ffn_work,
    branch, grads, d_normed, small, turned, normed_in, gated_in, branch_in, grads_in, small_in,
    edge_in, d_resid, *scratch,
):
    two_near, two_far = scratch[0:2], scratch[2:4]
    out_near, out_far = scratch[4:6], scratch[6:8]
    *landing, send, recv, local_sem = scratch[8:]
    mix_near, mix_far = landing_refs(MIX_REDUCE, landing[:MIX_LANDING])
    ffn_near, ffn_far = landing_refs(FFN_REDUCE, landing[MIX_LANDING:])
    here = Here()
    mail = Mail(send, recv)
    x, core = here.at["x"], here.core
    twin = here.twin()
    loads = [
        pltpu.make_async_copy(two_sum, work, local_sem.at[0]),
        pltpu.make_async_copy(mix_in, mix, local_sem.at[1]),
        pltpu.make_async_copy(ffn_sum, ffn_work, local_sem.at[2]),
    ]
    for load in loads:
        load.start()
    greet(
        near_list(here, ("x", "y", "z"))
        + [here.beside("x", 2), twin, here.along(1), here.along(-1)]
    )
    loads[0].wait()
    two_ring = RingReduce(here, mail, "x", row_pick(work), two_near, two_far)
    two_ring.start()
    early = [mail.post(normed, normed_in, twin), mail.post(gated, gated_in, twin)]
    ffn_twin = twin_send(here, mail, ffn, FFN_HALF, ffn_landed)
    turned[0, :, 0:ALL] = jnp.transpose(normed[...].astype(FLOAT)).astype(HALF)
    turned[2, :, 0:TOK] = jnp.transpose(gated[...].astype(FLOAT)).astype(HALF)
    two_ring.relay()
    ffn_twin.wait_recv()
    twin_sum(here, ffn, FFN_HALF, ffn_landed, ffn_total)
    ffn_rings = reduce_rings(here, mail, ffn_total, FFN_PARTS, FFN_REDUCE, ffn_near, ffn_far, 0)
    start_all(ffn_rings)
    two_ring.finish()

    value = resid[...]
    scale = norm_scale(value)
    unit = value * scale
    d_two = work[x].astype(FLOAT)
    small[...] = jnp.zeros_like(small)
    small[1:2] = jnp.sum(d_two * unit, axis=0, keepdims=True)
    d_value = flags[:, 2:3] * cotangent[...].astype(FLOAT) + norm_back(unit, scale, rows[1:2], d_two)
    d_resid[...] = d_value
    branch[0] = d_value[:, 0:HALF_D].astype(HALF)
    branch[1] = d_value[:, HALF_D:D].astype(HALF)
    late = [mail.post(branch.at[1 - core], branch_in, twin)]
    loads[1].wait()
    mixer_backward(here, flags, mix, proj, rows, branch, grads, small)
    late.append(mail.post(grads.at[1 - core], grads_in, twin))
    relay_all(ffn_rings)
    projection_back(mix, grads, d_normed)
    x_own, x_edge = tokens[...].astype(FLOAT), halo[...].astype(FLOAT)
    scale = norm_scale(x_own)
    unit = x_own * scale
    small[0:1] = jnp.sum(d_normed[0:TOK] * unit, axis=0, keepdims=True) + jnp.sum(
        d_normed[TOK:ALL] * x_edge * norm_scale(x_edge), axis=0, keepdims=True
    )
    late.append(mail.post(small, small_in, twin))
    edge = mail.post(d_normed.at[pl.ds(TOK, 8)], edge_in, here.along(-1))
    wait_all(early)
    turned[1, :, 0:ALL] = jnp.transpose(normed_in[...].astype(FLOAT)).astype(HALF)
    turned[3, :, 0:TOK] = jnp.transpose(gated_in[...].astype(FLOAT)).astype(HALF)
    wait_all(late)
    mixer_weight_grads(here, grads, branch, turned, grads_in, branch_in, total)
    small_sum = small[...] + small_in[...]
    total[:, :, :, :, :, SMALL_AT:MIX_HALF] = (
        jnp.transpose(small_sum).astype(HALF).reshape(GRID + (16, LANE))
    )
    mix_rings = reduce_rings(here, mail, total, MIX_PARTS, MIX_REDUCE, mix_near, mix_far, 0)
    start_all(mix_rings)
    loads[2].wait()
    out_ring = RingReduce(here, mail, "x", row_pick(ffn_work), out_near, out_far)
    out_ring.start()
    finish_all(ffn_rings)
    ffn_rings = reduce_rings(here, mail, ffn_total, FFN_PARTS, FFN_REDUCE, ffn_near, ffn_far, 1)
    start_all(ffn_rings)
    relay_all(mix_rings)
    out_ring.relay()
    relay_all(ffn_rings)
    edge.wait_recv()
    d_first = (
        d_normed[0:TOK] + flags[:, 3:4] * edge_in[0:1] + flags[:, 4:5] * edge_in[1:2]
    )
    grad_tokens[...] = (d_resid[...] + norm_back(unit, scale, rows[0:1], d_first)).astype(HALF)
    finish_all(mix_rings)
    mix_rings = reduce_rings(here, mail, total, MIX_PARTS, MIX_REDUCE, mix_near, mix_far, 1)
    start_all(mix_rings)
    finish_all(ffn_rings)
    copies = []
    for step in (1, 3, 2):
        there = here.ring("x", step)
        copies.append(
            mail.post(
                blocks(ffn_total, {**here.at, "x": there}, slice(None)),
                ffn_rest.at[x],
                here.beside("x", step),
            )
        )
    ffn_rest[x] = blocks(ffn_total, here.at, slice(None))[...]
    relay_all(mix_rings)
    out_ring.finish()
    mixed_out[...] = (flags[:, 2:3] * (resid[...] + ffn_work[x].astype(FLOAT))).astype(HALF)
    finish_all(mix_rings)
    mix_rings = reduce_rings(here, mail, total, MIX_PARTS, MIX_REDUCE, mix_near, mix_far, 2)
    start_all(mix_rings)
    wait_all(copies)
    ffn_swap = mail.post(ffn_rest, ffn_mate, twin)
    ffn_owned[:, :, cut(core * FFN_HALF, FFN_HALF)] = ffn_rest[...].astype(FLOAT)
    relay_all(mix_rings)
    ffn_swap.wait_recv()
    ffn_owned[:, :, cut((1 - core) * FFN_HALF, FFN_HALF)] = ffn_mate[...].astype(FLOAT)
    finish_all(mix_rings)
    own = blocks(total, here.at, slice(None))
    mix_swap = mail.post(own, mix_mate, twin)
    mix_owned[:, cut(core * MIX_HALF, MIX_HALF)] = own[...].astype(FLOAT)
    mix_swap.wait_recv()
    mix_owned[:, cut((1 - core) * MIX_HALF, MIX_HALF)] = mix_mate[...].astype(FLOAT)
    mail.close()


def vmem():
    return pl.BlockSpec(memory_space=pltpu.VMEM)


def anywhere():
    return pl.BlockSpec(memory_space=pl.ANY)


def sems(count):
    return pltpu.SemaphoreType.DMA((count,))


def params(number):
    return pltpu.CompilerParams(
        collective_id=number, has_side_effects=True, vmem_limit_bytes=VMEM_LIMIT
    )


def shape(dims, dtype):
    return jax.ShapeDtypeStruct(dims, dtype)


def forward(own, tail, back, tokens, flags):
    return pl.pallas_call(
        forward_kernel,
        out_shape=(
            shape(GRID + (16, MIX_COLS), HALF),
            shape(GRID + (16, FFN_COLS), HALF),
            shape((4, TOK, D), HALF),
            shape((4, TOK, D), HALF),
            shape((3, ALL, D), FLOAT),
            shape((ALL, D), HALF),
            shape((TOK, D), HALF),
            shape((TOK, D), FLOAT),
            shape((8, D), FLOAT),
            shape((16, D), HALF),
        ),
        in_specs=[vmem()] * 5,
        out_specs=(anywhere(),) * 4 + (vmem(),) * 6,
        scratch_shapes=[
            pltpu.VMEM((16, OWN_COLS), HALF),
            pltpu.VMEM((16, OWN_COLS), HALF),
            pltpu.VMEM(GRID + (16, MIX_COLS), HALF),
            pltpu.VMEM((TOK, D), HALF),
            sems(96),
            sems(96),
            sems(3),
        ],
        compiler_params=params(0),
        name="forward",
    )(own, tail, back, tokens, flags)


def backward(mix, proj, normed, gated, resid, rows, tokens, halo, flags, cotangent, two_sum, ffn_sum, ffn):
    landing = [
        pltpu.VMEM(dims, HALF)
        for part in landing_shapes(MIX_PARTS, MIX_REDUCE) + landing_shapes(FFN_PARTS, FFN_REDUCE)
        for dims in part
    ]
    stream_landing = [pltpu.VMEM((TOK, D), HALF)] * 2 + [pltpu.VMEM((TOK // 2, D), HALF)] * 2
    return pl.pallas_call(
        backward_kernel,
        out_shape=(
            shape((TOK, D), HALF),
            shape((TOK, D), HALF),
            shape((16, MIX_COLS), FLOAT),
            shape((4, 16, FFN_COLS), FLOAT),
        ),
        in_specs=[anywhere()] + [vmem()] * 9 + [anywhere()] * 2 + [vmem()],
        out_specs=(vmem(),) * 4,
        scratch_shapes=[
            pltpu.VMEM(GRID + (16, MIX_COLS), HALF),
            pltpu.VMEM(GRID + (16, MIX_HALF), HALF),
            pltpu.VMEM((16, MIX_HALF), HALF),
            pltpu.VMEM(GRID + (16, FFN_HALF), HALF),
            pltpu.VMEM(GRID + (16, FFN_HALF), HALF),
            pltpu.VMEM((4, 16, FFN_HALF), HALF),
            pltpu.VMEM((4, 16, FFN_HALF), HALF),
            pltpu.VMEM((4, TOK, D), HALF),
            pltpu.VMEM((4, TOK, D), HALF),
            pltpu.VMEM((2, TOK, HALF_D), HALF),
            pltpu.VMEM((2, ALL, OUT_AT), HALF),
            pltpu.VMEM((ALL, D), FLOAT),
            pltpu.VMEM((LANE, D), FLOAT),
            pltpu.VMEM((4, D, ALL), HALF),
            pltpu.VMEM((ALL, D), HALF),
            pltpu.VMEM((TOK, D), HALF),
            pltpu.VMEM((TOK, HALF_D), HALF),
            pltpu.VMEM((ALL, OUT_AT), HALF),
            pltpu.VMEM((LANE, D), FLOAT),
            pltpu.VMEM((8, D), FLOAT),
            pltpu.VMEM((TOK, D), FLOAT),
        ]
        + stream_landing * 2
        + landing
        + [sems(96), sems(96), sems(3)],
        compiler_params=params(1),
        name="backward",
    )(mix, proj, normed, gated, resid, rows, tokens, halo, flags, cotangent, two_sum, ffn_sum, ffn)


def dot_tn(left, right):
    return jnp.einsum("ta,tb->ab", left, right, preferred_element_type=FLOAT)


def local(
    tokens,
    gain_mix,
    in_weight,
    conv_weight,
    out_weight,
    gain_ffn,
    gate_weight,
    up_weight,
    down_weight,
    live_counts,
    positions,
    cotangent,
):
    core = lax.rem(lax.axis_index("seq"), 2)
    count = live_counts[0, 0]
    small = jnp.stack([gain_mix, gain_ffn, conv_weight[0], conv_weight[1], conv_weight[2]], axis=1)
    small = jnp.pad(small, ((0, 0), (0, LANE - 5)))
    mix_rows = jnp.concatenate(
        [
            in_weight.reshape(8, 3, 2, HALF_D).transpose(0, 2, 1, 3).reshape(8, 2, OUT_AT),
            out_weight.reshape(8, 2, HALF_D),
            jnp.stack([small, small], axis=1),
        ],
        axis=2,
    )
    ffn_rows = [
        weight.reshape(8, 4, SLAB) for weight in (gate_weight, up_weight, jnp.transpose(down_weight))
    ]
    ffn_rows = jnp.concatenate(ffn_rows + [jnp.zeros((8, 4, FFN_COLS - 3 * SLAB), HALF)], axis=2)
    ffn_rows = ffn_rows.reshape(8, 4, 2, FFN_HALF).transpose(0, 2, 1, 3).reshape(8, 2, 4 * FFN_HALF)
    own = jnp.concatenate([mix_rows, ffn_rows], axis=2).transpose(1, 0, 2)
    own = jnp.concatenate([own, own], axis=1)
    tail = jnp.pad(lax.dynamic_slice(tokens, (count - 2, 0), (2, D)), ((0, 14), (0, 0)))
    slots = jnp.arange(TOK, dtype=jnp.int32)
    flags = jnp.stack(
        [positions >= 1, positions >= 2, slots < count, slots == count - 2, slots == count - 1], axis=1
    )
    flags = jnp.pad(flags.astype(FLOAT), ((0, 0), (0, LANE - 5)))
    d_ffn = jnp.where(flags[:, 2:3] > 0, cotangent, jnp.zeros_like(cotangent))

    mix, ffn, backs, twos, proj, normed, gated, resid, rows, halo = forward(
        own, tail, d_ffn, tokens, flags
    )
    ffn = ffn.reshape(D, FFN_COLS)
    w_gate, w_up, w_down = ffn[:, :SLAB], ffn[:, SLAB : 2 * SLAB], ffn[:, 2 * SLAB : 3 * SLAB]
    twos = twos.reshape(4 * TOK, D)
    backs = backs.reshape(4 * TOK, D)
    gate = dot(twos, w_gate)
    upper = dot(twos, w_up)
    sig = jax.nn.sigmoid(gate)
    swish = gate * sig
    active = (swish * upper).astype(HALF)
    d_active = dot(backs, w_down)
    d_gate = (d_active * upper * (sig * (1.0 + gate * (1.0 - sig)))).astype(HALF)
    d_upper = (d_active * swish).astype(HALF)
    ffn_sum = dot_nt(active, w_down).astype(HALF)
    two_sum = (dot_nt(d_gate, w_gate) + dot_nt(d_upper, w_up)).astype(HALF)
    ffn_grads = jnp.concatenate(
        [
            dot_tn(twos, d_gate).astype(HALF),
            dot_tn(twos, d_upper).astype(HALF),
            dot_tn(backs, active).astype(HALF),
            jnp.zeros((D, FFN_COLS - 3 * SLAB), HALF),
        ],
        axis=1,
    )
    mixed_out, grad_tokens, owned_mix, owned_ffn = backward(
        mix, proj, normed, gated, resid, rows, tokens, halo, flags, cotangent,
        two_sum.reshape(4, TOK, D), ffn_sum.reshape(4, TOK, D), ffn_grads.reshape(GRID + (16, FFN_COLS)),
    )
    mine = lax.dynamic_slice(owned_mix, (8 * core, 0), (8, MIX_COLS)).reshape(8, 2, MIX_HALF)
    ffn_mine = lax.dynamic_slice(owned_ffn, (0, 8 * core, 0), (4, 8, FFN_COLS))
    ffn_mine = jnp.transpose(ffn_mine, (1, 0, 2))
    small_mine = jnp.transpose(mine[:, 0, SMALL_AT : SMALL_AT + 8])
    grad_in = mine[:, :, :OUT_AT].reshape(8, 2, 3, HALF_D).transpose(0, 2, 1, 3).reshape(8, 3 * D)
    return (
        mixed_out,
        grad_tokens,
        small_mine[0],
        grad_in,
        small_mine[2:5],
        mine[:, :, OUT_AT:SMALL_AT].reshape(8, D),
        small_mine[1],
        ffn_mine[:, :, :SLAB].reshape(8, 4 * SLAB),
        ffn_mine[:, :, SLAB : 2 * SLAB].reshape(8, 4 * SLAB),
        jnp.transpose(ffn_mine[:, :, 2 * SLAB : 3 * SLAB].reshape(8, 4 * SLAB)),
    )


def solution(mesh):
    rows = P(("fsdp", "seq"), None)
    flat = P(("fsdp", "seq"))
    cols = P(None, ("fsdp", "seq"))
    return jax.shard_map(
        local,
        mesh=mesh,
        in_specs=(rows, flat, rows, cols, rows, flat, rows, rows, cols, P("fsdp", "seq"), flat, rows),
        out_specs=(rows, rows, flat, rows, cols, rows, flat, rows, rows, cols),
        check_vma=False,
    )
```

time: 242 us -> 193 us (0.80)
  matrix products: 41.4 us -> 20.3 us
  other arithmetic: 21.4 us -> 7.33 us
  Pallas kernels: 161 us -> 151 us
    pallas_call x4 -> x2, Pallas kernels: 161 us -> 151 us  [the longest x1 78.4 us: backward(): pl.pallas_call(backward_kernel, out_shape=(shape((TOK, D), HALF), shape((...]
    dot_general x5 -> x3, matrix products: 15.3 us -> 6.72 us  [dot_nt(): lax.dot_general(left, right, (((1,), (1,)), ((), ())), preferred_element_...]
    dot_general x5 -> x3, matrix products: 17 us -> 8.64 us  [dot(): return jnp.dot(left, right, preferred_element_type=FLOAT)]
    convert_element_type x9 -> x1, other arithmetic: 6.53 us -> 0.01 us  [local(): flags = jnp.pad(flags.astype(FLOAT), ((0, 0), (0, LANE - 5)))]
    slice x9 -> x2, local copies, waits for them, and re-layouts: 6.18 us -> 0.62 us  [the longest x1 0.62 us: local(): mine[:, :, OUT_AT:SMALL_AT].reshape(8, D)]
    concatenate x2 -> x0, other arithmetic: 4.67 us -> none  [the longest x1 3.85 us: local(): jnp.concatenate([grad_in, grad_out, jnp.pad(small_grads, ((0, 0), (0, MIX...]
    dot_general x5 -> x3, matrix products: 9.07 us -> 4.97 us  [dot_tn(): return jnp.einsum('ta,tb->ab', left, right, preferred_element_type=FLOAT)]
    reduce_sum x3 -> x0, other arithmetic: 2.47 us -> none  [the longest x1 1.29 us: local(): grad_gain_two = jnp.sum(d_two * unit_two, axis=0)]
where the time goes in v2:
time: 193 us
  Pallas kernels  151 us (78%)
  matrix products  20.3 us (11%)
  local copies, waits for them, and re-layouts  13.2 us (7%)
  other arithmetic  7.33 us (4%)
    pallas_call x1, Pallas kernels, backward(): pl.pallas_call(backward_kernel, out_shape=(shape((TOK, D), HALF), shape((...  78.4 us
    pallas_call x1, Pallas kernels, forward(): pl.pallas_call(forward_kernel, out_shape=(shape(GRID + (16, MIX_COLS), HA...  72.4 us
    dot_general x3, matrix products, dot(): return jnp.dot(left, right, preferred_element_type=FLOAT)  8.64 us
    dot_general x3, matrix products, dot_nt(): lax.dot_general(left, right, (((1,), (1,)), ((), ())), preferred_element_...  6.72 us
    dot_general x3, matrix products, dot_tn(): return jnp.einsum('ta,tb->ab', left, right, preferred_element_type=FLOAT)  4.97 us

profile of v2, /device:TPU:1, one launch (start us, length us, event | category | flops | bytes accessed | tf_op | source)
XLA Modules:
  0.0 193.1 jit_solution(7696283614559216500)
XLA Ops:
  0.7 1.0 maximum_maximum_fusion.1
  1.8 0.7 copy.44
  2.6 0.7 copy.45
  3.3 0.8 slice_bitcast_fusion.1
  4.5 0.8 copy.43
  5.3 0.7 maximum_bitcast_fusion
  6.0 0.9 pad_maximum_fusion.own
  7.6 0.8 constant_dynamic-slice_fusion.1
  8.4 0.6 pad.13.tail
  9.4 0.8 broadcast_select_fusion.back
  10.2 0.6 pad.14.flags
  10.9 72.4 %forward.1 = (bf16[2,4,4,2,16,4352]{5,4,3,2,1,0:T(8,128)(2,1)}, bf16[2,4,4,2,16,3584]{5,4,3,2,1,0:T(8,128)(2,1)}, bf16[4,128,1024]{2,1,0:T(8,128)(2,1)}, bf16[4,...) custom-call(bf16[2,16,9344]{2,1,0:T(8,128)(2,1)} %pad_maximum_fusion, ...), custom_call_target="tpu_custom_call" | custom-call | tf_op jit(solution)/shard_map/forward/pallas_call | solution.py:704
  83.3 3.6 %fusion.3 = f32[512,1152]{1,0:T(8,128)S(1)} fusion(bf16[512,1024]{1,0:T(8,128)(2,1)} %bitcast.98, bf16[1024,3584]{1,0:T(8,128)(2,1)} %bitcast.92), kind=kOutput, calls=%fused_computation.12 | convolution fusion | flops 1207959552 | bytes 5767168 | tf_op jit(solution)/shard_map/dot_general | solution.py:257
  87.4 2.8 %fusion.11 = f32[512,1152]{1,0:T(8,128)S(1)} fusion(bf16[512,1024]{1,0:T(8,128)(2,1)} %bitcast.102, bf16[1024,3584]{1,0:T(8,128)(2,1)S(1)} %bitcast.93), kind=kOutput, calls=%fused_computation.20 | convolution fusion | flops 1207959552 | bytes 5767168 | tf_op jit(solution)/shard_map/dot_general | solution.py:257
  90.2 2.2 %multiply_convert_fusion = (bf16[512,1152]{1,0:T(8,128)(2,1)S(1)}, bf16[512,1152]{1,0:T(8,128)(2,1)S(1)}, bf16[512,1152]{1,0:T(8,128)(2,1)S(1)}) fusion(f32[512,1152]{1,0:T(8,128)S(1)} %fusion.3, f32[512,1152]{1,0:T(8,128)S(1)} %fusion.11, bf16[512,1024]{1,0:T(8,128)(2,1)S(1)} %bitcast.99, bf16[1024,3584]{1,0:T(8,128)(2,1)S(1)} %bitcast.94), kind=kOutput, calls=%fused_computation.4 | convolution fusion | flops 1216806912 | bytes 11665408 | tf_op jit(solution)/shard_map/dot_general | solution.py:257
  92.4 1.6 fusion.1
  93.9 2.6 %add_convert_fusion = bf16[512,1024]{1,0:T(8,128)(2,1)} fusion(f32[512,1024]{1,0:T(8,128)S(1)} %fusion.1, bf16[512,1152]{1,0:T(8,128)(2,1)S(1)} %get-tuple-element.72, bf16[1024,3584]{1,0:T(8,128)(2,1)S(1)} %bitcast.96), kind=kOutput, calls=%fused_computation.9 | convolution fusion | flops 1209008128 | bytes 6684672 | tf_op jit(solution)/shard_map/dot_general | solution.py:261
  96.5 2.6 %fusion.13 = bf16[512,1024]{1,0:T(8,128)(2,1)} fusion(bf16[512,1152]{1,0:T(8,128)(2,1)S(1)} %get-tuple-element.70, bf16[1024,3584]{1,0:T(8,128)(2,1)S(1)} %bitcast.97), kind=kOutput, calls=%fused_computation.22 | convolution fusion | flops 1208483840 | bytes 4587520 | tf_op jit(solution)/shard_map/dot_general | solution.py:261
  99.1 1.6 convolution_convert_fusion
  100.7 1.6 convolution_convert_fusion.1
  102.3 1.8 convolution_convert_fusion.2
  104.1 3.6 %maximum_maximum_fusion = bf16[1024,3584]{1,0:T(8,128)(2,1)} fusion(bf16[1024,1152]{1,0:T(8,128)(2,1)S(1)} %convolution_convert_fusion, bf16[1024,1152]{1,0:T(8,128)(2,1)S(1)} %convolution_convert_fusion.1, bf16[1024,1152]{1,0:T(8,128)(2,1)S(1)} %convolution_convert_fusion.2, bf16[3584]{0:T(1024)(128)(2,1)S(1)} %pad.29.clone), kind=kLoop, calls=%fused_computation | loop fusion | flops 29360128 | bytes 14425088 | tf_op jit(solution)/shard_map/concatenate | solution.py:844
  107.7 78.4 %backward.1 = (bf16[128,1024]{1,0:T(8,128)(2,1)}, bf16[128,1024]{1,0:T(8,128)(2,1)}, f32[16,4352]{1,0:T(8,128)}, f32[4,16,3584]{2,1,0:T(8,128)}) custom-call(bf16[2,4,4,2,16,4352]{5,4,3,2,1,0:T(8,128)(2,1)} %get-tuple-element.24.mix_in, f32[3,144,1024]{2,1,0:T(8,128)} %get-tuple-element.25.proj, bf16[144,1024]{1,0:T(8,128)(2,1)} %get-tuple-element.26.normed, ...), custom_call_target="tpu_custom_call" | custom-call | tf_op jit(solution)/shard_map/backward/pallas_call | solution.py:741
  186.1 1.0 constant_dynamic-slice_fusion
  187.1 0.7 slice_reduce_fusion
  187.8 0.6 copy.51
  188.6 0.7 copy.52
  189.2 0.6 slice.71
  189.8 1.0 dynamic-slice_bitcast_fusion
  190.9 0.8 fusion.19
  191.7 0.7 copy.56
  192.4 0.7 copy.57
  (33 shorter events, 1.4 us)
Async XLA Ops:
  0.6 8.8 %copy-start = (bf16[128,1024]{1,0:T(8,128)(2,1)S(1)}, bf16[128,1024]{1,0:T(8,128)(2,1)}, u32[]{:S(2)}) copy-start(bf16[128,1024]{1,0:T(8,128)(2,1)} %cotangent.1) | copy-start | bytes 786436
  0.7 8.4 %copy-start.6 = (s32[128]{0:T(128)S(1)}, s32[128]{0:T(128)}, u32[]{:S(2)}) copy-start(s32[128]{0:T(128)} %param.22) | copy-start | bytes 1540
  83.2 4.1 %copy-start.3 = (bf16[2,4,4,2,16,3584]{5,4,3,2,1,0:T(8,128)(2,1)S(1)}, bf16[2,4,4,2,16,3584]{5,4,3,2,1,0:T(8,128)(2,1)}, u32[]{:S(2)}) copy-start(bf16[2,4,4,2,16,3584]{5,4,3,2,1,0:T(8,128)(2,1)} %get-tuple-element.32) | copy-start | bytes 22020100
  87.4 2.8 %copy-start.4 = (bf16[4,128,1024]{2,1,0:T(8,128)(2,1)S(1)}, bf16[4,128,1024]{2,1,0:T(8,128)(2,1)}, u32[]{:S(2)}) copy-start(bf16[4,128,1024]{2,1,0:T(8,128)(2,1)} %get-tuple-element.33) | copy-start | bytes 3145732
  96.5 2.6 %copy-start.5 = (bf16[4,128,1024]{2,1,0:T(8,128)(2,1)S(1)}, bf16[4,128,1024]{2,1,0:T(8,128)(2,1)}, u32[]{:S(2)}) copy-start(bf16[4,128,1024]{2,1,0:T(8,128)(2,1)} %get-tuple-element.31) | copy-start | bytes 3145732
  186.1 5.5 %copy-start.2 = (bf16[128,1024]{1,0:T(8,128)(2,1)S(1)}, bf16[128,1024]{1,0:T(8,128)(2,1)}, u32[]{:S(2)}) copy-start(bf16[128,1024]{1,0:T(8,128)(2,1)} %get-tuple-element.93) | copy-start | bytes 786436
  186.1 6.2 %copy-start.1 = (bf16[128,1024]{1,0:T(8,128)(2,1)S(1)}, bf16[128,1024]{1,0:T(8,128)(2,1)}, u32[]{:S(2)}) copy-start(bf16[128,1024]{1,0:T(8,128)(2,1)} %get-tuple-element.94) | copy-start | bytes 786436

commit v3 on v2

--- a/solution.py
+++ b/solution.py
@@ -23,7 +23,7 @@
 TILE = 256
 TOK = 128
 ALL = TOK + 16
-MIX_PARTS = ((0, 9), (9, 4), (13, 4))
+MIX_PARTS = ((0, 6), (6, 6), (12, 5))
 MIX_GATHER = (("y", "z", "x"), ("z", "x", "y"), ("x", "y", "z"))
 MIX_REDUCE = (("x", "z", "y"), ("y", "x", "z"), ("z", "y", "x"))
 FFN_PARTS = ((0, 7), (7, 7))
@@ -75,7 +75,7 @@
 
 class Mail:
     def __init__(self, send, recv):
-        self.send, self.recv, self.posted = send, recv, []
+        self.send, self.recv, self.posted, self.settled = send, recv, [], 0
 
     def post(self, src, dst, device):
         place = len(self.posted)
@@ -91,9 +91,10 @@
         self.posted.append(copy)
         return copy
 
-    def close(self):
-        for copy in self.posted:
+    def settle(self, count):
+        for copy in self.posted[self.settled : count]:
             copy.wait_send()
+        self.settled = count
 
 
 def cut(start, count):
@@ -328,95 +329,13 @@
     two[...] = (value * norm_scale(value) * rows[1:2]).astype(HALF)
 
 
-def forward_kernel(
-    own, tail, back, tokens, flags,
-    mix_out, ffn, backs, twos, proj, normed, gated, resid, rows, halo,
-    mate, full, mix, two, send, recv, local_sem,
-):
-    here = Here()
-    mail = Mail(send, recv)
-    x = here.at["x"]
-    keep_back = pltpu.make_async_copy(back, backs.at[x], local_sem.at[0])
-    keep_back.start()
-    greet(
-        near_list(here, ("x", "y", "z"))
-        + [here.beside("x", 2), here.twin(), here.along(1), here.along(-1)]
-    )
-    rows_in = mail.post(own.at[1 - here.core], mate, here.twin())
-    halo_in = mail.post(tail, halo, here.along(1))
-    rows_in.wait_recv()
-    mine = lax.broadcasted_iota(jnp.int32, (16, OWN_COLS), 0) // 8 == here.core
-    full[...] = jnp.where(mine, own[here.core].astype(FLOAT), mate[...].astype(FLOAT)).astype(HALF)
-
-    mix_base, ffn_base = here.core * MIX_HALF, here.core * FFN_HALF
-    ffn_own = blocks(ffn, here.at, cut(ffn_base, FFN_HALF))
-
-    def slab(place):
-        return full.at[:, cut(MIX_HALF + place * FFN_HALF, FFN_HALF)]
-
-    rings = gather_rings(here, mail, mix, mix_base, MIX_PARTS, MIX_GATHER, 0)
-    for ring, (first, chunks) in zip(rings, MIX_PARTS):
-        ring.start(full.at[:, first * LANE : (first + chunks) * LANE])
-    slabs = [
-        mail.post(slab(here.ring("x", step)), ffn_own, here.beside("x", step)) for step in (1, 3, 2)
-    ]
-    keep_mix = pltpu.make_async_copy(
-        full.at[:, 0:MIX_HALF], blocks(mix, here.at, cut(mix_base, MIX_HALF)), local_sem.at[1]
-    )
-    keep_slab = pltpu.make_async_copy(slab(x), ffn_own, local_sem.at[2])
-    keep_mix.start()
-    keep_slab.start()
-    relay_all(rings)
-    finish_all(rings)
-    keep_mix.wait()
-    keep_slab.wait()
-    wait_all(slabs)
-    mix_rings = gather_rings(here, mail, mix, mix_base, MIX_PARTS, MIX_GATHER, 1)
-    ffn_rings = gather_rings(here, mail, ffn, ffn_base, FFN_PARTS, FFN_GATHER, 0)
-    run_rings(mix_rings + ffn_rings)
-    mix_rings = gather_rings(here, mail, mix, mix_base, MIX_PARTS, MIX_GATHER, 2)
-    ffn_rings = gather_rings(here, mail, ffn, ffn_base, FFN_PARTS, FFN_GATHER, 1)
-    start_all(mix_rings)
-    swaps = swap_pieces(here, mail, mix_rings, (0,))
-    relay_all(mix_rings)
-    swaps += swap_pieces(here, mail, mix_rings, (1, -1))
-    start_all(ffn_rings)
-    stream = RingGather(here, mail, "x", row_pick(backs))
-    stream.start(back)
-    finish_all(mix_rings)
-    swaps += swap_pieces(here, mail, mix_rings, (2,))
-    ffn_swaps = swap_pieces(here, mail, ffn_rings, (0,))
-    wait_all(swaps)
-    halo_in.wait_recv()
-    keep_all = pltpu.make_async_copy(mix, mix_out, local_sem.at[1])
-    keep_all.start()
-    mixer_forward(here, tokens, halo, flags, mix, proj, normed, gated, resid, rows, two)
-    two_ring = RingGather(here, mail, "x", row_pick(twos))
-    two_ring.start(two)
-    keep_two = pltpu.make_async_copy(two, twos.at[x], local_sem.at[2])
-    keep_two.start()
-    relay_all(ffn_rings)
-    stream.relay()
-    ffn_swaps += swap_pieces(here, mail, ffn_rings, (1, -1))
-    two_ring.relay()
-    finish_all(ffn_rings)
-    ffn_swaps += swap_pieces(here, mail, ffn_rings, (2,))
-    stream.finish()
-    two_ring.finish()
-    wait_all(ffn_swaps)
-    keep_back.wait()
-    keep_two.wait()
-    keep_all.wait()
-    mail.close()
-
-
-def reduce_rings(here, mail, ref, parts, orders, near, far, stage):
+def reduce_rings(here, mail, ref, base, parts, orders, near, far, stage):
     rings = []
     for number, ((first, chunks), order) in enumerate(zip(parts, orders)):
         fixed = {"x": None, "y": None, "z": None}
         for axis in order[:stage]:
             fixed[axis] = here.at[axis]
-        pick = column_pick(ref, fixed, order[stage], first * LANE, chunks)
+        pick = column_pick(ref, fixed, order[stage], base + first * LANE, chunks)
         rings.append(
             RingReduce(here, mail, order[stage], pick, near[number][stage], far[number][stage])
         )
@@ -458,23 +377,48 @@
     return near, far
 
 
-def twin_send(here, mail, grads, half, landed):
-    other = (1 - here.core) * half
-    return mail.post(grads.at[:, :, :, :, :, cut(other, half)], landed, here.twin())
-
-
-def twin_sum(here, grads, half, landed, total):
-    base = here.core * half
-
+def twin_sum(ref, cols, landed):
     @pl.loop(0, 32)
     def _(index):
         high, y = lax.div(index, 16), lax.rem(lax.div(index, 4), 4)
         x = lax.rem(index, 4)
         for low in range(2):
-            total[high, y, x, low] = (
-                grads[high, y, x, low, :, cut(base, half)].astype(FLOAT)
-                + landed[high, y, x, low].astype(FLOAT)
-            ).astype(HALF)
+            add_into(ref.at[high, y, x, low, :, cols], landed.at[high, y, x, low])
+
+
+def ffn_hidden(ffn, twos, backs, acts, start, width):
+    value = twos[...].reshape(4 * TOK, D)
+    gate = dot(value, mat(ffn, cut(start, width)))
+    upper = dot(value, mat(ffn, cut(SLAB + start, width)))
+    d_active = dot(backs[...].reshape(4 * TOK, D), mat(ffn, cut(2 * SLAB + start, width)))
+    sig = jax.nn.sigmoid(gate)
+    swish = gate * sig
+    acts[:, cut(start, width)] = (d_active * upper * (sig * (1.0 + gate * (1.0 - sig)))).astype(HALF)
+    acts[:, cut(SLAB + start, width)] = (d_active * swish).astype(HALF)
+    acts[:, cut(2 * SLAB + start, width)] = (swish * upper).astype(HALF)
+
+
+def ffn_tokens(ffn, acts, target, kinds):
+    @pl.loop(0, D // TILE)
+    def _(tile):
+        total = 0.0
+        for kind in kinds:
+            cols = slice(kind * SLAB, (kind + 1) * SLAB)
+            total += dot_nt(acts[:, cols], mat_rows(ffn, tile, cols))
+        target[:, :, cut(tile * TILE, TILE)] = total.astype(HALF).reshape(4, TOK, TILE)
+
+
+def ffn_weight_grads(ffn, acts, turned, half):
+    @pl.loop(0, FFN_HALF // TILE)
+    def _(tile):
+        cols = cut(half * FFN_HALF + tile * TILE, TILE)
+        side = half * jnp.minimum(lax.div(tile, 2), 1)
+        value = dot(turned[side], acts[:, cols])
+        ffn[:, :, :, :, :, cols] = value.astype(HALF).reshape(GRID + (16, TILE))
+
+
+def turn(target, value):
+    target[...] = jnp.transpose(value.astype(FLOAT)).astype(HALF)
 
 
 def mixer_backward(here, flags, mix, proj, rows, branch, grads, small):
@@ -552,10 +496,11 @@
         put(cut(OUT_AT + tile * TILE, TILE), value)
 
 
-def backward_kernel(
-    mix_in, proj, normed, gated, resid, rows, tokens, halo, flags, cotangent, two_sum, ffn_sum, ffn,
+def block_kernel(
+    own, tail, tokens, flags, cotangent,
     mixed_out, grad_tokens, mix_owned, ffn_owned,
-    mix, total, mix_mate, ffn_landed, ffn_total, ffn_rest, ffn_mate, work, ffn_work,
+    mate, full, halo, mix, ffn, twos, backs, proj, normed, gated, resid, rows, acts, turned_ffn,
+    total, mix_mate, ffn_landed, ffn_rest, ffn_mate, work, ffn_work,
     branch, grads, d_normed, small, turned, normed_in, gated_in, branch_in, grads_in, small_in,
     edge_in, d_resid, *scratch,
 ):
@@ -568,31 +513,100 @@
     mail = Mail(send, recv)
     x, core = here.at["x"], here.core
     twin = here.twin()
-    loads = [
-        pltpu.make_async_copy(two_sum, work, local_sem.at[0]),
-        pltpu.make_async_copy(mix_in, mix, local_sem.at[1]),
-        pltpu.make_async_copy(ffn_sum, ffn_work, local_sem.at[2]),
-    ]
-    for load in loads:
-        load.start()
     greet(
         near_list(here, ("x", "y", "z"))
         + [here.beside("x", 2), twin, here.along(1), here.along(-1)]
     )
-    loads[0].wait()
+    rows_in = mail.post(own.at[1 - core], mate, twin)
+    halo_in = mail.post(tail, halo, here.along(1))
+    backs[x] = (flags[:, 2:3] * cotangent[...].astype(FLOAT)).astype(HALF)
+    acts[:, 3 * SLAB : FFN_COLS] = jnp.zeros((4 * TOK, FFN_COLS - 3 * SLAB), HALF)
+    rows_in.wait_recv()
+    mine = lax.broadcasted_iota(jnp.int32, (16, OWN_COLS), 0) // 8 == core
+    full[...] = jnp.where(mine, own[core].astype(FLOAT), mate[...].astype(FLOAT)).astype(HALF)
+
+    mix_base, ffn_base = core * MIX_HALF, core * FFN_HALF
+    ffn_own = blocks(ffn, here.at, cut(ffn_base, FFN_HALF))
+
+    def slab(place):
+        return full.at[:, cut(MIX_HALF + place * FFN_HALF, FFN_HALF)]
+
+    rings = gather_rings(here, mail, mix, mix_base, MIX_PARTS, MIX_GATHER, 0)
+    for ring, (first, chunks) in zip(rings, MIX_PARTS):
+        ring.start(full.at[:, first * LANE : (first + chunks) * LANE])
+    slabs = [
+        mail.post(slab(here.ring("x", step)), ffn_own, here.beside("x", step)) for step in (1, 3, 2)
+    ]
+    keep_mix = pltpu.make_async_copy(
+        full.at[:, 0:MIX_HALF], blocks(mix, here.at, cut(mix_base, MIX_HALF)), local_sem.at[0]
+    )
+    keep_slab = pltpu.make_async_copy(slab(x), ffn_own, local_sem.at[1])
+    keep_mix.start()
+    keep_slab.start()
+    relay_all(rings)
+    finish_all(rings)
+    keep_mix.wait()
+    mix_rings = gather_rings(here, mail, mix, mix_base, MIX_PARTS, MIX_GATHER, 1)
+    start_all(mix_rings)
+    keep_slab.wait()
+    wait_all(slabs)
+    ffn_rings = gather_rings(here, mail, ffn, ffn_base, FFN_PARTS, FFN_GATHER, 0)
+    start_all(ffn_rings)
+    relay_all(mix_rings + ffn_rings)
+    finish_all(mix_rings)
+    mix_rings = gather_rings(here, mail, mix, mix_base, MIX_PARTS, MIX_GATHER, 2)
+    start_all(mix_rings)
+    swaps = swap_pieces(here, mail, mix_rings, (0,))
+    finish_all(ffn_rings)
+    ffn_rings = gather_rings(here, mail, ffn, ffn_base, FFN_PARTS, FFN_GATHER, 1)
+    relay_all(mix_rings)
+    swaps += swap_pieces(here, mail, mix_rings, (1, -1))
+    start_all(ffn_rings)
+    stream = RingGather(here, mail, "x", row_pick(backs))
+    stream.start()
+    finish_all(mix_rings)
+    swaps += swap_pieces(here, mail, mix_rings, (2,))
+    ffn_swaps = swap_pieces(here, mail, ffn_rings, (0,))
+    wait_all(swaps)
+    halo_in.wait_recv()
+    mixer_forward(here, tokens, halo, flags, mix, proj, normed, gated, resid, rows, twos.at[x])
+    two_ring = RingGather(here, mail, "x", row_pick(twos))
+    two_ring.start()
+    relay_all(ffn_rings)
+    stream.relay()
+    ffn_swaps += swap_pieces(here, mail, ffn_rings, (1, -1))
+    early = [mail.post(normed, normed_in, twin), mail.post(gated, gated_in, twin)]
+    two_ring.relay()
+    turn(turned.at[0, :, 0:ALL], normed[...])
+    turn(turned.at[2, :, 0:TOK], gated[...])
+    finish_all(ffn_rings)
+    ffn_swaps += swap_pieces(here, mail, ffn_rings, (2,))
+    stream.finish()
+    for block in range(4):
+        turn(turned_ffn.at[1, :, block * TOK : (block + 1) * TOK], backs[block])
+    wait_all(ffn_swaps)
+    two_ring.finish()
+    gathered = len(mail.posted)
+
+    @pl.loop(0, SLAB // TILE)
+    def _(tile):
+        ffn_hidden(ffn, twos, backs, acts, tile * TILE, TILE)
+
+    ffn_hidden(ffn, twos, backs, acts, SLAB // TILE * TILE, SLAB % TILE)
+    ffn_tokens(ffn, acts, work, (0, 1))
     two_ring = RingReduce(here, mail, "x", row_pick(work), two_near, two_far)
     two_ring.start()
-    early = [mail.post(normed, normed_in, twin), mail.post(gated, gated_in, twin)]
-    ffn_twin = twin_send(here, mail, ffn, FFN_HALF, ffn_landed)
-    turned[0, :, 0:ALL] = jnp.transpose(normed[...].astype(FLOAT)).astype(HALF)
-    turned[2, :, 0:TOK] = jnp.transpose(gated[...].astype(FLOAT)).astype(HALF)
+    ffn_tokens(ffn, acts, ffn_work, (2,))
+    for block in range(4):
+        turn(turned_ffn.at[0, :, block * TOK : (block + 1) * TOK], twos[block])
+    mail.settle(gathered)
+    ffn_weight_grads(ffn, acts, turned_ffn, 1 - core)
+    ffn_twin = mail.post(
+        ffn.at[:, :, :, :, :, cut((1 - core) * FFN_HALF, FFN_HALF)], ffn_landed, twin
+    )
     two_ring.relay()
-    ffn_twin.wait_recv()
-    twin_sum(here, ffn, FFN_HALF, ffn_landed, ffn_total)
-    ffn_rings = reduce_rings(here, mail, ffn_total, FFN_PARTS, FFN_REDUCE, ffn_near, ffn_far, 0)
-    start_all(ffn_rings)
+    ffn_weight_grads(ffn, acts, turned_ffn, core)
     two_ring.finish()
-
     value = resid[...]
     scale = norm_scale(value)
     unit = value * scale
@@ -604,10 +618,16 @@
     branch[0] = d_value[:, 0:HALF_D].astype(HALF)
     branch[1] = d_value[:, HALF_D:D].astype(HALF)
     late = [mail.post(branch.at[1 - core], branch_in, twin)]
-    loads[1].wait()
+    out_ring = RingReduce(here, mail, "x", row_pick(ffn_work), out_near, out_far)
+    out_ring.start()
+    ffn_twin.wait_recv()
+    twin_sum(ffn, cut(ffn_base, FFN_HALF), ffn_landed)
+    ffn_rings = reduce_rings(here, mail, ffn, ffn_base, FFN_PARTS, FFN_REDUCE, ffn_near, ffn_far, 0)
+    start_all(ffn_rings)
     mixer_backward(here, flags, mix, proj, rows, branch, grads, small)
     late.append(mail.post(grads.at[1 - core], grads_in, twin))
     relay_all(ffn_rings)
+    out_ring.relay()
     projection_back(mix, grads, d_normed)
     x_own, x_edge = tokens[...].astype(FLOAT), halo[...].astype(FLOAT)
     scale = norm_scale(x_own)
@@ -618,24 +638,20 @@
     late.append(mail.post(small, small_in, twin))
     edge = mail.post(d_normed.at[pl.ds(TOK, 8)], edge_in, here.along(-1))
     wait_all(early)
-    turned[1, :, 0:ALL] = jnp.transpose(normed_in[...].astype(FLOAT)).astype(HALF)
-    turned[3, :, 0:TOK] = jnp.transpose(gated_in[...].astype(FLOAT)).astype(HALF)
+    turn(turned.at[1, :, 0:ALL], normed_in[...])
+    turn(turned.at[3, :, 0:TOK], gated_in[...])
     wait_all(late)
     mixer_weight_grads(here, grads, branch, turned, grads_in, branch_in, total)
     small_sum = small[...] + small_in[...]
     total[:, :, :, :, :, SMALL_AT:MIX_HALF] = (
         jnp.transpose(small_sum).astype(HALF).reshape(GRID + (16, LANE))
     )
-    mix_rings = reduce_rings(here, mail, total, MIX_PARTS, MIX_REDUCE, mix_near, mix_far, 0)
+    mix_rings = reduce_rings(here, mail, total, 0, MIX_PARTS, MIX_REDUCE, mix_near, mix_far, 0)
     start_all(mix_rings)
-    loads[2].wait()
-    out_ring = RingReduce(here, mail, "x", row_pick(ffn_work), out_near, out_far)
-    out_ring.start()
     finish_all(ffn_rings)
-    ffn_rings = reduce_rings(here, mail, ffn_total, FFN_PARTS, FFN_REDUCE, ffn_near, ffn_far, 1)
+    ffn_rings = reduce_rings(here, mail, ffn, ffn_base, FFN_PARTS, FFN_REDUCE, ffn_near, ffn_far, 1)
     start_all(ffn_rings)
     relay_all(mix_rings)
-    out_ring.relay()
     relay_all(ffn_rings)
     edge.wait_recv()
     d_first = (
@@ -643,7 +659,7 @@
     )
     grad_tokens[...] = (d_resid[...] + norm_back(unit, scale, rows[0:1], d_first)).astype(HALF)
     finish_all(mix_rings)
-    mix_rings = reduce_rings(here, mail, total, MIX_PARTS, MIX_REDUCE, mix_near, mix_far, 1)
+    mix_rings = reduce_rings(here, mail, total, 0, MIX_PARTS, MIX_REDUCE, mix_near, mix_far, 1)
     start_all(mix_rings)
     finish_all(ffn_rings)
     copies = []
@@ -651,17 +667,17 @@
         there = here.ring("x", step)
         copies.append(
             mail.post(
-                blocks(ffn_total, {**here.at, "x": there}, slice(None)),
+                blocks(ffn, {**here.at, "x": there}, cut(ffn_base, FFN_HALF)),
                 ffn_rest.at[x],
                 here.beside("x", step),
             )
         )
-    ffn_rest[x] = blocks(ffn_total, here.at, slice(None))[...]
+    ffn_rest[x] = ffn_own[...]
     relay_all(mix_rings)
     out_ring.finish()
     mixed_out[...] = (flags[:, 2:3] * (resid[...] + ffn_work[x].astype(FLOAT))).astype(HALF)
     finish_all(mix_rings)
-    mix_rings = reduce_rings(here, mail, total, MIX_PARTS, MIX_REDUCE, mix_near, mix_far, 2)
+    mix_rings = reduce_rings(here, mail, total, 0, MIX_PARTS, MIX_REDUCE, mix_near, mix_far, 2)
     start_all(mix_rings)
     wait_all(copies)
     ffn_swap = mail.post(ffn_rest, ffn_mate, twin)
@@ -670,20 +686,16 @@
     ffn_swap.wait_recv()
     ffn_owned[:, :, cut((1 - core) * FFN_HALF, FFN_HALF)] = ffn_mate[...].astype(FLOAT)
     finish_all(mix_rings)
-    own = blocks(total, here.at, slice(None))
-    mix_swap = mail.post(own, mix_mate, twin)
-    mix_owned[:, cut(core * MIX_HALF, MIX_HALF)] = own[...].astype(FLOAT)
+    own_sum = blocks(total, here.at, slice(None))
+    mix_swap = mail.post(own_sum, mix_mate, twin)
+    mix_owned[:, cut(core * MIX_HALF, MIX_HALF)] = own_sum[...].astype(FLOAT)
     mix_swap.wait_recv()
     mix_owned[:, cut((1 - core) * MIX_HALF, MIX_HALF)] = mix_mate[...].astype(FLOAT)
-    mail.close()
+    mail.settle(len(mail.posted))
 
 
 def vmem():
     return pl.BlockSpec(memory_space=pltpu.VMEM)
-
-
-def anywhere():
-    return pl.BlockSpec(memory_space=pl.ANY)
 
 
 def sems(count):
@@ -700,38 +712,7 @@
     return jax.ShapeDtypeStruct(dims, dtype)
 
 
-def forward(own, tail, back, tokens, flags):
-    return pl.pallas_call(
-        forward_kernel,
-        out_shape=(
-            shape(GRID + (16, MIX_COLS), HALF),
-            shape(GRID + (16, FFN_COLS), HALF),
-            shape((4, TOK, D), HALF),
-            shape((4, TOK, D), HALF),
-            shape((3, ALL, D), FLOAT),
-            shape((ALL, D), HALF),
-            shape((TOK, D), HALF),
-            shape((TOK, D), FLOAT),
-            shape((8, D), FLOAT),
-            shape((16, D), HALF),
-        ),
-        in_specs=[vmem()] * 5,
-        out_specs=(anywhere(),) * 4 + (vmem(),) * 6,
-        scratch_shapes=[
-            pltpu.VMEM((16, OWN_COLS), HALF),
-            pltpu.VMEM((16, OWN_COLS), HALF),
-            pltpu.VMEM(GRID + (16, MIX_COLS), HALF),
-            pltpu.VMEM((TOK, D), HALF),
-            sems(96),
-            sems(96),
-            sems(3),
-        ],
-        compiler_params=params(0),
-        name="forward",
-    )(own, tail, back, tokens, flags)
-
-
-def backward(mix, proj, normed, gated, resid, rows, tokens, halo, flags, cotangent, two_sum, ffn_sum, ffn):
+def whole_block(own, tail, tokens, flags, cotangent):
     landing = [
         pltpu.VMEM(dims, HALF)
         for part in landing_shapes(MIX_PARTS, MIX_REDUCE) + landing_shapes(FFN_PARTS, FFN_REDUCE)
@@ -739,20 +720,32 @@
     ]
     stream_landing = [pltpu.VMEM((TOK, D), HALF)] * 2 + [pltpu.VMEM((TOK // 2, D), HALF)] * 2
     return pl.pallas_call(
-        backward_kernel,
+        block_kernel,
         out_shape=(
             shape((TOK, D), HALF),
             shape((TOK, D), HALF),
             shape((16, MIX_COLS), FLOAT),
             shape((4, 16, FFN_COLS), FLOAT),
         ),
-        in_specs=[anywhere()] + [vmem()] * 9 + [anywhere()] * 2 + [vmem()],
+        in_specs=[vmem()] * 5,
         out_specs=(vmem(),) * 4,
         scratch_shapes=[
+            pltpu.VMEM((16, OWN_COLS), HALF),
+            pltpu.VMEM((16, OWN_COLS), HALF),
+            pltpu.VMEM((16, D), HALF),
             pltpu.VMEM(GRID + (16, MIX_COLS), HALF),
+            pltpu.VMEM(GRID + (16, FFN_COLS), HALF),
+            pltpu.VMEM((4, TOK, D), HALF),
+            pltpu.VMEM((4, TOK, D), HALF),
+            pltpu.VMEM((3, ALL, D), FLOAT),
+            pltpu.VMEM((ALL, D), HALF),
+            pltpu.VMEM((TOK, D), HALF),
+            pltpu.VMEM((TOK, D), FLOAT),
+            pltpu.VMEM((8, D), FLOAT),
+            pltpu.VMEM((4 * TOK, FFN_COLS), HALF),
+            pltpu.VMEM((2, D, 4 * TOK), HALF),
             pltpu.VMEM(GRID + (16, MIX_HALF), HALF),
             pltpu.VMEM((16, MIX_HALF), HALF),
-            pltpu.VMEM(GRID + (16, FFN_HALF), HALF),
             pltpu.VMEM(GRID + (16, FFN_HALF), HALF),
             pltpu.VMEM((4, 16, FFN_HALF), HALF),
             pltpu.VMEM((4, 16, FFN_HALF), HALF),
@@ -773,14 +766,10 @@
         ]
         + stream_landing * 2
         + landing
-        + [sems(96), sems(96), sems(3)],
-        compiler_params=params(1),
-        name="backward",
-    )(mix, proj, normed, gated, resid, rows, tokens, halo, flags, cotangent, two_sum, ffn_sum, ffn)
-
-
-def dot_tn(left, right):
-    return jnp.einsum("ta,tb->ab", left, right, preferred_element_type=FLOAT)
+        + [sems(176), sems(176), sems(2)],
+        compiler_params=params(0),
+        name="whole_block",
+    )(own, tail, tokens, flags, cotangent)
 
 
 def local(
@@ -822,38 +811,7 @@
         [positions >= 1, positions >= 2, slots < count, slots == count - 2, slots == count - 1], axis=1
     )
     flags = jnp.pad(flags.astype(FLOAT), ((0, 0), (0, LANE - 5)))
-    d_ffn = jnp.where(flags[:, 2:3] > 0, cotangent, jnp.zeros_like(cotangent))
-
-    mix, ffn, backs, twos, proj, normed, gated, resid, rows, halo = forward(
-        own, tail, d_ffn, tokens, flags
-    )
-    ffn = ffn.reshape(D, FFN_COLS)
-    w_gate, w_up, w_down = ffn[:, :SLAB], ffn[:, SLAB : 2 * SLAB], ffn[:, 2 * SLAB : 3 * SLAB]
-    twos = twos.reshape(4 * TOK, D)
-    backs = backs.reshape(4 * TOK, D)
-    gate = dot(twos, w_gate)
-    upper = dot(twos, w_up)
-    sig = jax.nn.sigmoid(gate)
-    swish = gate * sig
-    active = (swish * upper).astype(HALF)
-    d_active = dot(backs, w_down)
-    d_gate = (d_active * upper * (sig * (1.0 + gate * (1.0 - sig)))).astype(HALF)
-    d_upper = (d_active * swish).astype(HALF)
-    ffn_sum = dot_nt(active, w_down).astype(HALF)
-    two_sum = (dot_nt(d_gate, w_gate) + dot_nt(d_upper, w_up)).astype(HALF)
-    ffn_grads = jnp.concatenate(
-        [
-            dot_tn(twos, d_gate).astype(HALF),
-            dot_tn(twos, d_upper).astype(HALF),
-            dot_tn(backs, active).astype(HALF),
-            jnp.zeros((D, FFN_COLS - 3 * SLAB), HALF),
-        ],
-        axis=1,
-    )
-    mixed_out, grad_tokens, owned_mix, owned_ffn = backward(
-        mix, proj, normed, gated, resid, rows, tokens, halo, flags, cotangent,
-        two_sum.reshape(4, TOK, D), ffn_sum.reshape(4, TOK, D), ffn_grads.reshape(GRID + (16, FFN_COLS)),
-    )
+    mixed_out, grad_tokens, owned_mix, owned_ffn = whole_block(own, tail, tokens, flags, cotangent)
     mine = lax.dynamic_slice(owned_mix, (8 * core, 0), (8, MIX_COLS)).reshape(8, 2, MIX_HALF)
     ffn_mine = lax.dynamic_slice(owned_ffn, (0, 8 * core, 0), (4, 8, FFN_COLS))
     ffn_mine = jnp.transpose(ffn_mine, (1, 0, 2))

time: 193 us -> 155 us (0.80)
  matrix products: 20.3 us -> 0 us
  Pallas kernels: 151 us -> 142 us
  other arithmetic: 7.33 us -> 2.57 us
  local copies, waits for them, and re-layouts: 13.2 us -> 9.17 us
    dot_general x9 -> x0, matrix products: 20.3 us -> none  [the longest x3 8.64 us: dot(): return jnp.dot(left, right, preferred_element_type=FLOAT)]
    pallas_call x2 -> x1, Pallas kernels: 151 us -> 142 us  [whole_block(): pl.pallas_call(block_kernel, out_shape=(shape((TOK, D), HALF), shape((TOK...]
    concatenate x1 -> x0, other arithmetic: 3.64 us -> none  [local(): jnp.concatenate([dot_tn(twos, d_gate).astype(HALF), dot_tn(twos, d_upper)...]
    another operation x7, local copies, waits for them, and re-layouts: 2.66 us -> 0.58 us  [local(): jnp.stack([gain_mix, gain_ffn, conv_weight[0], conv_weight[1], conv_weigh...]
where the time goes in v3:
time: 155 us
  Pallas kernels  142 us (92%)
  local copies, waits for them, and re-layouts  9.17 us (6%)
  other arithmetic  2.57 us (2%)
    pallas_call x1, Pallas kernels, whole_block(): pl.pallas_call(block_kernel, out_shape=(shape((TOK, D), HALF), shape((TOK...  142 us

profile of v3, /device:TPU:1, one launch (start us, length us, event | category | flops | bytes accessed | tf_op | source)
XLA Modules:
  0.0 155.3 jit_solution(11713386863238983575)
XLA Ops:
  0.6 0.0 copy-start.5
  0.7 0.0 copy-start.6
  0.7 0.0 copy-start.4
  0.7 1.0 maximum_maximum_fusion
  1.7 0.1 reshape.92
  1.8 0.0 copy-start.7
  1.8 0.0 copy-done.5
  1.8 0.1 copy.44
  1.9 0.1 copy.45
  2.0 0.1 copy.46
  2.1 0.1 copy.47
  2.2 0.1 copy.48
  2.3 0.1 stack.30
  2.4 0.0 copy-done.2
  2.5 0.9 pad_maximum_fusion.own
  4.0 0.8 constant_dynamic-slice_fusion.1
  4.8 0.6 pad.15.tail
  5.4 0.0 copy-done.7
  5.5 0.1 copy.50
  5.6 0.6 pad_convert_fusion.flags
  6.3 142.1 %whole_block.1 = (bf16[128,1024]{1,0:T(8,128)(2,1)}, bf16[128,1024]{1,0:T(8,128)(2,1)}, f32[16,4352]{1,0:T(8,128)}, f32[4,16,3584]{2,1,0:T(8,128)}) custom-call(bf16[2,16,9344]{2,1,0:T(8,128)(2,1)} %pad_maximum_fusion.own, bf16[16,1024]{1,0:T(8,128)(2,1)} %pad.15.tail, bf16[128,1024]{1,0:T(8,128)(2,1)} %tokens.1, f32[128,128]{1,0:T(8,128)} %pad_convert_fusion.flags, ...), custom_call_target="tpu_custom_call" | custom-call | tf_op jit(solution)/shard_map/whole_block/pallas_call | solution.py:722
  148.4 0.9 constant_dynamic-slice_fusion
  149.3 0.7 slice_reduce_fusion
  150.0 0.6 copy.51
  150.7 0.1 slice.42
  150.7 0.7 copy.52
  151.4 0.6 slice.50
  152.0 1.1 dynamic-slice_bitcast_fusion
  153.1 0.0 copy-start
  153.1 0.8 fusion
  153.9 0.7 copy.56
  154.6 0.7 copy.57
  (21 shorter events, 0.2 us)
Async XLA Ops:
  0.6 1.2 copy-start.5
  0.7 1.3 copy-start.6
  0.7 1.4 copy-start.4
  0.7 1.8 %copy-start.3 = (bf16[8,1024]{1,0:T(8,128)(2,1)S(1)}, bf16[8,1024]{1,0:T(8,128)(2,1)}, u32[]{:S(2)}) copy-start(bf16[8,1024]{1,0:T(8,128)(2,1)} %param.16) | copy-start | bytes 49156
  0.7 1.8 %copy-start.2 = (bf16[8,3072]{1,0:T(8,128)(2,1)S(1)}, bf16[8,3072]{1,0:T(8,128)(2,1)}, u32[]{:S(2)}) copy-start(bf16[8,3072]{1,0:T(8,128)(2,1)} %param.14) | copy-start | bytes 147460
  1.8 3.6 %copy-start.7 = (s32[128]{0:T(128)S(1)}, s32[128]{0:T(128)}, u32[]{:S(2)}) copy-start(s32[128]{0:T(128)} %param.22) | copy-start | bytes 1540
  152.0 1.9 %copy-start.1 = (bf16[128,1024]{1,0:T(8,128)(2,1)S(1)}, bf16[128,1024]{1,0:T(8,128)(2,1)}, u32[]{:S(2)}) copy-start(bf16[128,1024]{1,0:T(8,128)(2,1)} %get-tuple-element.70) | copy-start | bytes 786436
  153.1 1.5 copy-start

commit v4 on v3

--- a/solution.py
+++ b/solution.py
@@ -26,7 +26,7 @@
 MIX_PARTS = ((0, 6), (6, 6), (12, 5))
 MIX_GATHER = (("y", "z", "x"), ("z", "x", "y"), ("x", "y", "z"))
 MIX_REDUCE = (("x", "z", "y"), ("y", "x", "z"), ("z", "y", "x"))
-FFN_PARTS = ((0, 7), (7, 7))
+FFN_PARTS = ((0, 8), (8, 6))
 FFN_GATHER = (("y", "z"), ("z", "y"))
 FFN_REDUCE = (("y", "z"), ("z", "y"))
 GRID = (2, 4, 4, 2)
@@ -70,7 +70,7 @@
     barrier = pltpu.get_barrier_semaphore()
     for device in devices:
         pl.semaphore_signal(barrier, inc=1, device_id=device, device_id_type=MESH)
-    pl.semaphore_wait(barrier, len(devices))
+    return barrier, len(devices)
 
 
 class Mail:
@@ -163,7 +163,45 @@
         add_into(own, self.near[0], self.near[1])
 
 
+class DirectGather(RingGather):
+    def start(self, source=None):
+        here, axis = self.here, self.axis
+        own = self.pick(here.at[axis], None)
+        source = own if source is None else source
+        self.copies = [
+            self.mail.post(source, own, here.beside(axis, step)) for step in (1, -1, 2)
+        ]
+
+    def relay(self):
+        pass
+
+    def finish(self):
+        wait_all(self.copies)
+
+
+class DirectReduce(RingReduce):
+    def start(self):
+        here, axis = self.here, self.axis
+        self.landed = [self.near[0], self.near[1], self.far[0]]
+        self.copies = [
+            self.mail.post(
+                self.pick(here.ring(axis, step), None), landed, here.beside(axis, step)
+            )
+            for step, landed in zip((1, -1, 2), self.landed)
+        ]
+
+    def relay(self):
+        pass
+
+    def finish(self):
+        wait_all(self.copies)
+        add_into(self.pick(self.here.at[self.axis], None), *self.landed)
+
+
 def add_into(target, *terms):
+    if len(terms) == 1:
+        target[...] = target[...] + terms[0][...]
+        return
     total = target[...].astype(FLOAT)
     for term in terms:
         total = total + term[...].astype(FLOAT)
@@ -189,7 +227,7 @@
     return pick
 
 
-def gather_rings(here, mail, ref, base, parts, orders, stage):
+def gather_rings(here, mail, ref, base, parts, orders, stage, kind=RingGather):
     rings = []
     for (first, chunks), order in zip(parts, orders):
         fixed = dict(here.at)
@@ -197,7 +235,7 @@
             if axis not in order or axis in order[:stage]:
                 fixed[axis] = None
         pick = column_pick(ref, fixed, order[stage], base + first * LANE, chunks)
-        rings.append(RingGather(here, mail, order[stage], pick))
+        rings.append(kind(here, mail, order[stage], pick))
     return rings
 
 
@@ -336,9 +374,8 @@
         for axis in order[:stage]:
             fixed[axis] = here.at[axis]
         pick = column_pick(ref, fixed, order[stage], base + first * LANE, chunks)
-        rings.append(
-            RingReduce(here, mail, order[stage], pick, near[number][stage], far[number][stage])
-        )
+        kind = RingReduce if stage == 0 else DirectReduce
+        rings.append(kind(here, mail, order[stage], pick, near[number][stage], far[number][stage]))
     return rings
 
 
@@ -358,8 +395,11 @@
                 lead += (4,)
             if "z" not in gone:
                 lead += (2,)
-            for count, copies in ((chunks, 2), (split, 1), (chunks - split, 1)):
-                done += [lead + (16, count * LANE)] * copies
+            done += [lead + (16, chunks * LANE)] * 2
+            if stage == 0:
+                done += [lead + (16, split * LANE), lead + (16, (chunks - split) * LANE)]
+            else:
+                done += [lead + (16, chunks * LANE), (16, LANE)]
         shapes.append(done)
     return shapes
 
@@ -377,13 +417,13 @@
     return near, far
 
 
-def twin_sum(ref, cols, landed):
+def twin_sum(ref, cols, landed, landed_cols):
     @pl.loop(0, 32)
     def _(index):
         high, y = lax.div(index, 16), lax.rem(lax.div(index, 4), 4)
         x = lax.rem(index, 4)
         for low in range(2):
-            add_into(ref.at[high, y, x, low, :, cols], landed.at[high, y, x, low])
+            add_into(ref.at[high, y, x, low, :, cols], landed.at[high, y, x, low, :, landed_cols])
 
 
 def ffn_hidden(ffn, twos, backs, acts, start, width):
@@ -408,8 +448,10 @@
         target[:, :, cut(tile * TILE, TILE)] = total.astype(HALF).reshape(4, TOK, TILE)
 
 
-def ffn_weight_grads(ffn, acts, turned, half):
-    @pl.loop(0, FFN_HALF // TILE)
+def ffn_weight_grads(ffn, acts, turned, half, part):
+    first, chunks = part
+
+    @pl.loop(first * LANE // TILE, (first + chunks) * LANE // TILE)
     def _(tile):
         cols = cut(half * FFN_HALF + tile * TILE, TILE)
         side = half * jnp.minimum(lax.div(tile, 2), 1)
@@ -496,9 +538,35 @@
         put(cut(OUT_AT + tile * TILE, TILE), value)
 
 
+def twice(value):
+    value = value.astype(FLOAT)
+    return jnp.concatenate([value, value], axis=0).astype(HALF)
+
+
+def lay_out(own, in_rows, out_rows, gate_rows, up_rows, down_rows, small_rows):
+    for half in range(2):
+        for which in range(3):
+            start = which * D + half * HALF_D
+            own[half, :, which * HALF_D : (which + 1) * HALF_D] = twice(
+                in_rows[:, start : start + HALF_D]
+            )
+        own[half, :, OUT_AT:SMALL_AT] = twice(out_rows[:, half * HALF_D : (half + 1) * HALF_D])
+        own[half, :, SMALL_AT:MIX_HALF] = twice(small_rows[...])
+    early = FFN_HALF - SLAB
+    rest = SLAB - early
+    for place in range(4):
+        at, start = MIX_HALF + place * FFN_HALF, place * SLAB
+        own[0, :, at : at + SLAB] = twice(gate_rows[:, start : start + SLAB])
+        own[0, :, at + SLAB : at + FFN_HALF] = twice(up_rows[:, start : start + early])
+        own[1, :, at : at + rest] = twice(up_rows[:, start + early : start + SLAB])
+        own[1, :, at + rest : at + rest + SLAB] = twice(down_rows[:, start : start + SLAB])
+        own[1, :, at + rest + SLAB : at + FFN_HALF] = jnp.zeros((16, LANE), HALF)
+
+
 def block_kernel(
-    own, tail, tokens, flags, cotangent,
-    mixed_out, grad_tokens, mix_owned, ffn_owned,
+    in_rows, out_rows, gate_rows, up_rows, down_rows, small_rows, tail, tokens, flags, cotangent,
+    mixed_out, grad_tokens, grad_in, grad_out, grad_small, grad_gate, grad_up, grad_down,
+    own, mix_owned, ffn_owned,
     mate, full, halo, mix, ffn, twos, backs, proj, normed, gated, resid, rows, acts, turned_ffn,
     total, mix_mate, ffn_landed, ffn_rest, ffn_mate, work, ffn_work,
     branch, grads, d_normed, small, turned, normed_in, gated_in, branch_in, grads_in, small_in,
@@ -513,10 +581,13 @@
     mail = Mail(send, recv)
     x, core = here.at["x"], here.core
     twin = here.twin()
-    greet(
+    barrier, count = greet(
         near_list(here, ("x", "y", "z"))
-        + [here.beside("x", 2), twin, here.along(1), here.along(-1)]
-    )
+        + [here.beside(axis, 2) for axis in ("x", "y", "z")]
+        + [twin, here.along(1), here.along(-1)]
+    )
+    lay_out(own, in_rows, out_rows, gate_rows, up_rows, down_rows, small_rows)
+    pl.semaphore_wait(barrier, count)
     rows_in = mail.post(own.at[1 - core], mate, twin)
     halo_in = mail.post(tail, halo, here.along(1))
     backs[x] = (flags[:, 2:3] * cotangent[...].astype(FLOAT)).astype(HALF)
@@ -531,7 +602,7 @@
     def slab(place):
         return full.at[:, cut(MIX_HALF + place * FFN_HALF, FFN_HALF)]
 
-    rings = gather_rings(here, mail, mix, mix_base, MIX_PARTS, MIX_GATHER, 0)
+    rings = gather_rings(here, mail, mix, mix_base, MIX_PARTS, MIX_GATHER, 0, DirectGather)
     for ring, (first, chunks) in zip(rings, MIX_PARTS):
         ring.start(full.at[:, first * LANE : (first + chunks) * LANE])
     slabs = [
@@ -543,29 +614,29 @@
     keep_slab = pltpu.make_async_copy(slab(x), ffn_own, local_sem.at[1])
     keep_mix.start()
     keep_slab.start()
-    relay_all(rings)
     finish_all(rings)
     keep_mix.wait()
-    mix_rings = gather_rings(here, mail, mix, mix_base, MIX_PARTS, MIX_GATHER, 1)
+    mix_rings = gather_rings(here, mail, mix, mix_base, MIX_PARTS, MIX_GATHER, 1, DirectGather)
     start_all(mix_rings)
     keep_slab.wait()
     wait_all(slabs)
     ffn_rings = gather_rings(here, mail, ffn, ffn_base, FFN_PARTS, FFN_GATHER, 0)
     start_all(ffn_rings)
-    relay_all(mix_rings + ffn_rings)
+    stream = RingGather(here, mail, "x", row_pick(backs))
+    stream.start()
     finish_all(mix_rings)
     mix_rings = gather_rings(here, mail, mix, mix_base, MIX_PARTS, MIX_GATHER, 2)
     start_all(mix_rings)
     swaps = swap_pieces(here, mail, mix_rings, (0,))
+    relay_all(ffn_rings)
+    relay_all(mix_rings)
+    swaps += swap_pieces(here, mail, mix_rings, (1, -1))
     finish_all(ffn_rings)
     ffn_rings = gather_rings(here, mail, ffn, ffn_base, FFN_PARTS, FFN_GATHER, 1)
-    relay_all(mix_rings)
-    swaps += swap_pieces(here, mail, mix_rings, (1, -1))
-    start_all(ffn_rings)
-    stream = RingGather(here, mail, "x", row_pick(backs))
-    stream.start()
+    stream.relay()
     finish_all(mix_rings)
     swaps += swap_pieces(here, mail, mix_rings, (2,))
+    start_all(ffn_rings)
     ffn_swaps = swap_pieces(here, mail, ffn_rings, (0,))
     wait_all(swaps)
     halo_in.wait_recv()
@@ -573,7 +644,6 @@
     two_ring = RingGather(here, mail, "x", row_pick(twos))
     two_ring.start()
     relay_all(ffn_rings)
-    stream.relay()
     ffn_swaps += swap_pieces(here, mail, ffn_rings, (1, -1))
     early = [mail.post(normed, normed_in, twin), mail.post(gated, gated_in, twin)]
     two_ring.relay()
@@ -600,12 +670,35 @@
     for block in range(4):
         turn(turned_ffn.at[0, :, block * TOK : (block + 1) * TOK], twos[block])
     mail.settle(gathered)
-    ffn_weight_grads(ffn, acts, turned_ffn, 1 - core)
-    ffn_twin = mail.post(
-        ffn.at[:, :, :, :, :, cut((1 - core) * FFN_HALF, FFN_HALF)], ffn_landed, twin
-    )
-    two_ring.relay()
-    ffn_weight_grads(ffn, acts, turned_ffn, core)
+    pieces, base = [], (1 - core) * FFN_HALF
+    for number, (first, chunks) in enumerate(FFN_PARTS):
+        ffn_weight_grads(ffn, acts, turned_ffn, 1 - core, (first, chunks))
+        piece = slice(first * LANE, (first + chunks) * LANE)
+        pieces.append(
+            mail.post(
+                ffn.at[:, :, :, :, :, cut(base + first * LANE, chunks * LANE)],
+                ffn_landed.at[:, :, :, :, :, piece],
+                twin,
+            )
+        )
+        if number == 0:
+            two_ring.relay()
+    ffn_rings = reduce_rings(here, mail, ffn, ffn_base, FFN_PARTS, FFN_REDUCE, ffn_near, ffn_far, 0)
+    for part in FFN_PARTS:
+        ffn_weight_grads(ffn, acts, turned_ffn, core, part)
+
+    def join(number):
+        first, chunks = FFN_PARTS[number]
+        pieces[number].wait_recv()
+        twin_sum(
+            ffn,
+            cut(ffn_base + first * LANE, chunks * LANE),
+            ffn_landed,
+            slice(first * LANE, (first + chunks) * LANE),
+        )
+        ffn_rings[number].start()
+
+    join(0)
     two_ring.finish()
     value = resid[...]
     scale = norm_scale(value)
@@ -620,10 +713,7 @@
     late = [mail.post(branch.at[1 - core], branch_in, twin)]
     out_ring = RingReduce(here, mail, "x", row_pick(ffn_work), out_near, out_far)
     out_ring.start()
-    ffn_twin.wait_recv()
-    twin_sum(ffn, cut(ffn_base, FFN_HALF), ffn_landed)
-    ffn_rings = reduce_rings(here, mail, ffn, ffn_base, FFN_PARTS, FFN_REDUCE, ffn_near, ffn_far, 0)
-    start_all(ffn_rings)
+    join(1)
     mixer_backward(here, flags, mix, proj, rows, branch, grads, small)
     late.append(mail.post(grads.at[1 - core], grads_in, twin))
     relay_all(ffn_rings)
@@ -685,12 +775,26 @@
     relay_all(mix_rings)
     ffn_swap.wait_recv()
     ffn_owned[:, :, cut((1 - core) * FFN_HALF, FFN_HALF)] = ffn_mate[...].astype(FLOAT)
+    lines = pl.ds(pl.multiple_of(8 * core, 8), 8)
+    for place in range(4):
+        cols = slice(place * SLAB, (place + 1) * SLAB)
+        for kind, target in enumerate((grad_gate, grad_up, grad_down)):
+            target[:, cols] = ffn_owned[place, lines, kind * SLAB : (kind + 1) * SLAB]
     finish_all(mix_rings)
     own_sum = blocks(total, here.at, slice(None))
     mix_swap = mail.post(own_sum, mix_mate, twin)
     mix_owned[:, cut(core * MIX_HALF, MIX_HALF)] = own_sum[...].astype(FLOAT)
     mix_swap.wait_recv()
     mix_owned[:, cut((1 - core) * MIX_HALF, MIX_HALF)] = mix_mate[...].astype(FLOAT)
+    for half in range(2):
+        at = half * MIX_HALF
+        for which in range(3):
+            start = which * D + half * HALF_D
+            grad_in[:, start : start + HALF_D] = mix_owned[
+                lines, at + which * HALF_D : at + (which + 1) * HALF_D
+            ]
+        grad_out[:, half * HALF_D : (half + 1) * HALF_D] = mix_owned[lines, at + OUT_AT : at + SMALL_AT]
+    grad_small[...] = mix_owned[lines, SMALL_AT:MIX_HALF]
     mail.settle(len(mail.posted))
 
 
@@ -712,7 +816,7 @@
     return jax.ShapeDtypeStruct(dims, dtype)
 
 
-def whole_block(own, tail, tokens, flags, cotangent):
+def whole_block(*operands):
     landing = [
         pltpu.VMEM(dims, HALF)
         for part in landing_shapes(MIX_PARTS, MIX_REDUCE) + landing_shapes(FFN_PARTS, FFN_REDUCE)
@@ -724,12 +828,19 @@
         out_shape=(
             shape((TOK, D), HALF),
             shape((TOK, D), HALF),
-            shape((16, MIX_COLS), FLOAT),
-            shape((4, 16, FFN_COLS), FLOAT),
+            shape((8, 3 * D), FLOAT),
+            shape((8, D), FLOAT),
+            shape((8, LANE), FLOAT),
+            shape((8, 4 * SLAB), FLOAT),
+            shape((8, 4 * SLAB), FLOAT),
+            shape((8, 4 * SLAB), FLOAT),
         ),
-        in_specs=[vmem()] * 5,
-        out_specs=(vmem(),) * 4,
+        in_specs=[vmem()] * 10,
+        out_specs=(vmem(),) * 8,
         scratch_shapes=[
+            pltpu.VMEM((2, 16, OWN_COLS), HALF),
+            pltpu.VMEM((16, MIX_COLS), FLOAT),
+            pltpu.VMEM((4, 16, FFN_COLS), FLOAT),
             pltpu.VMEM((16, OWN_COLS), HALF),
             pltpu.VMEM((16, OWN_COLS), HALF),
             pltpu.VMEM((16, D), HALF),
@@ -769,7 +880,7 @@
         + [sems(176), sems(176), sems(2)],
         compiler_params=params(0),
         name="whole_block",
-    )(own, tail, tokens, flags, cotangent)
+    )(*operands)
 
 
 def local(
@@ -786,48 +897,31 @@
     positions,
     cotangent,
 ):
-    core = lax.rem(lax.axis_index("seq"), 2)
     count = live_counts[0, 0]
     small = jnp.stack([gain_mix, gain_ffn, conv_weight[0], conv_weight[1], conv_weight[2]], axis=1)
     small = jnp.pad(small, ((0, 0), (0, LANE - 5)))
-    mix_rows = jnp.concatenate(
-        [
-            in_weight.reshape(8, 3, 2, HALF_D).transpose(0, 2, 1, 3).reshape(8, 2, OUT_AT),
-            out_weight.reshape(8, 2, HALF_D),
-            jnp.stack([small, small], axis=1),
-        ],
-        axis=2,
-    )
-    ffn_rows = [
-        weight.reshape(8, 4, SLAB) for weight in (gate_weight, up_weight, jnp.transpose(down_weight))
-    ]
-    ffn_rows = jnp.concatenate(ffn_rows + [jnp.zeros((8, 4, FFN_COLS - 3 * SLAB), HALF)], axis=2)
-    ffn_rows = ffn_rows.reshape(8, 4, 2, FFN_HALF).transpose(0, 2, 1, 3).reshape(8, 2, 4 * FFN_HALF)
-    own = jnp.concatenate([mix_rows, ffn_rows], axis=2).transpose(1, 0, 2)
-    own = jnp.concatenate([own, own], axis=1)
     tail = jnp.pad(lax.dynamic_slice(tokens, (count - 2, 0), (2, D)), ((0, 14), (0, 0)))
     slots = jnp.arange(TOK, dtype=jnp.int32)
     flags = jnp.stack(
         [positions >= 1, positions >= 2, slots < count, slots == count - 2, slots == count - 1], axis=1
     )
     flags = jnp.pad(flags.astype(FLOAT), ((0, 0), (0, LANE - 5)))
-    mixed_out, grad_tokens, owned_mix, owned_ffn = whole_block(own, tail, tokens, flags, cotangent)
-    mine = lax.dynamic_slice(owned_mix, (8 * core, 0), (8, MIX_COLS)).reshape(8, 2, MIX_HALF)
-    ffn_mine = lax.dynamic_slice(owned_ffn, (0, 8 * core, 0), (4, 8, FFN_COLS))
-    ffn_mine = jnp.transpose(ffn_mine, (1, 0, 2))
-    small_mine = jnp.transpose(mine[:, 0, SMALL_AT : SMALL_AT + 8])
-    grad_in = mine[:, :, :OUT_AT].reshape(8, 2, 3, HALF_D).transpose(0, 2, 1, 3).reshape(8, 3 * D)
+    mixed_out, grad_tokens, grad_in, grad_out, grad_small, grad_gate, grad_up, grad_down = whole_block(
+        in_weight, out_weight, gate_weight, up_weight, jnp.transpose(down_weight), small,
+        tail, tokens, flags, cotangent,
+    )
+    grad_small = jnp.transpose(grad_small[:, :8])
     return (
         mixed_out,
         grad_tokens,
-        small_mine[0],
+        grad_small[0],
         grad_in,
-        small_mine[2:5],
-        mine[:, :, OUT_AT:SMALL_AT].reshape(8, D),
-        small_mine[1],
-        ffn_mine[:, :, :SLAB].reshape(8, 4 * SLAB),
-        ffn_mine[:, :, SLAB : 2 * SLAB].reshape(8, 4 * SLAB),
-        jnp.transpose(ffn_mine[:, :, 2 * SLAB : 3 * SLAB].reshape(8, 4 * SLAB)),
+        grad_small[2:5],
+        grad_out,
+        grad_small[1],
+        grad_gate,
+        grad_up,
+        jnp.transpose(grad_down),
     )
 
 

time: 155 us -> 154 us (level)
  local copies, waits for them, and re-layouts: 9.17 us -> 13.5 us
  Pallas kernels: 142 us -> 138 us
  other arithmetic: 2.57 us -> 0.66 us
    unnamed x19 -> x28, local copies, waits for them, and re-layouts: 2.1 us -> 9.29 us
    pallas_call x1, Pallas kernels: 142 us -> 138 us  [whole_block(): pl.pallas_call(block_kernel, out_shape=(shape((TOK, D), HALF), shape((TOK...]
    concatenate x2 -> x0, other arithmetic: 1.88 us -> none  [the longest x1 1.01 us: local(): jnp.concatenate(ffn_rows + [jnp.zeros((8, 4, FFN_COLS - 3 * SLAB), HALF)]...]
where the time goes in v4:
time: 154 us
  Pallas kernels  138 us (90%)
  local copies, waits for them, and re-layouts  13.5 us (9%)
    pallas_call x1, Pallas kernels, whole_block(): pl.pallas_call(block_kernel, out_shape=(shape((TOK, D), HALF), shape((TOK...  138 us
    unnamed x28, local copies, waits for them, and re-layouts  9.29 us

profile of v4, /device:TPU:1, one launch (start us, length us, event | category | flops | bytes accessed | tf_op | source)
XLA Modules:
  0.0 153.6 jit_solution(4570426915595893816)
XLA Ops:
  1.3 0.0 copy-start.9
  1.3 0.6 copy-done.9
  2.0 0.1 copy.43
  2.1 0.6 pad_convert_fusion.flags
  2.8 0.8 constant_dynamic-slice_fusion
  3.6 0.6 pad.15.tail
  4.2 0.0 copy-done.6
  4.2 0.1 copy.40
  4.3 0.1 copy.41
  4.4 0.1 copy.42
  4.5 0.7 copy-done.7
  5.2 0.1 copy.38
  5.3 0.7 copy-done.8
  5.9 0.1 copy.39
  6.0 0.1 stack.23
  6.1 0.6 pad.14.small_rows
  6.7 138.2 %whole_block.1 = (bf16[128,1024]{1,0:T(8,128)(2,1)}, bf16[128,1024]{1,0:T(8,128)(2,1)}, f32[8,3072]{1,0:T(8,128)}, f32[8,1024]{1,0:T(8,128)}, f32[8,128]{1,0:T(8...) custom-call(bf16[8,3072]{1,0:T(8,128)(2,1)} %in_rows.1, bf16[8,1024]{1,0:T(8,128)(2,1)} %out_rows.1, ...), custom_call_target="tpu_custom_call" | custom-call | tf_op jit(solution)/shard_map/whole_block/pallas_call | solution.py:826
  144.9 0.7 slice_bitcast_fusion
  145.6 0.7 slice_reduce_fusion
  146.3 0.1 slice.26
  146.3 0.7 copy.44
  147.0 1.7 %copy.53 = bf16[128,1024]{1,0:T(8,128)(2,1)} copy(bf16[128,1024]{1,0:T(8,128)(2,1)} %get-tuple-element.75) | data formatting | bytes 524288
  148.7 0.7 copy.54
  149.4 0.3 copy-done.4
  149.7 0.6 copy.55
  150.3 0.1 copy-done.5
  150.4 0.6 copy.56
  151.1 0.7 copy.57
  151.7 0.3 copy-done.2
  152.0 0.7 copy.58
  152.7 0.3 copy-done.1
  153.0 0.7 copy.59
  (16 shorter events, 0.1 us)
Async XLA Ops:
  1.3 0.7 copy-start.9
  3.6 0.7 copy-start.6
  4.5 0.7 copy-start.7
  5.3 0.7 copy-start.8
  147.0 1.7 %copy-start = (bf16[128,1024]{1,0:T(8,128)(2,1)S(1)}, bf16[128,1024]{1,0:T(8,128)(2,1)}, u32[]{:S(2)}) copy-start(bf16[128,1024]{1,0:T(8,128)(2,1)} %get-tuple-element.76) | copy-start | bytes 786436
  148.7 1.0 copy-start.4
  149.7 0.8 copy-start.5
  149.7 1.4 copy-start.3
  151.1 1.0 copy-start.2
  152.0 1.0 copy-start.1

commit v5 on v4

--- a/solution.py
+++ b/solution.py
@@ -417,15 +417,6 @@
     return near, far
 
 
-def twin_sum(ref, cols, landed, landed_cols):
-    @pl.loop(0, 32)
-    def _(index):
-        high, y = lax.div(index, 16), lax.rem(lax.div(index, 4), 4)
-        x = lax.rem(index, 4)
-        for low in range(2):
-            add_into(ref.at[high, y, x, low, :, cols], landed.at[high, y, x, low, :, landed_cols])
-
-
 def ffn_hidden(ffn, twos, backs, acts, start, width):
     value = twos[...].reshape(4 * TOK, D)
     gate = dot(value, mat(ffn, cut(start, width)))
@@ -448,14 +439,15 @@
         target[:, :, cut(tile * TILE, TILE)] = total.astype(HALF).reshape(4, TOK, TILE)
 
 
-def ffn_weight_grads(ffn, acts, turned, half, part):
+def ffn_weight_grads(ffn, acts, acts_in, turned, half, part):
     first, chunks = part
 
     @pl.loop(first * LANE // TILE, (first + chunks) * LANE // TILE)
     def _(tile):
         cols = cut(half * FFN_HALF + tile * TILE, TILE)
         side = half * jnp.minimum(lax.div(tile, 2), 1)
-        value = dot(turned[side], acts[:, cols])
+        value = dot(turned[0, side], acts[:, cols])
+        value += dot(turned[1, side], acts_in[:, cut(tile * TILE, TILE)])
         ffn[:, :, :, :, :, cols] = value.astype(HALF).reshape(GRID + (16, TILE))
 
 
@@ -563,12 +555,36 @@
         own[1, :, at + rest + SLAB : at + FFN_HALF] = jnp.zeros((16, LANE), HALF)
 
 
+def lay_flags(board, flags, tail, tokens, positions, counts):
+    slots = lax.broadcasted_iota(jnp.int32, (1, LANE), 1)
+    place, count = positions[...], jnp.broadcast_to(counts[...], (1, LANE))
+
+    def bit(condition):
+        return jnp.where(condition, jnp.ones((1, LANE), FLOAT), jnp.zeros((1, LANE), FLOAT))
+
+    board[...] = jnp.zeros_like(board)
+    board[0:1] = bit(place >= 1)
+    board[1:2] = bit(place >= 2)
+    board[2:3] = bit(slots < count)
+    for row in (3, 16):
+        board[row : row + 1] = bit(slots == count - 2)
+        board[row + 1 : row + 2] = bit(slots == count - 1)
+    flags[...] = jnp.transpose(board[...])
+    tail[...] = dot(board[16:32].astype(HALF), tokens[...]).astype(HALF)
+
+
+def lay_small(board, small_rows, vectors):
+    board[...] = jnp.zeros_like(board)
+    board[0:5, 0:8] = vectors[...].astype(FLOAT)
+    small_rows[...] = jnp.transpose(board[...])[0:8].astype(HALF)
+
+
 def block_kernel(
-    in_rows, out_rows, gate_rows, up_rows, down_rows, small_rows, tail, tokens, flags, cotangent,
+    in_rows, out_rows, gate_rows, up_rows, down_rows, vectors, tokens, positions, counts, cotangent,
     mixed_out, grad_tokens, grad_in, grad_out, grad_small, grad_gate, grad_up, grad_down,
-    own, mix_owned, ffn_owned,
+    own, mix_owned, ffn_owned, board, small_rows, flags, tail,
     mate, full, halo, mix, ffn, twos, backs, proj, normed, gated, resid, rows, acts, turned_ffn,
-    total, mix_mate, ffn_landed, ffn_rest, ffn_mate, work, ffn_work,
+    total, mix_mate, acts_in, ffn_rest, ffn_mate, work, ffn_work,
     branch, grads, d_normed, small, turned, normed_in, gated_in, branch_in, grads_in, small_in,
     edge_in, d_resid, *scratch,
 ):
@@ -586,6 +602,8 @@
         + [here.beside(axis, 2) for axis in ("x", "y", "z")]
         + [twin, here.along(1), here.along(-1)]
     )
+    lay_flags(board, flags, tail, tokens, positions, counts)
+    lay_small(board, small_rows, vectors)
     lay_out(own, in_rows, out_rows, gate_rows, up_rows, down_rows, small_rows)
     pl.semaphore_wait(barrier, count)
     rows_in = mail.post(own.at[1 - core], mate, twin)
@@ -622,8 +640,6 @@
     wait_all(slabs)
     ffn_rings = gather_rings(here, mail, ffn, ffn_base, FFN_PARTS, FFN_GATHER, 0)
     start_all(ffn_rings)
-    stream = RingGather(here, mail, "x", row_pick(backs))
-    stream.start()
     finish_all(mix_rings)
     mix_rings = gather_rings(here, mail, mix, mix_base, MIX_PARTS, MIX_GATHER, 2)
     start_all(mix_rings)
@@ -631,12 +647,14 @@
     relay_all(ffn_rings)
     relay_all(mix_rings)
     swaps += swap_pieces(here, mail, mix_rings, (1, -1))
+    stream = RingGather(here, mail, "x", row_pick(backs))
+    stream.start()
     finish_all(ffn_rings)
     ffn_rings = gather_rings(here, mail, ffn, ffn_base, FFN_PARTS, FFN_GATHER, 1)
-    stream.relay()
     finish_all(mix_rings)
     swaps += swap_pieces(here, mail, mix_rings, (2,))
     start_all(ffn_rings)
+    stream.relay()
     ffn_swaps = swap_pieces(here, mail, ffn_rings, (0,))
     wait_all(swaps)
     halo_in.wait_recv()
@@ -653,7 +671,8 @@
     ffn_swaps += swap_pieces(here, mail, ffn_rings, (2,))
     stream.finish()
     for block in range(4):
-        turn(turned_ffn.at[1, :, block * TOK : (block + 1) * TOK], backs[block])
+        turn(turned_ffn.at[0, 1, :, block * TOK : (block + 1) * TOK], backs[block])
+    shared = [mail.post(turned_ffn.at[0, 1], turned_ffn.at[1, 1], twin)]
     wait_all(ffn_swaps)
     two_ring.finish()
     gathered = len(mail.posted)
@@ -663,42 +682,23 @@
         ffn_hidden(ffn, twos, backs, acts, tile * TILE, TILE)
 
     ffn_hidden(ffn, twos, backs, acts, SLAB // TILE * TILE, SLAB % TILE)
+    shared.append(
+        mail.post(acts.at[:, cut((1 - core) * FFN_HALF, FFN_HALF)], acts_in, twin)
+    )
     ffn_tokens(ffn, acts, work, (0, 1))
     two_ring = RingReduce(here, mail, "x", row_pick(work), two_near, two_far)
     two_ring.start()
+    for block in range(4):
+        turn(turned_ffn.at[0, 0, :, block * TOK : (block + 1) * TOK], twos[block])
+    shared.append(mail.post(turned_ffn.at[0, 0], turned_ffn.at[1, 0], twin))
     ffn_tokens(ffn, acts, ffn_work, (2,))
-    for block in range(4):
-        turn(turned_ffn.at[0, :, block * TOK : (block + 1) * TOK], twos[block])
+    two_ring.relay()
     mail.settle(gathered)
-    pieces, base = [], (1 - core) * FFN_HALF
-    for number, (first, chunks) in enumerate(FFN_PARTS):
-        ffn_weight_grads(ffn, acts, turned_ffn, 1 - core, (first, chunks))
-        piece = slice(first * LANE, (first + chunks) * LANE)
-        pieces.append(
-            mail.post(
-                ffn.at[:, :, :, :, :, cut(base + first * LANE, chunks * LANE)],
-                ffn_landed.at[:, :, :, :, :, piece],
-                twin,
-            )
-        )
-        if number == 0:
-            two_ring.relay()
+    wait_all(shared)
     ffn_rings = reduce_rings(here, mail, ffn, ffn_base, FFN_PARTS, FFN_REDUCE, ffn_near, ffn_far, 0)
-    for part in FFN_PARTS:
-        ffn_weight_grads(ffn, acts, turned_ffn, core, part)
-
-    def join(number):
-        first, chunks = FFN_PARTS[number]
-        pieces[number].wait_recv()
-        twin_sum(
-            ffn,
-            cut(ffn_base + first * LANE, chunks * LANE),
-            ffn_landed,
-            slice(first * LANE, (first + chunks) * LANE),
-        )
-        ffn_rings[number].start()
-
-    join(0)
+    for part, ring in zip(FFN_PARTS, ffn_rings):
+        ffn_weight_grads(ffn, acts, acts_in, turned_ffn, core, part)
+        ring.start()
     two_ring.finish()
     value = resid[...]
     scale = norm_scale(value)
@@ -713,7 +713,6 @@
     late = [mail.post(branch.at[1 - core], branch_in, twin)]
     out_ring = RingReduce(here, mail, "x", row_pick(ffn_work), out_near, out_far)
     out_ring.start()
-    join(1)
     mixer_backward(here, flags, mix, proj, rows, branch, grads, small)
     late.append(mail.post(grads.at[1 - core], grads_in, twin))
     relay_all(ffn_rings)
@@ -798,6 +797,17 @@
     mail.settle(len(mail.posted))
 
 
+def write_kernel(*refs):
+    count = (len(refs) - 2) // 2
+    ins, outs = refs[:count], refs[count:]
+    for source, target in zip(ins[:-1], outs):
+        target[...] = source[...]
+    small = jnp.transpose(ins[-1][...])
+    outs[-3][...] = small[0:1, 0:8]
+    outs[-2][...] = small[1:2, 0:8]
+    outs[-1][...] = small[2:5, 0:8]
+
+
 def vmem():
     return pl.BlockSpec(memory_space=pltpu.VMEM)
 
@@ -841,6 +851,10 @@
             pltpu.VMEM((2, 16, OWN_COLS), HALF),
             pltpu.VMEM((16, MIX_COLS), FLOAT),
             pltpu.VMEM((4, 16, FFN_COLS), FLOAT),
+            pltpu.VMEM((LANE, LANE), FLOAT),
+            pltpu.VMEM((8, LANE), HALF),
+            pltpu.VMEM((TOK, LANE), FLOAT),
+            pltpu.VMEM((16, D), HALF),
             pltpu.VMEM((16, OWN_COLS), HALF),
             pltpu.VMEM((16, OWN_COLS), HALF),
             pltpu.VMEM((16, D), HALF),
@@ -854,10 +868,10 @@
             pltpu.VMEM((TOK, D), FLOAT),
             pltpu.VMEM((8, D), FLOAT),
             pltpu.VMEM((4 * TOK, FFN_COLS), HALF),
-            pltpu.VMEM((2, D, 4 * TOK), HALF),
+            pltpu.VMEM((2, 2, D, 4 * TOK), HALF),
             pltpu.VMEM(GRID + (16, MIX_HALF), HALF),
             pltpu.VMEM((16, MIX_HALF), HALF),
-            pltpu.VMEM(GRID + (16, FFN_HALF), HALF),
+            pltpu.VMEM((4 * TOK, FFN_HALF), HALF),
             pltpu.VMEM((4, 16, FFN_HALF), HALF),
             pltpu.VMEM((4, 16, FFN_HALF), HALF),
             pltpu.VMEM((4, TOK, D), HALF),
@@ -897,28 +911,35 @@
     positions,
     cotangent,
 ):
-    count = live_counts[0, 0]
-    small = jnp.stack([gain_mix, gain_ffn, conv_weight[0], conv_weight[1], conv_weight[2]], axis=1)
-    small = jnp.pad(small, ((0, 0), (0, LANE - 5)))
-    tail = jnp.pad(lax.dynamic_slice(tokens, (count - 2, 0), (2, D)), ((0, 14), (0, 0)))
-    slots = jnp.arange(TOK, dtype=jnp.int32)
-    flags = jnp.stack(
-        [positions >= 1, positions >= 2, slots < count, slots == count - 2, slots == count - 1], axis=1
-    )
-    flags = jnp.pad(flags.astype(FLOAT), ((0, 0), (0, LANE - 5)))
+    vectors = jnp.concatenate([gain_mix[None], gain_ffn[None], conv_weight], axis=0)
     mixed_out, grad_tokens, grad_in, grad_out, grad_small, grad_gate, grad_up, grad_down = whole_block(
-        in_weight, out_weight, gate_weight, up_weight, jnp.transpose(down_weight), small,
-        tail, tokens, flags, cotangent,
-    )
-    grad_small = jnp.transpose(grad_small[:, :8])
+        in_weight, out_weight, gate_weight, up_weight, jnp.transpose(down_weight), vectors,
+        tokens, positions.reshape(1, TOK), live_counts, cotangent,
+    )
+    plain = (mixed_out, grad_tokens, grad_in, grad_out, grad_gate, grad_up, grad_down)
+    mixed_out, grad_tokens, grad_in, grad_out, grad_gate, grad_up, grad_down, one, two, taps = (
+        pl.pallas_call(
+            write_kernel,
+            out_shape=tuple(shape(value.shape, value.dtype) for value in plain)
+            + (
+                shape((1, 8), FLOAT),
+                shape((1, 8), FLOAT),
+                shape((3, 8), FLOAT),
+            ),
+            in_specs=[vmem()] * 8,
+            out_specs=(vmem(),) * 10,
+            name="write",
+            compiler_params=pltpu.CompilerParams(vmem_limit_bytes=VMEM_LIMIT),
+        )(*plain, grad_small)
+    )
     return (
         mixed_out,
         grad_tokens,
-        grad_small[0],
+        one.reshape(8),
         grad_in,
-        grad_small[2:5],
+        taps,
         grad_out,
-        grad_small[1],
+        two.reshape(8),
         grad_gate,
         grad_up,
         jnp.transpose(grad_down),

time: 154 us -> 136 us (0.88)
  local copies, waits for them, and re-layouts: 13.5 us -> 0.67 us
  Pallas kernels: 138 us -> 134 us
    unnamed x28 -> x6, local copies, waits for them, and re-layouts: 9.29 us -> 0.67 us
    pallas_call x1, Pallas kernels: 138 us -> 131 us  [whole_block(): pl.pallas_call(block_kernel, out_shape=(shape((TOK, D), HALF), shape((TOK...]
    pallas_call x0 -> x1, Pallas kernels: none -> 2.26 us  [local(): pl.pallas_call(write_kernel, out_shape=tuple((shape(value.shape, value.dt...]
where the time goes in v5:
time: 136 us
  Pallas kernels  134 us (99%)
    pallas_call x1, Pallas kernels, whole_block(): pl.pallas_call(block_kernel, out_shape=(shape((TOK, D), HALF), shape((TOK...  131 us

profile of v5, /device:TPU:1, one launch (start us, length us, event | category | flops | bytes accessed | tf_op | source)
XLA Modules:
  0.0 136.1 jit_solution(15000060198013043809)
XLA Ops:
  1.3 0.0 copy-start.2
  1.3 0.0 copy-start
  1.3 0.0 copy-start.1
  1.3 0.6 copy-done.2
  1.9 0.0 copy-done
  2.0 0.0 copy-done.1
  2.0 0.6 pad_maximum_fusion.vectors
  2.6 131.3 %whole_block.1 = (bf16[128,1024]{1,0:T(8,128)(2,1)}, bf16[128,1024]{1,0:T(8,128)(2,1)}, f32[8,3072]{1,0:T(8,128)}, f32[8,1024]{1,0:T(8,128)}, f32[8,128]{1,0:T(8...) custom-call(bf16[8,3072]{1,0:T(8,128)(2,1)} %in_rows.1, bf16[8,1024]{1,0:T(8,128)(2,1)} %out_rows.1, ...), custom_call_target="tpu_custom_call" | custom-call | tf_op jit(solution)/shard_map/whole_block/pallas_call | solution.py:836
  133.9 2.3 %write.1 = (bf16[128,1024]{1,0:T(8,128)(2,1)}, bf16[128,1024]{1,0:T(8,128)(2,1)}, f32[8,3072]{1,0:T(8,128)}, f32[8,1024]{1,0:T(8,128)}, f32[8,4608]{1,0:T(8,128)...) custom-call(bf16[128,1024]{1,0:T(8,128)(2,1)} %get-tuple-element.28.refs_0_, ...), custom_call_target="tpu_custom_call" | custom-call | tf_op jit(solution)/shard_map/write/pallas_call | solution.py:921
Async XLA Ops:
  1.3 0.7 copy-start.2
  1.3 0.7 copy-start
  1.3 0.7 copy-start.1

commit v6 on v5

--- a/solution.py
+++ b/solution.py
@@ -254,10 +254,11 @@
         ring.finish()
 
 
-def run_rings(rings):
-    start_all(rings)
-    relay_all(rings)
-    finish_all(rings)
+def chain(rings, later):
+    for ring, following in zip(rings, later):
+        ring.finish()
+        following.start()
+    return later
 
 
 def swap_pieces(here, mail, rings, steps):
@@ -513,14 +514,18 @@
         normed_grad[:, cut(tile * TILE, TILE)] = total
 
 
-def mixer_weight_grads(here, grads, branch, turned, grads_in, branch_in, total):
+def mixer_weight_grads(here, grads, branch, turned, grads_in, branch_in, total, rings):
     def put(cols, value):
         total[:, :, :, :, :, cols] = value.astype(HALF).reshape(GRID + (16, TILE))
 
-    @pl.loop(0, OUT_AT // TILE)
-    def _(tile):
-        cols = cut(tile * TILE, TILE)
-        put(cols, dot(turned[0], grads[here.core, :, cols]) + dot(turned[1], grads_in[:, cols]))
+    for ring, (first, chunks) in zip(rings[:2], MIX_PARTS):
+
+        @pl.loop(first * LANE // TILE, (first + chunks) * LANE // TILE)
+        def _(tile):
+            cols = cut(tile * TILE, TILE)
+            put(cols, dot(turned[0], grads[here.core, :, cols]) + dot(turned[1], grads_in[:, cols]))
+
+        ring.start()
 
     @pl.loop(0, HALF_D // TILE)
     def _(tile):
@@ -632,17 +637,18 @@
     keep_slab = pltpu.make_async_copy(slab(x), ffn_own, local_sem.at[1])
     keep_mix.start()
     keep_slab.start()
-    finish_all(rings)
     keep_mix.wait()
-    mix_rings = gather_rings(here, mail, mix, mix_base, MIX_PARTS, MIX_GATHER, 1, DirectGather)
-    start_all(mix_rings)
+    mix_rings = chain(
+        rings,
+        gather_rings(here, mail, mix, mix_base, MIX_PARTS, MIX_GATHER, 1, DirectGather),
+    )
     keep_slab.wait()
     wait_all(slabs)
     ffn_rings = gather_rings(here, mail, ffn, ffn_base, FFN_PARTS, FFN_GATHER, 0)
     start_all(ffn_rings)
-    finish_all(mix_rings)
-    mix_rings = gather_rings(here, mail, mix, mix_base, MIX_PARTS, MIX_GATHER, 2)
-    start_all(mix_rings)
+    mix_rings = chain(
+        mix_rings, gather_rings(here, mail, mix, mix_base, MIX_PARTS, MIX_GATHER, 2)
+    )
     swaps = swap_pieces(here, mail, mix_rings, (0,))
     relay_all(ffn_rings)
     relay_all(mix_rings)
@@ -651,9 +657,10 @@
     stream.start()
     finish_all(ffn_rings)
     ffn_rings = gather_rings(here, mail, ffn, ffn_base, FFN_PARTS, FFN_GATHER, 1)
-    finish_all(mix_rings)
-    swaps += swap_pieces(here, mail, mix_rings, (2,))
     start_all(ffn_rings)
+    for ring in mix_rings:
+        ring.finish()
+        swaps += swap_pieces(here, mail, [ring], (2,))
     stream.relay()
     ffn_swaps = swap_pieces(here, mail, ffn_rings, (0,))
     wait_all(swaps)
@@ -730,16 +737,17 @@
     turn(turned.at[1, :, 0:ALL], normed_in[...])
     turn(turned.at[3, :, 0:TOK], gated_in[...])
     wait_all(late)
-    mixer_weight_grads(here, grads, branch, turned, grads_in, branch_in, total)
+    mix_rings = reduce_rings(here, mail, total, 0, MIX_PARTS, MIX_REDUCE, mix_near, mix_far, 0)
+    mixer_weight_grads(here, grads, branch, turned, grads_in, branch_in, total, mix_rings)
     small_sum = small[...] + small_in[...]
     total[:, :, :, :, :, SMALL_AT:MIX_HALF] = (
         jnp.transpose(small_sum).astype(HALF).reshape(GRID + (16, LANE))
     )
-    mix_rings = reduce_rings(here, mail, total, 0, MIX_PARTS, MIX_REDUCE, mix_near, mix_far, 0)
-    start_all(mix_rings)
-    finish_all(ffn_rings)
-    ffn_rings = reduce_rings(here, mail, ffn, ffn_base, FFN_PARTS, FFN_REDUCE, ffn_near, ffn_far, 1)
-    start_all(ffn_rings)
+    mix_rings[2].start()
+    ffn_rings = chain(
+        ffn_rings,
+        reduce_rings(here, mail, ffn, ffn_base, FFN_PARTS, FFN_REDUCE, ffn_near, ffn_far, 1),
+    )
     relay_all(mix_rings)
     relay_all(ffn_rings)
     edge.wait_recv()
@@ -747,9 +755,10 @@
         d_normed[0:TOK] + flags[:, 3:4] * edge_in[0:1] + flags[:, 4:5] * edge_in[1:2]
     )
     grad_tokens[...] = (d_resid[...] + norm_back(unit, scale, rows[0:1], d_first)).astype(HALF)
-    finish_all(mix_rings)
-    mix_rings = reduce_rings(here, mail, total, 0, MIX_PARTS, MIX_REDUCE, mix_near, mix_far, 1)
-    start_all(mix_rings)
+    mix_rings = chain(
+        mix_rings,
+        reduce_rings(here, mail, total, 0, MIX_PARTS, MIX_REDUCE, mix_near, mix_far, 1),
+    )
     finish_all(ffn_rings)
     copies = []
     for step in (1, 3, 2):
@@ -765,9 +774,10 @@
     relay_all(mix_rings)
     out_ring.finish()
     mixed_out[...] = (flags[:, 2:3] * (resid[...] + ffn_work[x].astype(FLOAT))).astype(HALF)
-    finish_all(mix_rings)
-    mix_rings = reduce_rings(here, mail, total, 0, MIX_PARTS, MIX_REDUCE, mix_near, mix_far, 2)
-    start_all(mix_rings)
+    mix_rings = chain(
+        mix_rings,
+        reduce_rings(here, mail, total, 0, MIX_PARTS, MIX_REDUCE, mix_near, mix_far, 2),
+    )
     wait_all(copies)
     ffn_swap = mail.post(ffn_rest, ffn_mate, twin)
     ffn_owned[:, :, cut(core * FFN_HALF, FFN_HALF)] = ffn_rest[...].astype(FLOAT)

time: 136 us -> 133 us (0.978)
  Pallas kernels: 134 us -> 131 us
    pallas_call x1, Pallas kernels: 131 us -> 128 us  [whole_block(): pl.pallas_call(block_kernel, out_shape=(shape((TOK, D), HALF), shape((TOK...]
where the time goes in v6:
time: 133 us
  Pallas kernels  131 us (98%)
    pallas_call x1, Pallas kernels, whole_block(): pl.pallas_call(block_kernel, out_shape=(shape((TOK, D), HALF), shape((TOK...  128 us

profile of v6, /device:TPU:1, one launch (start us, length us, event | category | flops | bytes accessed | tf_op | source)
XLA Modules:
  0.0 133.3 jit_solution(14297904376426672030)
XLA Ops:
  1.3 0.0 copy-start.2
  1.3 0.0 copy-start
  1.3 0.0 copy-start.1
  1.3 0.6 copy-done.2
  1.9 0.0 copy-done
  2.0 0.0 copy-done.1
  2.0 0.6 pad_maximum_fusion.vectors
  2.6 128.4 %whole_block.1 = (bf16[128,1024]{1,0:T(8,128)(2,1)}, bf16[128,1024]{1,0:T(8,128)(2,1)}, f32[8,3072]{1,0:T(8,128)}, f32[8,1024]{1,0:T(8,128)}, f32[8,128]{1,0:T(8...) custom-call(bf16[8,3072]{1,0:T(8,128)(2,1)} %in_rows.1, bf16[8,1024]{1,0:T(8,128)(2,1)} %out_rows.1, ...), custom_call_target="tpu_custom_call" | custom-call | tf_op jit(solution)/shard_map/whole_block/pallas_call | solution.py:846
  131.0 2.3 %write.1 = (bf16[128,1024]{1,0:T(8,128)(2,1)}, bf16[128,1024]{1,0:T(8,128)(2,1)}, f32[8,3072]{1,0:T(8,128)}, f32[8,1024]{1,0:T(8,128)}, f32[8,4608]{1,0:T(8,128)...) custom-call(bf16[128,1024]{1,0:T(8,128)(2,1)} %get-tuple-element.28.refs_0_, ...), custom_call_target="tpu_custom_call" | custom-call | tf_op jit(solution)/shard_map/write/pallas_call | solution.py:931
Async XLA Ops:
  1.3 0.7 copy-start.2
  1.3 0.7 copy-start
  1.3 0.7 copy-start.1

commit v7 on v6

--- a/solution.py
+++ b/solution.py
@@ -375,7 +375,7 @@
         for axis in order[:stage]:
             fixed[axis] = here.at[axis]
         pick = column_pick(ref, fixed, order[stage], base + first * LANE, chunks)
-        kind = RingReduce if stage == 0 else DirectReduce
+        kind = RingReduce if stage <= 1 else DirectReduce
         rings.append(kind(here, mail, order[stage], pick, near[number][stage], far[number][stage]))
     return rings
 
@@ -397,7 +397,7 @@
             if "z" not in gone:
                 lead += (2,)
             done += [lead + (16, chunks * LANE)] * 2
-            if stage == 0:
+            if stage <= 1:
                 done += [lead + (16, split * LANE), lead + (16, (chunks - split) * LANE)]
             else:
                 done += [lead + (16, chunks * LANE), (16, LANE)]

time: 133 us -> 132 us (level)
  Pallas kernels: 131 us -> 129 us
    pallas_call x1, Pallas kernels: 128 us -> 127 us  [whole_block(): pl.pallas_call(block_kernel, out_shape=(shape((TOK, D), HALF), shape((TOK...]
where the time goes in v7:
time: 132 us
  Pallas kernels  129 us (98%)
  between operations  1.32 us (1%)
    pallas_call x1, Pallas kernels, whole_block(): pl.pallas_call(block_kernel, out_shape=(shape((TOK, D), HALF), shape((TOK...  127 us

profile of v7, /device:TPU:1, one launch (start us, length us, event | category | flops | bytes accessed | tf_op | source)
XLA Modules:
  0.0 131.7 jit_solution(944486859942107675)
XLA Ops:
  1.3 0.0 copy-start.2
  1.3 0.0 copy-start
  1.3 0.0 copy-start.1
  1.3 0.6 copy-done.2
  1.9 0.0 copy-done
  2.0 0.0 copy-done.1
  2.0 0.6 pad_maximum_fusion.vectors
  2.6 126.9 %whole_block.1 = (bf16[128,1024]{1,0:T(8,128)(2,1)}, bf16[128,1024]{1,0:T(8,128)(2,1)}, f32[8,3072]{1,0:T(8,128)}, f32[8,1024]{1,0:T(8,128)}, f32[8,128]{1,0:T(8...) custom-call(bf16[8,3072]{1,0:T(8,128)(2,1)} %in_rows.1, bf16[8,1024]{1,0:T(8,128)(2,1)} %out_rows.1, ...), custom_call_target="tpu_custom_call" | custom-call | tf_op jit(solution)/shard_map/whole_block/pallas_call | solution.py:846
  129.5 2.3 %write.1 = (bf16[128,1024]{1,0:T(8,128)(2,1)}, bf16[128,1024]{1,0:T(8,128)(2,1)}, f32[8,3072]{1,0:T(8,128)}, f32[8,1024]{1,0:T(8,128)}, f32[8,4608]{1,0:T(8,128)...) custom-call(bf16[128,1024]{1,0:T(8,128)(2,1)} %get-tuple-element.28.refs_0_, ...), custom_call_target="tpu_custom_call" | custom-call | tf_op jit(solution)/shard_map/write/pallas_call | solution.py:931
Async XLA Ops:
  1.3 0.7 copy-start.2
  1.3 0.7 copy-start
  1.3 0.7 copy-start.1

commit v8 on v7

--- a/solution.py
+++ b/solution.py
@@ -672,6 +672,9 @@
     ffn_swaps += swap_pieces(here, mail, ffn_rings, (1, -1))
     early = [mail.post(normed, normed_in, twin), mail.post(gated, gated_in, twin)]
     two_ring.relay()
+    for step in (0, 1, -1):
+        block = here.ring("x", step)
+        turn(turned_ffn.at[0, 0, :, cut(block * TOK, TOK)], twos[block])
     turn(turned.at[0, :, 0:ALL], normed[...])
     turn(turned.at[2, :, 0:TOK], gated[...])
     finish_all(ffn_rings)
@@ -682,7 +685,10 @@
     shared = [mail.post(turned_ffn.at[0, 1], turned_ffn.at[1, 1], twin)]
     wait_all(ffn_swaps)
     two_ring.finish()
+    block = here.ring("x", 2)
+    turn(turned_ffn.at[0, 0, :, cut(block * TOK, TOK)], twos[block])
     gathered = len(mail.posted)
+    shared.append(mail.post(turned_ffn.at[0, 0], turned_ffn.at[1, 0], twin))
 
     @pl.loop(0, SLAB // TILE)
     def _(tile):
@@ -695,9 +701,6 @@
     ffn_tokens(ffn, acts, work, (0, 1))
     two_ring = RingReduce(here, mail, "x", row_pick(work), two_near, two_far)
     two_ring.start()
-    for block in range(4):
-        turn(turned_ffn.at[0, 0, :, block * TOK : (block + 1) * TOK], twos[block])
-    shared.append(mail.post(turned_ffn.at[0, 0], turned_ffn.at[1, 0], twin))
     ffn_tokens(ffn, acts, ffn_work, (2,))
     two_ring.relay()
     mail.settle(gathered)

time: 132 us -> 132 us (level)
  no operation moved by 1% of the time
where the time goes in v8:
time: 132 us
  Pallas kernels  129 us (98%)
  between operations  1.32 us (1%)
    pallas_call x1, Pallas kernels, whole_block(): pl.pallas_call(block_kernel, out_shape=(shape((TOK, D), HALF), shape((TOK...  127 us

profile of v8, /device:TPU:1, one launch (start us, length us, event | category | flops | bytes accessed | tf_op | source)
XLA Modules:
  0.0 131.9 jit_solution(17964901229538426542)
XLA Ops:
  1.3 0.0 copy-start.2
  1.3 0.0 copy-start
  1.3 0.0 copy-start.1
  1.3 0.6 copy-done.2
  1.9 0.0 copy-done
  2.0 0.0 copy-done.1
  2.0 0.6 pad_maximum_fusion.vectors
  2.6 127.1 %whole_block.1 = (bf16[128,1024]{1,0:T(8,128)(2,1)}, bf16[128,1024]{1,0:T(8,128)(2,1)}, f32[8,3072]{1,0:T(8,128)}, f32[8,1024]{1,0:T(8,128)}, f32[8,128]{1,0:T(8...) custom-call(bf16[8,3072]{1,0:T(8,128)(2,1)} %in_rows.1, bf16[8,1024]{1,0:T(8,128)(2,1)} %out_rows.1, ...), custom_call_target="tpu_custom_call" | custom-call | tf_op jit(solution)/shard_map/whole_block/pallas_call | solution.py:849
  129.7 2.3 %write.1 = (bf16[128,1024]{1,0:T(8,128)(2,1)}, bf16[128,1024]{1,0:T(8,128)(2,1)}, f32[8,3072]{1,0:T(8,128)}, f32[8,1024]{1,0:T(8,128)}, f32[8,4608]{1,0:T(8,128)...) custom-call(bf16[128,1024]{1,0:T(8,128)(2,1)} %get-tuple-element.28.refs_0_, ...), custom_call_target="tpu_custom_call" | custom-call | tf_op jit(solution)/shard_map/write/pallas_call | solution.py:934
Async XLA Ops:
  1.3 0.7 copy-start.2
  1.3 0.7 copy-start
  1.3 0.7 copy-start.1
